TPU v7x, 32 devices: a whole 2x2x4 slice. The times are simulated.
32 devices in a mesh: dp: 16 (over z, x, core), tensor: 2 (over y).
Axes of the slice: x: 2, y: 2, z: 4, core: 2. Of those that a mesh axis runs over, the one named last changes fastest.
Arguments:
- inputs: bfloat16 [32768, 768], P(('dp', 'tensor')), may hold values from -6 to 6
- lengths: int32 [32], P('dp'), may hold values from 100 to 1024, as said below
- norm1_gain: float32 [768], replicated, may hold values from 0.1 to 1.9
- norm1_shift: float32 [768], replicated, may hold values from -3 to 3
- query_weight: bfloat16 [768, 768], P(None, 'tensor'), may hold values from -0.21875 to 0.21875
- query_bias: float32 [768], P('tensor'), may hold values from -3 to 3
- key_weight: bfloat16 [768, 768], P(None, 'tensor'), may hold values from -0.21875 to 0.21875
- key_bias: float32 [768], P('tensor'), may hold values from -3 to 3
- value_weight: bfloat16 [768, 768], P(None, 'tensor'), may hold values from -0.21875 to 0.21875
- value_bias: float32 [768], P('tensor'), may hold values from -3 to 3
- out_weight: bfloat16 [768, 768], P('tensor'), may hold values from -0.875 to 0.875
- out_bias: float32 [768], replicated, may hold values from -3 to 3
- norm2_gain: float32 [768], replicated, may hold values from 0.1 to 1.9
- norm2_shift: float32 [768], replicated, may hold values from -3 to 3
- up_weight: bfloat16 [768, 3072], P(None, 'tensor'), may hold values from -0.21875 to 0.21875
- up_bias: float32 [3072], P('tensor'), may hold values from -3 to 3
- down_weight: bfloat16 [3072, 768], P('tensor'), may hold values from -0.109375 to 0.109375
- down_bias: float32 [768], replicated, may hold values from -3 to 3
- out_grad: bfloat16 [32768, 768], P(('dp', 'tensor')), may hold values from -6 to 6
Outputs:
- layer_out: bfloat16 [32768, 768], P(('dp', 'tensor'))
- input_grad: bfloat16 [32768, 768], P(('dp', 'tensor'))
- grad_norm1_gain: float32 [768], replicated
- grad_norm1_shift: float32 [768], replicated
- grad_query_weight: float32 [768, 768], P(None, 'tensor')
- grad_query_bias: float32 [768], P('tensor')
- grad_key_weight: float32 [768, 768], P(None, 'tensor')
- grad_key_bias: float32 [768], P('tensor')
- grad_value_weight: float32 [768, 768], P(None, 'tensor')
- grad_value_bias: float32 [768], P('tensor')
- grad_out_weight: float32 [768, 768], P('tensor')
- grad_out_bias: float32 [768], replicated
- grad_norm2_gain: float32 [768], replicated
- grad_norm2_shift: float32 [768], replicated
- grad_up_weight: float32 [768, 3072], P(None, 'tensor')
- grad_up_bias: float32 [3072], P('tensor')
- grad_down_weight: float32 [3072, 768], P('tensor')
- grad_down_bias: float32 [768], replicated
Inputs may be any that keep to these rules, and one draw needn't show every extreme that they name: `lengths`: valid tokens of each sequence; in every draw some sequence has exactly 1024.
All inputs are finite; a program needn't handle non-finite values.
Results may differ from a plain program's by a relative error of at most 0.034.
Values may be sent and summed in bfloat16 or wider, within the bound.
No kernel may reach another device: no remote copies, remote signals or barrier semaphores. Data moves between devices by JAX's collectives and lax.ppermute only.
A program may use at most 256 MiB of HBM per device.

v0:
```python
import jax
import jax.numpy as jnp
from jax import lax
from jax.sharding import PartitionSpec as P

HEAD_DIM = 64


epsilon = 1e-05


def layer_norm(values, gain_vec, shift_vec):
    average = jnp.mean(values, axis=-1, keepdims=True)
    centered = values - average
    spread = jnp.mean(centered * centered, axis=-1, keepdims=True)
    return centered * lax.rsqrt(spread + epsilon) * gain_vec + shift_vec


def exact_gelu(values):
    return jax.nn.gelu(values, approximate=False)


def rotary_tables(length_rows, head_size):
    halfway = head_size // 2
    places = jnp.arange(length_rows, dtype=jnp.float32)[:, None, None]
    frequencies = 10000.0 ** (-2.0 * jnp.arange(halfway, dtype=jnp.float32) / head_size)
    angles = places * frequencies
    return (jnp.cos(angles), jnp.sin(angles))


def rotate(tensor, cosine_table, sine_table):
    halfway = tensor.shape[-1] // 2
    leading = tensor[..., :halfway]
    trailing = tensor[..., halfway:]
    return jnp.concatenate(
        [
            leading * cosine_table - trailing * sine_table,
            trailing * cosine_table + leading * sine_table,
        ],
        axis=-1,
    )


def rotate_back(tensor, cosine_table, sine_table):
    halfway = tensor.shape[-1] // 2
    leading = tensor[..., :halfway]
    trailing = tensor[..., halfway:]
    return jnp.concatenate(
        [
            leading * cosine_table + trailing * sine_table,
            trailing * cosine_table - leading * sine_table,
        ],
        axis=-1,
    )


def attend_forward(queries, keys, values_h, length):
    seq_rows = queries.shape[0]
    valid_rows = (jnp.arange(seq_rows) < length).astype(jnp.float32)
    scores = jnp.einsum("qhd,khd->hqk", queries, keys, preferred_element_type=jnp.float32)
    scores = scores + ((valid_rows - 1.0) * 1e30)[None, None, :]
    log_total = jax.nn.logsumexp(scores, axis=-1, keepdims=True)
    attn_probs = jnp.exp(scores - log_total).astype(jnp.bfloat16)
    context = jnp.einsum("hqk,khd->qhd", attn_probs, values_h, preferred_element_type=jnp.float32)
    context = context * valid_rows[:, None, None]
    return (context.astype(jnp.bfloat16), jnp.transpose(log_total[:, :, 0]))


def attend_backward(queries, keys, values_h, log_total, grad_context, length):
    seq_rows = queries.shape[0]
    valid_rows = (jnp.arange(seq_rows) < length).astype(jnp.float32)
    scores = jnp.einsum("qhd,khd->hqk", queries, keys, preferred_element_type=jnp.float32)
    scores = scores + ((valid_rows - 1.0) * 1e30)[None, None, :]
    attn_probs = jnp.exp(scores - jnp.transpose(log_total)[:, :, None])
    probs_low = attn_probs.astype(jnp.bfloat16)
    grad_masked = grad_context * valid_rows[:, None, None].astype(jnp.bfloat16)
    grad_values = jnp.einsum(
        "hqk,qhd->khd", probs_low, grad_masked, preferred_element_type=jnp.float32
    )
    grad_probs = jnp.einsum(
        "qhd,khd->hqk", grad_masked, values_h, preferred_element_type=jnp.float32
    )
    row_terms = jnp.sum(attn_probs * grad_probs, axis=-1, keepdims=True)
    grad_scores = (attn_probs * (grad_probs - row_terms)).astype(jnp.bfloat16)
    grad_queries = jnp.einsum("hqk,khd->qhd", grad_scores, keys, preferred_element_type=jnp.float32)
    grad_keys = jnp.einsum("hqk,qhd->khd", grad_scores, queries, preferred_element_type=jnp.float32)
    return (grad_queries, grad_keys, grad_values)


def attention_pass(kernel, length, arrays):
    return tuple(kernel(*arrays, length))


def shards(
    inputs,
    lengths,
    norm1_gain,
    norm1_shift,
    query_weight,
    query_bias,
    key_weight,
    key_bias,
    value_weight,
    value_bias,
    out_weight,
    out_bias,
    norm2_gain,
    norm2_shift,
    up_weight,
    up_bias,
    down_weight,
    down_bias,
    out_grad,
):
    seq_rows = inputs.shape[0]
    local_heads = query_weight.shape[1] // HEAD_DIM
    query_scale = HEAD_DIM ** (-0.5)
    cosine_table, sine_table = rotary_tables(seq_rows, HEAD_DIM)
    residual_in = inputs.astype(jnp.float32)
    normed, norm1_pull = jax.vjp(layer_norm, residual_in, norm1_gain, norm1_shift)
    normed_low = normed.astype(jnp.bfloat16)
    normed_all = lax.all_gather(normed_low, "tensor", axis=0, tiled=True)
    sequences = normed_all.shape[0] // seq_rows

    def heads_view(flat_rows):
        return flat_rows.reshape(sequences, seq_rows, local_heads, HEAD_DIM)

    def flatten_heads(shaped):
        return shaped.reshape(sequences * seq_rows, local_heads * HEAD_DIM)

    query_pre = jnp.dot(normed_all, query_weight, preferred_element_type=jnp.float32) + query_bias
    key_pre = jnp.dot(normed_all, key_weight, preferred_element_type=jnp.float32) + key_bias
    value_pre = jnp.dot(normed_all, value_weight, preferred_element_type=jnp.float32) + value_bias
    queries = (rotate(heads_view(query_pre), cosine_table, sine_table) * query_scale).astype(
        jnp.bfloat16
    )
    keys = rotate(heads_view(key_pre), cosine_table, sine_table).astype(jnp.bfloat16)
    values_h = heads_view(value_pre).astype(jnp.bfloat16)
    context, log_total = lax.map(
        lambda bundle: attention_pass(attend_forward, bundle[3], bundle[:3]),
        (queries, keys, values_h, lengths),
    )
    context_flat = flatten_heads(context)
    block_rows = context_flat
    attended = lax.psum_scatter(
        jnp.dot(block_rows, out_weight, preferred_element_type=jnp.float32).astype(jnp.bfloat16),
        "tensor",
        scatter_dimension=0,
        tiled=True,
    ).astype(jnp.float32)
    middle = residual_in + attended + out_bias
    normed2, norm2_pull = jax.vjp(layer_norm, middle, norm2_gain, norm2_shift)
    normed2_low = normed2.astype(jnp.bfloat16)
    normed2_all = lax.all_gather(normed2_low, "tensor", axis=0, tiled=True)
    hidden = jnp.dot(normed2_all, up_weight, preferred_element_type=jnp.float32) + up_bias
    activated, gelu_pull = jax.vjp(exact_gelu, hidden)
    activated_low = activated.astype(jnp.bfloat16)
    block_rows = activated_low
    ffn_out = lax.psum_scatter(
        jnp.dot(block_rows, down_weight, preferred_element_type=jnp.float32).astype(jnp.bfloat16),
        "tensor",
        scatter_dimension=0,
        tiled=True,
    ).astype(jnp.float32)
    layer_out = (middle + ffn_out + down_bias).astype(jnp.bfloat16)
    grad_out_all = lax.all_gather(out_grad, "tensor", axis=0, tiled=True)
    grad_down_weight = jnp.einsum(
        "rf,rd->fd", activated_low, grad_out_all, preferred_element_type=jnp.float32
    )
    grad_act = jnp.einsum(
        "rd,fd->rf", grad_out_all, down_weight, preferred_element_type=jnp.float32
    )
    grad_hidden = gelu_pull(grad_act)[0].astype(jnp.bfloat16)
    grad_up_weight = jnp.einsum(
        "rd,rf->df", normed2_all, grad_hidden, preferred_element_type=jnp.float32
    )
    grad_up_bias = jnp.sum(grad_hidden, axis=0, dtype=jnp.float32)
    block_rows = grad_hidden
    grad_normed2 = lax.psum_scatter(
        jnp.einsum("rf,df->rd", block_rows, up_weight, preferred_element_type=jnp.float32).astype(
            jnp.bfloat16
        ),
        "tensor",
        scatter_dimension=0,
        tiled=True,
    ).astype(jnp.float32)
    grad_middle_norm, grad_norm2_gain, grad_norm2_shift = norm2_pull(grad_normed2)
    out_grad_wide = out_grad.astype(jnp.float32)
    grad_middle = out_grad_wide + grad_middle_norm
    grad_down_bias = jnp.sum(out_grad_wide, axis=0)
    grad_out_bias = jnp.sum(grad_middle, axis=0)
    grad_middle_low = grad_middle.astype(jnp.bfloat16)
    grad_middle_all = lax.all_gather(grad_middle_low, "tensor", axis=0, tiled=True)
    grad_out_weight = jnp.einsum(
        "rk,rd->kd", context_flat, grad_middle_all, preferred_element_type=jnp.float32
    )
    grad_context = jnp.einsum(
        "rd,kd->rk", grad_middle_all, out_weight, preferred_element_type=jnp.float32
    ).astype(jnp.bfloat16)
    grad_queries, grad_keys, grad_values = lax.map(
        lambda bundle: attention_pass(attend_backward, bundle[5], bundle[:5]),
        (queries, keys, values_h, log_total, heads_view(grad_context), lengths),
    )
    grad_query_pre = flatten_heads(
        rotate_back(grad_queries * query_scale, cosine_table, sine_table)
    ).astype(jnp.bfloat16)
    grad_key_pre = flatten_heads(rotate_back(grad_keys, cosine_table, sine_table)).astype(
        jnp.bfloat16
    )
    grad_value_pre = flatten_heads(grad_values).astype(jnp.bfloat16)
    grad_query_weight = jnp.einsum(
        "rd,rk->dk", normed_all, grad_query_pre, preferred_element_type=jnp.float32
    )
    grad_key_weight = jnp.einsum(
        "rd,rk->dk", normed_all, grad_key_pre, preferred_element_type=jnp.float32
    )
    grad_value_weight = jnp.einsum(
        "rd,rk->dk", normed_all, grad_value_pre, preferred_element_type=jnp.float32
    )
    grad_query_bias = jnp.sum(grad_query_pre, axis=0, dtype=jnp.float32)
    grad_key_bias = jnp.sum(grad_key_pre, axis=0, dtype=jnp.float32)
    grad_value_bias = jnp.sum(grad_value_pre, axis=0, dtype=jnp.float32)
    partial_sum = jnp.einsum(
        "rk,dk->rd", grad_query_pre, query_weight, preferred_element_type=jnp.float32
    )
    partial_sum = partial_sum + jnp.einsum(
        "rk,dk->rd", grad_key_pre, key_weight, preferred_element_type=jnp.float32
    )
    grad_normed = lax.psum_scatter(
        (
            partial_sum
            + jnp.einsum(
                "rk,dk->rd", grad_value_pre, value_weight, preferred_element_type=jnp.float32
            )
        ).astype(jnp.bfloat16),
        "tensor",
        scatter_dimension=0,
        tiled=True,
    ).astype(jnp.float32)
    grad_input_norm, grad_norm1_gain, grad_norm1_shift = norm1_pull(grad_normed)
    input_grad = (grad_middle + grad_input_norm).astype(jnp.bfloat16)
    (
        grad_query_weight,
        grad_query_bias,
        grad_key_weight,
        grad_key_bias,
        grad_value_weight,
        grad_value_bias,
        grad_out_weight,
        grad_up_weight,
        grad_up_bias,
        grad_down_weight,
    ) = lax.psum(
        (
            grad_query_weight,
            grad_query_bias,
            grad_key_weight,
            grad_key_bias,
            grad_value_weight,
            grad_value_bias,
            grad_out_weight,
            grad_up_weight,
            grad_up_bias,
            grad_down_weight,
        ),
        "dp",
    )
    (
        grad_norm1_gain,
        grad_norm1_shift,
        grad_out_bias,
        grad_norm2_gain,
        grad_norm2_shift,
        grad_down_bias,
    ) = lax.psum(
        (
            grad_norm1_gain,
            grad_norm1_shift,
            grad_out_bias,
            grad_norm2_gain,
            grad_norm2_shift,
            grad_down_bias,
        ),
        ("dp", "tensor"),
    )
    return (
        layer_out,
        input_grad,
        grad_norm1_gain,
        grad_norm1_shift,
        grad_query_weight,
        grad_query_bias,
        grad_key_weight,
        grad_key_bias,
        grad_value_weight,
        grad_value_bias,
        grad_out_weight,
        grad_out_bias,
        grad_norm2_gain,
        grad_norm2_shift,
        grad_up_weight,
        grad_up_bias,
        grad_down_weight,
        grad_down_bias,
    )


def solution(mesh):
    return jax.shard_map(
        shards,
        mesh=mesh,
        in_specs=(
            P(("dp", "tensor"), None),
            P("dp"),
            P(),
            P(),
            P(None, "tensor"),
            P("tensor"),
            P(None, "tensor"),
            P("tensor"),
            P(None, "tensor"),
            P("tensor"),
            P("tensor", None),
            P(),
            P(),
            P(),
            P(None, "tensor"),
            P("tensor"),
            P("tensor", None),
            P(),
            P(("dp", "tensor"), None),
        ),
        out_specs=(
            P(("dp", "tensor"), None),
            P(("dp", "tensor"), None),
            P(),
            P(),
            P(None, "tensor"),
            P("tensor"),
            P(None, "tensor"),
            P("tensor"),
            P(None, "tensor"),
            P("tensor"),
            P("tensor", None),
            P(),
            P(),
            P(),
            P(None, "tensor"),
            P("tensor"),
            P("tensor", None),
            P(),
        ),
        check_vma=False,
    )
```

profile of v0, /device:TPU:0, one launch (start us, length us, event | category | flops | bytes accessed | tf_op | source)
XLA Modules:
  0.0 1169.8 jit_solution(10381343771209068899)
XLA Ops:
  13.8 47.1 %all-gather.5.cloned.1.call-done = bf16[2048,768]{1,0:T(8,128)(2,1)} async-done(((bf16[1024,768]{1,0:T(8,128)(2,1)}), bf16[2048,768]{1,0:T(8,128)(2,1)}) %all-gather.5.cloned.1.call-update) | async-done | bytes 3145744 | tf_op jit(solution)/shard_map/all_gather | solution.py:122
  115.6 80.9 %while.30 = (s32[]{:T(128)}, bf16[2,1024,6,64]{1,3,2,0:T(8,128)(2,1)}, f32[2,1024,6]{1,2,0:T(8,128)S(1)}, bf16[2,1024,6,64]{1,3,2,0:T(8,128)(2,1)}, bf16[2,1024,...) while((s32[]{:T(128)}, bf16[2,1024,6,64]{1,3,2,0:T(8,128)(2,1)}, ...), condition=%wide.region_5.6_spmd, body=%wide.region_2.5_spmd.sunk | while | flops 1661786112 | bytes 91580584 | solution.py:139
  117.5 13.4 %add_reduce_fusion.2 = (f32[6,1024]{1,0:T(8,128)S(1)}, f32[6,1024,1024]{1,2,0:T(8,128)}) fusion(f32[1024]{0:T(1024)S(1)} %add_multiply_fusion.2, bf16[2,1024,6,64]{1,3,2,0:T(8,128)(2,1)} %get-tuple-element.498, s32[]{:T(128)S(6)} %copy.110, bf16[2,1024,6,64]{1,3,2,0:T(8,128)(2,1)} %get-tuple-element.497), kind=kOutput, calls=%fused_computation.2.clone.1 | convolution fusion | flops 817883136 | bytes 26768384 | tf_op jit(solution)/shard_map/while/body/eval_jaxpr/qhd,khd->hqk/dot_general | solution.py:60
  157.9 13.4 %add_reduce_fusion.2 = (f32[6,1024]{1,0:T(8,128)S(1)}, f32[6,1024,1024]{1,2,0:T(8,128)}) fusion(f32[1024]{0:T(1024)S(1)} %add_multiply_fusion.2, bf16[2,1024,6,64]{1,3,2,0:T(8,128)(2,1)} %get-tuple-element.498, s32[]{:T(128)S(6)} %copy.110, bf16[2,1024,6,64]{1,3,2,0:T(8,128)(2,1)} %get-tuple-element.497), kind=kOutput, calls=%fused_computation.2.clone.1 | convolution fusion | flops 817883136 | bytes 26768384 | tf_op jit(solution)/shard_map/while/body/eval_jaxpr/qhd,khd->hqk/dot_general | solution.py:60
  204.9 43.4 %reduce-scatter.5.cloned.1.call-done = bf16[1024,768]{1,0:T(8,128)(2,1)} async-done(((bf16[2048,768]{1,0:T(8,128)(2,1)}), bf16[1024,768]{1,0:T(8,128)(2,1)}) %reduce-scatter.5.cloned.1.call-update) | async-done | bytes 1572880 | tf_op jit(solution)/shard_map/reduce_scatter | solution.py:145
  255.9 44.5 %all-gather.7.cloned.1.call-done = bf16[2048,768]{1,0:T(8,128)(2,1)} async-done(((bf16[1024,768]{1,0:T(8,128)(2,1)}), bf16[2048,768]{1,0:T(8,128)(2,1)}) %all-gather.7.cloned.1.call-update) | async-done | bytes 3145744 | tf_op jit(solution)/shard_map/all_gather | solution.py:154
  300.3 34.2 %multiply_convert_fusion.2 = (bf16[2048,1536]{1,0:T(8,128)(2,1)}, f32[2048,1536]{1,0:T(8,128)}, f32[2048,1536]{1,0:T(8,128)}) fusion(f32[1536]{0:T(1024)S(1)} %copy-done.69, bf16[2048,768]{1,0:T(8,128)(2,1)} %all-gather.7.cloned.1.call-done, bf16[768,1536]{1,0:T(8,128)(2,1)S(1)} %copy-done), kind=kOutput, calls=%fused_computation.63 | convolution fusion | flops 5039456256 | bytes 36968448 | tf_op jit(solution)/shard_map/dot_general | solution.py:155
  346.8 17.5 %convert_reduce_fusion = (f32[1536]{0:T(1024)}, bf16[2048,1536]{1,0:T(8,128)(2,1)S(1)}) fusion(f32[2048,1536]{1,0:T(8,128)} %get-tuple-element.339, bf16[2048,768]{1,0:T(8,128)(2,1)} %all-gather.9.cloned.1.call-done, bf16[1536,768]{1,0:T(8,128)(2,1)} %param.39, f32[2048,1536]{1,0:T(8,128)} %get-tuple-element.360, f32[1536]{0:T(1024)S(1)} %copy-done.69), kind=kOutput, calls=%fused_computation.61 | convolution fusion | flops 4885314048 | bytes 36974592 | tf_op jit(solution)/shard_map/rd,fd->rf/dot_general | solution.py:170
  384.7 32.1 %reduce-scatter.9.cloned.1.call-done = bf16[1024,768]{1,0:T(8,128)(2,1)} async-done(((bf16[2048,768]{1,0:T(8,128)(2,1)}), bf16[1024,768]{1,0:T(8,128)(2,1)}) %reduce-scatter.9.cloned.1.call-update) | async-done | bytes 1572880 | tf_op jit(solution)/shard_map/reduce_scatter | solution.py:179
  424.9 38.1 %reduce-scatter.7.cloned.1.call-done = bf16[1024,768]{1,0:T(8,128)(2,1)} async-done(((bf16[2048,768]{1,0:T(8,128)(2,1)}), bf16[1024,768]{1,0:T(8,128)(2,1)}) %reduce-scatter.7.cloned.1.call-update) | async-done | bytes 1572880 | tf_op jit(solution)/shard_map/reduce_scatter | solution.py:159
  471.8 45.0 %all-gather.11.cloned.1.call-done = bf16[2048,768]{1,0:T(8,128)(2,1)} async-done(((bf16[1024,768]{1,0:T(8,128)(2,1)}), bf16[2048,768]{1,0:T(8,128)(2,1)}) %all-gather.11.cloned.1.call-update) | async-done | bytes 3145744 | tf_op jit(solution)/shard_map/all_gather | solution.py:193
  528.8 284.5 %while.31 = (s32[]{:T(128)}, f32[2,1024,6,64]{1,0,3,2:T(2,128)}, f32[2,1024,6,64]{1,0,3,2:T(2,128)}, bf16[2,1024,6,64]{1,3,2,0:T(8,128)(2,1)}, bf16[2,1024,6,64]...) while((s32[]{:T(128)}, f32[2,1024,6,64]{1,0,3,2:T(2,128)}, ...), condition=%wide.region_15.16_spmd, body=%wide.region_13.15_spmd.sunk | while | flops 4102816768 | bytes 218039472 | solution.py:200
  530.8 13.1 %fusion.147 = f32[6,1024,1024]{1,2,0:T(8,128)} fusion(bf16[2,1024,6,64]{1,3,2,0:T(8,128)(2,1)} %get-tuple-element.530, s32[]{:T(128)S(6)} %copy.120, bf16[2,1024,6,64]{1,3,2,0:T(8,128)(2,1)} %get-tuple-element.529), kind=kOutput, calls=%fused_computation.38.clone.1 | convolution fusion | flops 805306368 | bytes 26739712 | tf_op jit(solution)/shard_map/while/body/eval_jaxpr/qhd,khd->hqk/dot_general | solution.py:72
  555.7 16.5 %multiply_reduce_fusion.3 = (f32[6,1024]{1,0:T(8,128)S(1)}, f32[6,1024,1024]{1,2,0:T(8,128)}) fusion(f32[6,1024,1024]{1,2,0:T(8,128)} %fusion.147, f32[6,1024]{1,0:T(8,128)S(1)} %dynamic-slice_bitcast_fusion.2, f32[1024]{0:T(1024)S(1)} %fusion.148, bf16[2,1024,6,64]{1,3,2,0:T(8,128)(2,1)} %get-tuple-element.534, s32[]{:T(128)S(6)} %copy.120, ...), kind=kOutput, calls=%fused_computation.27.clone.1 | convolution fusion | flops 830859264 | bytes 51960832 | tf_op jit(solution)/shard_map/while/body/eval_jaxpr/qhd,khd->hqk/dot_general | solution.py:80
  572.3 21.6 %multiply_convert_fusion.4 = bf16[6,1024,1024]{1,2,0:T(8,128)(2,1)} fusion(f32[6,1024,1024]{1,2,0:T(8,128)} %get-tuple-element.475, f32[6,1024,1024]{1,2,0:T(8,128)} %fusion.147, f32[6,1024]{1,0:T(8,128)S(1)} %get-tuple-element.476, f32[6,1024]{1,0:T(8,128)S(1)} %dynamic-slice_bitcast_fusion.2, f32[1024]{0:T(1024)S(1)} %fusion.148), kind=kLoop, calls=%fused_computation.26.clone.1 | loop fusion | flops 31457280 | bytes 62967808 | tf_op jit(solution)/shard_map/while/body/eval_jaxpr/convert_element_type | solution.py:84
  615.4 27.9 %dynamic_update_slice.45 = f32[2,1024,6,64]{1,0,3,2:T(2,128)} dynamic-update-slice(f32[2,1024,6,64]{1,0,3,2:T(2,128)} %get-tuple-element.515, f32[1,1024,6,64]{1,0,3,2:T(1,128)} %copy.101, s32[]{:T(128)S(6)} %copy.120, s32[]{:T(128)} %constant.136.clone.1..sunk, s32[]{:T(128)} %constant.136.clone.1..sunk, s32[]{:T(128)} %constant.136.clone.1..sunk) | dynamic-update-slice | bytes 3145732 | tf_op jit(solution)/shard_map/while/body/jit(dynamic_update_index_in_dim)/dynamic_update_slice | solution.py:200
  643.2 27.7 %dynamic_update_slice.44 = f32[2,1024,6,64]{1,0,3,2:T(2,128)} dynamic-update-slice(f32[2,1024,6,64]{1,0,3,2:T(2,128)} %get-tuple-element.514, f32[1,1024,6,64]{1,0,3,2:T(1,128)S(1)} %copy-done.6, s32[]{:T(128)S(6)} %copy.120, s32[]{:T(128)} %constant.136.clone.1..sunk, s32[]{:T(128)} %constant.136.clone.1..sunk, s32[]{:T(128)} %constant.136.clone.1..sunk) | dynamic-update-slice | bytes 3145732 | tf_op jit(solution)/shard_map/while/body/jit(dynamic_update_index_in_dim)/dynamic_update_slice | solution.py:200
  697.7 16.5 %multiply_reduce_fusion.3 = (f32[6,1024]{1,0:T(8,128)S(1)}, f32[6,1024,1024]{1,2,0:T(8,128)}) fusion(f32[6,1024,1024]{1,2,0:T(8,128)} %fusion.147, f32[6,1024]{1,0:T(8,128)S(1)} %dynamic-slice_bitcast_fusion.2, f32[1024]{0:T(1024)S(1)} %fusion.148, bf16[2,1024,6,64]{1,3,2,0:T(8,128)(2,1)} %get-tuple-element.534, s32[]{:T(128)S(6)} %copy.120, ...), kind=kOutput, calls=%fused_computation.27.clone.1 | convolution fusion | flops 830859264 | bytes 51960832 | tf_op jit(solution)/shard_map/while/body/eval_jaxpr/qhd,khd->hqk/dot_general | solution.py:80
  714.2 21.6 %multiply_convert_fusion.4 = bf16[6,1024,1024]{1,2,0:T(8,128)(2,1)} fusion(f32[6,1024,1024]{1,2,0:T(8,128)} %get-tuple-element.475, f32[6,1024,1024]{1,2,0:T(8,128)} %fusion.147, f32[6,1024]{1,0:T(8,128)S(1)} %get-tuple-element.476, f32[6,1024]{1,0:T(8,128)S(1)} %dynamic-slice_bitcast_fusion.2, f32[1024]{0:T(1024)S(1)} %fusion.148), kind=kLoop, calls=%fused_computation.26.clone.1 | loop fusion | flops 31457280 | bytes 62967808 | tf_op jit(solution)/shard_map/while/body/eval_jaxpr/convert_element_type | solution.py:84
  757.3 27.9 %dynamic_update_slice.45 = f32[2,1024,6,64]{1,0,3,2:T(2,128)} dynamic-update-slice(f32[2,1024,6,64]{1,0,3,2:T(2,128)} %get-tuple-element.515, f32[1,1024,6,64]{1,0,3,2:T(1,128)} %copy.101, s32[]{:T(128)S(6)} %copy.120, s32[]{:T(128)} %constant.136.clone.1..sunk, s32[]{:T(128)} %constant.136.clone.1..sunk, s32[]{:T(128)} %constant.136.clone.1..sunk) | dynamic-update-slice | bytes 3145732 | tf_op jit(solution)/shard_map/while/body/jit(dynamic_update_index_in_dim)/dynamic_update_slice | solution.py:200
  785.2 27.7 %dynamic_update_slice.44 = f32[2,1024,6,64]{1,0,3,2:T(2,128)} dynamic-update-slice(f32[2,1024,6,64]{1,0,3,2:T(2,128)} %get-tuple-element.514, f32[1,1024,6,64]{1,0,3,2:T(1,128)S(1)} %copy-done.6, s32[]{:T(128)S(6)} %copy.120, s32[]{:T(128)} %constant.136.clone.1..sunk, s32[]{:T(128)} %constant.136.clone.1..sunk, s32[]{:T(128)} %constant.136.clone.1..sunk) | dynamic-update-slice | bytes 3145732 | tf_op jit(solution)/shard_map/while/body/jit(dynamic_update_index_in_dim)/dynamic_update_slice | solution.py:200
  872.0 63.8 %all-reduce.1 = (f32[384]{0:T(512)}, f32[384]{0:T(512)}, f32[384]{0:T(512)}, f32[1536]{0:T(1024)}) all-reduce(f32[384]{0:T(512)S(1)} %reduce_sum.235, f32[384]{0:T(512)S(1)} %reduce_sum.237, f32[384]{0:T(512)S(1)} %reduce_sum.239, f32[1536]{0:T(1024)S(1)} %copy-done.58), channel_id=1, replica_groups=mesh['dp'=16,'tensor'=2] {'dp'}, use_global_device_ids=true, to_apply=%region_25.26 | all-reduce | flops 2688 | bytes 21504 | tf_op jit(solution)/shard_map/psum | solution.py:253
  940.6 39.4 %all-reduce = (f32[768]{0:T(1024)}, f32[768]{0:T(1024)}, f32[768]{0:T(1024)}, f32[768]{0:T(1024)}, f32[768]{0:T(1024)}, /*index=5*/f32[768]{0:T(1024)}) all-reduce(f32[768]{0:T(1024)S(1)} %get-tuple-element.276, f32[768]{0:T(1024)S(1)} %get-tuple-element.280, ...), channel_id=1, replica_groups=mesh['dp'=16,'tensor'=2] {'dp','tensor'}, use_global_device_ids=true, to_apply=%region_20.21 | all-reduce | flops 4608 | bytes 36864 | tf_op jit(solution)/shard_map/psum | solution.py:275
  983.9 168.2 %all-reduce.5.cloned.1.call-done = (f32[768,384]{1,0:T(8,128)}, f32[768,384]{1,0:T(8,128)}, f32[768,384]{1,0:T(8,128)}, f32[384,768]{1,0:T(8,128)}, f32[768,1536]{1,0:T(8,128)}, /*index=5*/f32[1536,768]{1,0:T(8,128)}) async-done(((f32[768,384]{1,0:T(8,128)}, f32[768,384]{1,0:T(8,128)}, f32[768,384]{1,0:T(8,128)}, f32[384,768]{1,0:T(8,128)}, f32[768,1536]{1,0:T(8,128)}, /*index=5*/f32[1536,768]{1,0:T(8,128)}), ...) | async-done | bytes 14155792 | tf_op jit(solution)/shard_map/psum | solution.py:253
  (296 shorter events, 353.5 us)
Async XLA Ops:
  7.2 293.2 %copy-start = (bf16[768,1536]{1,0:T(8,128)(2,1)S(1)}, bf16[768,1536]{1,0:T(8,128)(2,1)}, u32[]{:S(2)}) copy-start(bf16[768,1536]{1,0:T(8,128)(2,1)} %param.37) | copy-start | bytes 7077892
  7.2 53.7 %all-gather.5.cloned.1.call-start = ((), (), s32[]{:S(2)}) async-start(), calls=%async_computation.4 | async-start | bytes 4718592 | tf_op jit(solution)/shard_map/all_gather | solution.py:122
  9.1 51.8 %copy-start.32 = (bf16[768,384]{1,0:T(8,128)(2,1)S(1)}, bf16[768,384]{1,0:T(8,128)(2,1)}, u32[]{:S(2)}) copy-start(bf16[768,384]{1,0:T(8,128)(2,1)} %param.31) | copy-start | bytes 1769476
  9.2 51.8 %copy-start.70 = (f32[384]{0:T(512)S(1)}, f32[384]{0:T(512)}, u32[]{:S(2)}) copy-start(f32[384]{0:T(512)} %param.32) | copy-start | bytes 4612
  13.1 235.2 %reduce-scatter.5.cloned.1.call-start = ((), (), s32[]{:S(2)}) async-start(), calls=%async_computation.5 | async-start | bytes 4718592 | tf_op jit(solution)/shard_map/reduce_scatter | solution.py:145
  13.8 89.4 %copy-start.21 = (f32[1024,32]{0,1:T(8,128)}, f32[1024,32]{0,1:T(8,128)S(1)}, u32[]{:S(2)}) copy-start(f32[1024,32]{0,1:T(8,128)S(1)} %get-tuple-element.358) | copy-start | bytes 393220
  13.8 89.4 %copy-start.23 = (f32[1024,32]{0,1:T(8,128)}, f32[1024,32]{0,1:T(8,128)S(1)}, u32[]{:S(2)}) copy-start(f32[1024,32]{0,1:T(8,128)S(1)} %get-tuple-element.359) | copy-start | bytes 393220
  204.8 43.5 %copy-start.38 = (f32[768]{0:T(1024)S(1)}, f32[768]{0:T(1024)}, u32[]{:S(2)}) copy-start(f32[768]{0:T(1024)} %param.34) | copy-start | bytes 9220
  204.8 48.4 %copy-start.48 = (f32[768]{0:T(1024)S(1)}, f32[768]{0:T(1024)}, u32[]{:S(2)}) copy-start(f32[768]{0:T(1024)} %param.35) | copy-start | bytes 9220
  204.8 48.4 %copy-start.61 = (f32[768]{0:T(1024)S(1)}, f32[768]{0:T(1024)}, u32[]{:S(2)}) copy-start(f32[768]{0:T(1024)} %param.36) | copy-start | bytes 9220
  204.8 95.5 %all-gather.7.cloned.1.call-start = ((), (), s32[]{:S(2)}) async-start(), calls=%async_computation.6 | async-start | bytes 4718592 | tf_op jit(solution)/shard_map/all_gather | solution.py:154
  253.2 47.1 %copy-start.69 = (f32[1536]{0:T(1024)S(1)}, f32[1536]{0:T(1024)}, u32[]{:S(2)}) copy-start(f32[1536]{0:T(1024)} %param.38) | copy-start | bytes 18436
  255.3 91.5 %all-gather.9.cloned.1.call-start = ((), (), s32[]{:S(2)}) async-start(), calls=%async_computation.8 | async-start | bytes 4718592 | tf_op jit(solution)/shard_map/all_gather | solution.py:166
  255.8 161.0 %reduce-scatter.9.cloned.1.call-start = ((), (), s32[]{:S(2)}) async-start(), calls=%async_computation.9 | async-start | bytes 4718592 | tf_op jit(solution)/shard_map/reduce_scatter | solution.py:179
  373.4 89.6 %reduce-scatter.7.cloned.1.call-start = ((), (), s32[]{:S(2)}) async-start(), calls=%async_computation.7 | async-start | bytes 4718592 | tf_op jit(solution)/shard_map/reduce_scatter | solution.py:159
  384.2 132.5 %all-gather.11.cloned.1.call-start = ((), (), s32[]{:S(2)}) async-start(), calls=%async_computation.10 | async-start | bytes 4718592 | tf_op jit(solution)/shard_map/all_gather | solution.py:193
  470.3 46.5 %copy-start.68 = (bf16[384,768]{1,0:T(8,128)(2,1)S(1)}, bf16[384,768]{1,0:T(8,128)(2,1)}, u32[]{:S(2)}) copy-start(bf16[384,768]{1,0:T(8,128)(2,1)} %param.33) | copy-start | bytes 1769476
  471.7 464.1 %reduce-scatter.11.cloned.1.call-start = ((), (), s32[]{:S(2)}) async-start(), calls=%async_computation.11 | async-start | bytes 4718592 | tf_op jit(solution)/shard_map/reduce_scatter | solution.py:229
  840.0 312.1 %all-reduce.5.cloned.1.call-start = ((), (), s32[]{:S(2)}) async-start(), calls=%async_computation.12 | async-start | bytes 28311552 | tf_op jit(solution)/shard_map/psum | solution.py:253
  869.9 65.9 %copy-start.5 = (bf16[1024,768]{1,0:T(8,128)(2,1)S(1)}, bf16[1024,768]{1,0:T(8,128)(2,1)}, u32[]{:S(2)}) copy-start(bf16[1024,768]{1,0:T(8,128)(2,1)} %param.23) | copy-start | bytes 4718596
  869.9 65.9 %copy-start.37 = (f32[1024]{0:T(1024)S(1)}, f32[1024]{0:T(1024)}, u32[]{:S(2)}) copy-start(f32[1024]{0:T(1024)} %copy-done.36) | copy-start | bytes 12292
  869.9 65.9 %copy-start.43 = (f32[768]{0:T(1024)S(1)}, f32[768]{0:T(1024)}, u32[]{:S(2)}) copy-start(f32[768]{0:T(1024)} %param.25) | copy-start | bytes 9220
  869.9 68.6 %copy-start.51 = (f32[1024]{0:T(1024)S(1)}, f32[1024]{0:T(1024)}, u32[]{:S(2)}) copy-start(f32[1024]{0:T(1024)} %copy-done.50) | copy-start | bytes 12292
  869.9 68.6 %copy-start.45 = (f32[1024]{0:T(1024)S(1)}, f32[1024]{0:T(1024)}, u32[]{:S(2)}) copy-start(f32[1024]{0:T(1024)} %copy-done.44) | copy-start | bytes 12292
  (66 other events, 533.8 us)
Sparse Core Ops, SparseCore 0:
  13.2 47.6 all-gather.4
  204.9 43.3 reduce-scatter.4
  255.4 44.9 all-gather.6
  301.8 44.9 all-gather.8
  373.5 43.3 reduce-scatter.8
  419.5 43.3 reduce-scatter.6
  471.8 44.9 all-gather.10
  840.2 43.3 reduce-scatter.10
  890.4 261.6 all-reduce.4
where the time goes:
time: 1180 us; the launch traced here: 1170 us
  waiting for transfers between devices  431 us (37%)
  matrix products  294 us (25%)
  local copies, waits for them, and re-layouts  194 us (16%)
  other arithmetic  131 us (11%)
  blocking collectives  103 us (9%)
  between operations  14.9 us (1%)
    psum x1, waiting for transfers between devices, shards(): lax.psum((grad_query_weight, grad_query_bias, grad_key_weight, grad_key_b...  168 us
    dynamic_update_slice x8, local copies, waits for them, and re-layouts, shards(): lax.map(lambda bundle: attention_pass(attend_backward, bundle[5], bundle[...  122 us
    psum x1, blocking collectives, shards(): lax.psum((grad_query_weight, grad_query_bias, grad_key_weight, grad_key_b...  63.8 us
    all_gather x1, waiting for transfers between devices, shards(): normed_all = lax.all_gather(normed_low, 'tensor', axis=0, tiled=True)  47.1 us
    all_gather x1, waiting for transfers between devices, shards(): lax.all_gather(grad_middle_low, 'tensor', axis=0, tiled=True)  45 us
    all_gather x1, waiting for transfers between devices, shards(): normed2_all = lax.all_gather(normed2_low, 'tensor', axis=0, tiled=True)  44.5 us
    reduce_scatter x1, waiting for transfers between devices, shards(): lax.psum_scatter(jnp.dot(block_rows, out_weight, preferred_element_type=j...  43.4 us
    convert_element_type x2, other arithmetic, attend_backward(): grad_scores = (attn_probs * (grad_probs - row_terms)).astype(jnp.bfloat16)  43.2 us
  transfers between devices with their start and end apart: 9, of which 8 were waited for; matrix products, arithmetic and copies ran while one was open for 8% of the time, Pallas kernels for 0%

commit v1 on v0

v1 whole, which is shorter than its diff:
```python
import math

import jax
import jax.numpy as jnp
import numpy as np
from jax import lax
from jax.experimental import pallas as pl
from jax.experimental.pallas import tpu as pltpu
from jax.sharding import PartitionSpec as P

HEAD_DIM = 64
EPS = 1e-05
LOG2E = math.log2(math.e)
LN2 = math.log(2.0)
F32 = jnp.float32
BF = jnp.bfloat16
VMEM_LIMIT = 56 << 20
BIG = -1e30


def dot(a, b, ca=1, cb=0):
    return lax.dot_general(a, b, (((ca,), (cb,)), ((), ())), preferred_element_type=F32)


def params():
    return pltpu.CompilerParams(vmem_limit_bytes=VMEM_LIMIT)


def cost(macs, nbytes, exps=0):
    return pl.CostEstimate(flops=int(2 * macs), bytes_accessed=int(nbytes), transcendentals=int(exps))


def struct(shape, dtype):
    return jax.ShapeDtypeStruct(shape, dtype)


def whole(shape):
    return pl.BlockSpec(shape, lambda *_: (0,) * len(shape), pipeline_mode=pl.Buffered(1))


def whole_out(shape):
    return pl.BlockSpec(shape, lambda *_: (0,) * len(shape))


def norm_rows(v):
    mean = jnp.mean(v, axis=1, keepdims=True)
    cent = v - mean
    var = jnp.mean(cent * cent, axis=1, keepdims=True)
    r = lax.rsqrt(var + EPS)
    return cent * r, r


def norm_back(e, n, r):
    return r * (e - jnp.mean(e, axis=1, keepdims=True) - n * jnp.mean(e * n, axis=1, keepdims=True))


def rotary_tables(rows):
    half = HEAD_DIM // 2
    freq = (10000.0 ** (-2.0 * np.arange(half, dtype=np.float32) / HEAD_DIM)).astype(np.float32)
    ang = (np.arange(rows, dtype=np.float32)[:, None] * freq[None, :]).astype(np.float64)
    cos = np.cos(ang).astype(np.float32)
    sin = np.sin(ang).astype(np.float32)
    return np.concatenate([cos] * 4, 1), np.concatenate([-sin, sin] * 2, 1)


def swap_halves(v):
    lane = lax.broadcasted_iota(jnp.int32, v.shape, 1)
    return jnp.where((lane & 32) == 0, pltpu.roll(v, 96, 1), pltpu.roll(v, 32, 1))


def rotate(v, cos, sin):
    return v * cos + swap_halves(v) * sin


def rotate_back(v, cos, sin):
    return v * cos - swap_halves(v) * sin


def put_qkv(pre, cos, sin, q_ref, k_ref, v_ref):
    width = q_ref.shape[1]
    for i in range(width // 128):
        sl = slice(i * 128, (i + 1) * 128)
        q_ref[:, sl] = (rotate(pre[0][:, sl], cos, sin) * (LOG2E / 8.0)).astype(BF)
        k_ref[:, sl] = rotate(pre[1][:, sl], cos, sin).astype(BF)
        v_ref[:, sl] = pre[2][:, sl].astype(BF)


def project_own_kernel(
    x_ref, gain_ref, shift_ref, wq_ref, wk_ref, wv_ref, b_ref, cos_ref, sin_ref,
    n_ref, nt_ref, q_ref, k_ref, v_ref,
):
    width = q_ref.shape[1]
    n, _ = norm_rows(x_ref[...].astype(F32))
    low = (n * gain_ref[...] + shift_ref[...]).astype(BF)
    n_ref[...] = low
    nt_ref[...] = low.T
    pre = [
        dot(low, w[...]) + b_ref[:, i * width : (i + 1) * width]
        for i, w in enumerate((wq_ref, wk_ref, wv_ref))
    ]
    put_qkv(pre, cos_ref[...], sin_ref[...], q_ref, k_ref, v_ref)


def project_other_kernel(n_ref, w_ref, b_ref, cos_ref, sin_ref, q_ref, k_ref, v_ref):
    width = q_ref.shape[1]
    low = n_ref[...]
    pre = [
        dot(low, w_ref[:, i * width : (i + 1) * width]) + b_ref[:, i * width : (i + 1) * width]
        for i in range(3)
    ]
    put_qkv(pre, cos_ref[...], sin_ref[...], q_ref, k_ref, v_ref)


def project_own(x, gain, shift, wq, wk, wv, bias, cos, sin):
    rows, d = x.shape
    width = wq.shape[1]
    blk = 256
    row = lambda w: pl.BlockSpec((blk, w), lambda i: (i, 0))
    return pl.pallas_call(
        project_own_kernel,
        grid=(rows // blk,),
        in_specs=[row(d), whole((1, d)), whole((1, d))]
        + [whole((d, width))] * 3
        + [whole((1, 3 * width)), row(128), row(128)],
        out_specs=[row(d), pl.BlockSpec((d, blk), lambda i: (0, i))] + [row(width)] * 3,
        out_shape=[struct((rows, d), BF), struct((d, rows), BF)] + [struct((rows, width), BF)] * 3,
        compiler_params=params(),
        cost_estimate=cost(rows * d * width * 3, 12e6),
        name="project_own",
    )(x, gain, shift, wq, wk, wv, bias, cos, sin)


def project_other(n, w, bias, cos, sin):
    rows, d = n.shape
    width = w.shape[1] // 3
    blk = 256
    row = lambda w_: pl.BlockSpec((blk, w_), lambda i: (i, 0))
    return pl.pallas_call(
        project_other_kernel,
        grid=(rows // blk,),
        in_specs=[row(d), whole((d, 3 * width)), whole((1, 3 * width)), row(128), row(128)],
        out_specs=[row(width)] * 3,
        out_shape=[struct((rows, width), BF)] * 3,
        compiler_params=params(),
        cost_estimate=cost(rows * d * width * 3, 8e6),
        name="project_other",
    )(n, w, bias, cos, sin)


def split3(v):
    hi = v.astype(BF)
    rest = v - hi.astype(F32)
    mid = rest.astype(BF)
    lo = rest - mid.astype(F32)
    return hi.astype(F32), mid.astype(F32), lo


def spread(lane, first, one, two):
    out = jnp.where(lane == 0, first, 0.0)
    for at, part in enumerate((*split3(one), *split3(two))):
        out = jnp.where(lane == at + 1, part, out)
    return out.astype(BF)


def attend_kernel(bq, len_ref, q_ref, k_ref, v_ref, ctx_ref, aug_ref):
    rows = q_ref.shape[0]
    length = len_ref[0]
    lane1 = lax.broadcasted_iota(jnp.int32, (1, 128), 1)
    krow = lax.broadcasted_iota(jnp.int32, (rows, 128), 0)
    klane = lax.broadcasted_iota(jnp.int32, (rows, 128), 1)
    lane = lax.broadcasted_iota(jnp.int32, (bq, 128), 1)
    qrow = lax.broadcasted_iota(jnp.int32, (bq, 128), 0)
    kaug = jnp.where((klane == 0) & (krow >= length), BIG, 0.0).astype(BF)
    k = jnp.concatenate([k_ref[...], kaug], 1)
    v = jnp.concatenate([v_ref[...], jnp.ones((rows, 128), BF)], 1)
    qaug = jnp.where(lane == 0, 1.0, 0.0).astype(BF)
    for i in range(rows // bq):
        sl = slice(i * bq, (i + 1) * bq)
        q = q_ref[sl, :]
        outs, totals = [], []
        for h in range(2):
            keep = ((lane1 < 64) if h == 0 else (lane1 >= 64)).astype(BF)
            s = dot(jnp.concatenate([q * keep, qaug], 1), k, 1, 1)
            top = jnp.max(s, axis=1, keepdims=True)
            p = jnp.exp2(s - top).astype(BF)
            o = dot(p, v)
            total = o[:, 128:]
            outs.append(o[:, :128] / total)
            totals.append(top + jnp.log2(total))
        ctx = jnp.where(lane < 64, outs[0], outs[1])
        ctx_ref[sl, :] = jnp.where(qrow + i * bq < length, ctx, 0.0).astype(BF)
        aug_ref[sl, :] = spread(lane, 1.0, totals[0], totals[1])


def attend(length, q, k, v):
    rows, width = q.shape
    bs = pl.BlockSpec((rows, 128), lambda j, *_: (0, j))
    heads = width // HEAD_DIM
    return pl.pallas_call(
        lambda *refs: attend_kernel(256, *refs),
        grid_spec=pltpu.PrefetchScalarGridSpec(
            num_scalar_prefetch=1, grid=(width // 128,), in_specs=[bs] * 3, out_specs=[bs] * 2
        ),
        out_shape=[struct((rows, width), BF)] * 2,
        compiler_params=params(),
        cost_estimate=cost(heads * rows * rows * 256 * 2, rows * width * 10, heads * rows * rows),
        name="attend",
    )(length, q, k, v)


def attend_back_kernel(
    bq, len_ref, q_ref, k_ref, v_ref, g_ref, ctx_ref, aug_ref, cos_ref, sin_ref,
    dq_ref, dk_ref, dv_ref, sum_ref, dqt,
):
    rows = q_ref.shape[0]
    length = len_ref[0]
    lane1 = lax.broadcasted_iota(jnp.int32, (1, 128), 1)
    krow = lax.broadcasted_iota(jnp.int32, (rows, 128), 0)
    klane = lax.broadcasted_iota(jnp.int32, (rows, 128), 1)
    lane = lax.broadcasted_iota(jnp.int32, (bq, 128), 1)
    k = k_ref[...]
    v = v_ref[...]
    kt = k.T
    dks, dvs = [], []
    for h in range(2):
        keep = ((lane1 < 64) if h == 0 else (lane1 >= 64)).astype(BF)
        first = 1 + 3 * h
        mine = jnp.where((klane >= first) & (klane < first + 3), -1.0, 0.0)
        kaug = jnp.where((klane == 0) & (krow >= length), BIG, mine).astype(BF)
        kh = jnp.concatenate([k * keep, kaug], 1)
        vh = jnp.concatenate([v * keep, mine.astype(BF)], 1)
        dk = jnp.zeros((rows, 128), F32)
        dv = jnp.zeros((rows, 128), F32)
        for i in range(rows // bq):
            sl = slice(i * bq, (i + 1) * bq)
            q = q_ref[sl, :]
            g = g_ref[sl, :]
            prod = g.astype(F32) * ctx_ref[sl, :].astype(F32)
            d0 = jnp.sum(jnp.where(lane < 64, prod, 0.0), 1, keepdims=True)
            d1 = jnp.sum(jnp.where(lane < 64, 0.0, prod), 1, keepdims=True)
            gaug = spread(lane, 0.0, d0, d1)
            st = dot(kh, jnp.concatenate([q, aug_ref[sl, :]], 1), 1, 1)
            pt = jnp.exp2(st)
            dpt = dot(vh, jnp.concatenate([g, gaug], 1), 1, 1)
            ds = (pt * dpt).astype(BF)
            dv = dv + dot(pt.astype(BF), g)
            dk = dk + dot(ds, q)
            dqt[h * 64 : (h + 1) * 64, sl] = dot(kt[h * 64 : (h + 1) * 64, :], ds)
        dks.append(dk)
        dvs.append(dv)
    cos = cos_ref[...]
    sin = sin_ref[...]
    dq = rotate_back(dqt[...].T * (1.0 / 8.0), cos, sin).astype(BF)
    dk = rotate_back(jnp.where(klane < 64, dks[0], dks[1]) * LN2, cos, sin).astype(BF)
    dv = jnp.where(klane < 64, dvs[0], dvs[1]).astype(BF)
    for at, (ref, val) in enumerate(((dq_ref, dq), (dk_ref, dk), (dv_ref, dv))):
        ref[...] = val
        sum_ref[at : at + 1, :] = jnp.sum(val.astype(F32), axis=0, keepdims=True)
    sum_ref[3:, :] = jnp.zeros((5, 128), F32)


def attend_back(length, q, k, v, g, ctx, aug, cos, sin):
    rows, width = q.shape
    bs = pl.BlockSpec((rows, 128), lambda j, *_: (0, j))
    heads = width // HEAD_DIM
    return pl.pallas_call(
        lambda *refs: attend_back_kernel(256, *refs),
        grid_spec=pltpu.PrefetchScalarGridSpec(
            num_scalar_prefetch=1,
            grid=(width // 128,),
            in_specs=[bs] * 6 + [whole((rows, 128))] * 2,
            out_specs=[bs] * 3 + [pl.BlockSpec((8, 128), lambda j, *_: (0, j))],
            scratch_shapes=[pltpu.VMEM((128, rows), F32)],
        ),
        out_shape=[struct((rows, width), BF)] * 3 + [struct((8, width), F32)],
        compiler_params=params(),
        cost_estimate=cost(heads * rows * rows * 256 * 5, rows * width * 18, heads * rows * rows),
        name="attend_back",
    )(length, q, k, v, g, ctx, aug, cos, sin)


def gelu_pair(h):
    z = jnp.abs(h) * (0.3275911 / math.sqrt(2.0)) + 1.0
    t = pl.reciprocal(z, approx=True)
    t = t * (2.0 - z * t)
    e = jnp.exp2(h * h * (-0.5 * LOG2E))
    poly = 0.5 * 1.061405429 * t - 0.5 * 1.453152027
    poly = poly * t + 0.5 * 1.421413741
    poly = poly * t - 0.5 * 0.284496736
    poly = poly * t + 0.5 * 0.254829592
    w = poly * t * e
    cdf = jnp.where(h >= 0.0, 1.0 - w, w)
    return h * cdf, cdf + h * e * (1.0 / math.sqrt(2.0 * math.pi))


def ffn_tile(n2, n2t, og, wu_ref, wd_ref, b_ref, out_acc, dn_acc, act_s, dh_s, first):
    rows = og.shape[0]
    blk = 256
    wu = wu_ref[...]
    wd = wd_ref[...]
    bias = b_ref[...]
    dbias = jnp.zeros((1, wu.shape[1]), F32)
    for i in range(rows // blk):
        sl = slice(i * blk, (i + 1) * blk)
        h = dot(n2[sl, :], wu) + bias
        act, slope = gelu_pair(h)
        act = act.astype(BF)
        dh = (slope * dot(og[sl, :], wd, 1, 1)).astype(BF)
        act_s[sl, :] = act
        dh_s[sl, :] = dh
        dbias = dbias + jnp.sum(dh.astype(F32), axis=0, keepdims=True)
        out_acc[sl, :] += dot(act, wd)
        dn_acc[sl, :] += dot(dh, wu, 1, 1)
    return dot(act_s[...], og[...], 0, 0), dot(n2t[...], dh_s[...]), dbias


def ffn_own_kernel(
    per, c_ref, x_ref, co_ref, cx_ref, woo_ref, wox_ref, ob_ref, gain_ref, shift_ref, og_ref, wu_ref, wd_ref, b_ref,
    mid_ref, n2_ref, n2t_ref, out_ref, dn_ref, ddo_ref, dup_ref, ddk_ref, dupk_ref, db_ref, act_s, dh_s,
):
    j = pl.program_id(0)
    rows = x_ref.shape[0]

    @pl.when(j == 0)
    def _():
        @pl.loop(0, rows // 256)
        def _(i):
            sl = pl.ds(pl.multiple_of(i * 256, 256), 256)
            att = dot(co_ref[sl, :], woo_ref[...]) + dot(cx_ref[sl, :], wox_ref[...])
            mid = x_ref[sl, :].astype(F32) + att + ob_ref[...]
            mid_ref[sl, :] = mid
            n, _ = norm_rows(mid)
            low = (n * gain_ref[...] + shift_ref[...]).astype(BF)
            n2_ref[sl, :] = low
            n2t_ref[:, sl] = low.T
            out_ref[sl, :] = jnp.zeros_like(mid)
            dn_ref[sl, :] = jnp.zeros_like(mid)

    dwd, dwu, db = ffn_tile(
        n2_ref, n2t_ref, og_ref, wu_ref, wd_ref, b_ref, out_ref, dn_ref, act_s, dh_s, False
    )
    db_ref[...] = db

    @pl.when(j < per)
    def _():
        ddo_ref[...] = dwd.astype(BF)
        dup_ref[...] = dwu.astype(BF)

    @pl.when(j >= per)
    def _():
        ddk_ref[...] = dwd.astype(BF)
        dupk_ref[...] = dwu.astype(BF)


TILE = 256


def send_keep_specs(per, d):
    send = lambda j: jnp.minimum(j, per - 1)
    keep = lambda j: jnp.maximum(j - per, 0)
    return [
        pl.BlockSpec((TILE, d), lambda j, *_: (send(j), 0)),
        pl.BlockSpec((d, TILE), lambda j, *_: (0, send(j))),
        pl.BlockSpec((TILE, d), lambda j, *_: (keep(j), 0)),
        pl.BlockSpec((d, TILE), lambda j, *_: (0, keep(j))),
    ]


def ffn_own(core, x, ctx_own, ctx_other, wo_own, wo_other, ob, gain, shift, og, wu, wd, bias):
    rows, d = x.shape
    ff = wu.shape[1]
    tiles = ff // TILE
    per = tiles // 2
    half = ctx_own.shape[1]
    tile = lambda j, c: jnp.where(j < per, (1 - c[0]) * per + j, c[0] * per + j - per)
    return pl.pallas_call(
        lambda *refs: ffn_own_kernel(per, *refs),
        grid_spec=pltpu.PrefetchScalarGridSpec(
            num_scalar_prefetch=1,
            grid=(tiles,),
            in_specs=[
                whole((rows, d)), whole((rows, half)), whole((rows, half)), whole((half, d)), whole((half, d)),
                whole((1, d)), whole((1, d)), whole((1, d)), whole((rows, d)),
                pl.BlockSpec((d, TILE), lambda j, c: (0, tile(j, c))),
                pl.BlockSpec((TILE, d), lambda j, c: (tile(j, c), 0)),
                pl.BlockSpec((1, TILE), lambda j, c: (0, tile(j, c))),
            ],
            out_specs=[whole_out((rows, d)), whole_out((rows, d)), whole_out((d, rows)), whole_out((rows, d)), whole_out((rows, d))]
            + send_keep_specs(per, d)
            + [pl.BlockSpec((1, TILE), lambda j, c: (0, tile(j, c)))],
            scratch_shapes=[pltpu.VMEM((rows, TILE), BF), pltpu.VMEM((rows, TILE), BF)],
        ),
        out_shape=[
            struct((rows, d), F32), struct((rows, d), BF), struct((d, rows), BF), struct((rows, d), F32), struct((rows, d), F32),
            struct((ff // 2, d), BF), struct((d, ff // 2), BF), struct((ff // 2, d), BF), struct((d, ff // 2), BF),
            struct((1, ff), F32),
        ],
        compiler_params=params(),
        cost_estimate=cost(rows * d * (ff * 6 + d), 40e6, rows * ff),
        name="ffn_own",
    )(core, x, ctx_own, ctx_other, wo_own, wo_other, ob, gain, shift, og, wu, wd, bias)


def ffn_other_kernel(
    per, c_ref, len_ref, mid_ref, n2_ref, n2t_ref, out_ref, dn_ref, og_ref,
    wua_ref, wda_ref, wub_ref, wdb_ref, b_ref, co_ref, cx_ref, woo_ref, wox_ref, gain_ref, db_in_ref,
    lay_ref, gm_ref, dco_ref, dcx_ref, dwoo_ref, dwox_ref, sums_ref,
    dds_ref, dus_ref, ddk_ref, duk_ref, db_ref, act_s, dh_s, out_s, dn_s, gmb_s,
):
    j = pl.program_id(0)
    rows, d = og_ref.shape

    @pl.when(j == 0)
    def _():
        out_s[...] = out_ref[...]
        dn_s[...] = dn_ref[...]

    @pl.when(j < per)
    def _():
        dwd, dwu, db = ffn_tile(
            n2_ref, n2t_ref, og_ref, wua_ref, wda_ref, b_ref, out_s, dn_s, act_s, dh_s, False
        )
        db_ref[...] = db
        dds_ref[...] = dwd.astype(BF)
        dus_ref[...] = dwu.astype(BF)

    @pl.when(j >= per)
    def _():
        dwd, dwu, db = ffn_tile(
            n2_ref, n2t_ref, og_ref, wub_ref, wdb_ref, b_ref, out_s, dn_s, act_s, dh_s, False
        )
        db_ref[...] = db
        ddk_ref[...] = dwd.astype(BF)
        duk_ref[...] = dwu.astype(BF)

    @pl.when(j == 2 * per - 1)
    def _():
        length = len_ref[0]
        sums_ref[...] = jnp.zeros_like(sums_ref)

        @pl.loop(0, rows // 256)
        def _(i):
            sl = pl.ds(pl.multiple_of(i * 256, 256), 256)
            mid = mid_ref[sl, :]
            lay_ref[sl, :] = (mid + out_s[sl, :] + db_in_ref[...]).astype(BF)
            n, r = norm_rows(mid)
            gn = dn_s[sl, :]
            og = og_ref[sl, :].astype(F32)
            gm = og + norm_back(gn * gain_ref[...], n, r)
            gm_ref[sl, :] = gm
            low = gm.astype(BF)
            gmb_s[sl, :] = low
            for at, val in enumerate((gn * n, gn, gm, og)):
                sums_ref[at : at + 1, :] += jnp.sum(val, axis=0, keepdims=True)
            valid = lax.broadcasted_iota(jnp.int32, (256, 1), 0) + i * 256 < length
            dco_ref[sl, :] = jnp.where(valid, dot(low, woo_ref[...], 1, 1), 0.0).astype(BF)
            dcx_ref[sl, :] = jnp.where(valid, dot(low, wox_ref[...], 1, 1), 0.0).astype(BF)

        dwoo_ref[...] = dot(co_ref[...], gmb_s[...], 0, 0).astype(BF)
        dwox_ref[...] = dot(cx_ref[...], gmb_s[...], 0, 0).astype(BF)


def ffn_other(core, length, mid, n2, n2t, out, dn, og, wua, wda, wub, wdb, bias, ctx_own, ctx_other, wo_own, wo_other, gain, db_in):
    rows, d = og.shape
    part = wua.shape[1]
    per = part // TILE
    half = ctx_own.shape[1]
    ia = lambda j: jnp.minimum(j, per - 1)
    ib = lambda j: jnp.maximum(j - per, 0)
    tile = lambda j, c: jnp.where(j < per, (1 - c[0]) * per + j, c[0] * per + j - per)
    return pl.pallas_call(
        lambda *refs: ffn_other_kernel(per, *refs),
        grid_spec=pltpu.PrefetchScalarGridSpec(
            num_scalar_prefetch=2,
            grid=(2 * per,),
            in_specs=[
                whole((rows, d)), whole((rows, d)), whole((d, rows)), whole((rows, d)), whole((rows, d)), whole((rows, d)),
                pl.BlockSpec((d, TILE), lambda j, *_: (0, ia(j))),
                pl.BlockSpec((TILE, d), lambda j, *_: (ia(j), 0)),
                pl.BlockSpec((d, TILE), lambda j, *_: (0, ib(j))),
                pl.BlockSpec((TILE, d), lambda j, *_: (ib(j), 0)),
                pl.BlockSpec((1, TILE), lambda j, c, n: (0, tile(j, c))),
                whole((rows, half)), whole((rows, half)), whole((half, d)), whole((half, d)), whole((1, d)), whole((1, d)),
            ],
            out_specs=[
                whole_out((rows, d)), whole_out((rows, d)), whole_out((rows, half)), whole_out((rows, half)),
                whole_out((half, d)), whole_out((half, d)), whole_out((8, d)),
            ]
            + send_keep_specs(per, d)
            + [pl.BlockSpec((1, TILE), lambda j, c, n: (0, tile(j, c)))],
            scratch_shapes=[
                pltpu.VMEM((rows, TILE), BF), pltpu.VMEM((rows, TILE), BF),
                pltpu.VMEM((rows, d), F32), pltpu.VMEM((rows, d), F32), pltpu.VMEM((rows, d), BF),
            ],
        ),
        out_shape=[
            struct((rows, d), BF), struct((rows, d), F32), struct((rows, half), BF), struct((rows, half), BF),
            struct((half, d), BF), struct((half, d), BF), struct((8, d), F32),
            struct((part, d), BF), struct((d, part), BF), struct((part, d), BF), struct((d, part), BF),
            struct((1, 2 * part), F32),
        ],
        compiler_params=params(),
        cost_estimate=cost(rows * d * (part * 12 + 2 * d), 50e6, rows * part * 2),
        name="ffn_other",
    )(core, length, mid, n2, n2t, out, dn, og, wua, wda, wub, wdb, bias, ctx_own, ctx_other, wo_own, wo_other, gain, db_in)


def project_grad_kernel(c_ref, nt_ref, dq_ref, dk_ref, dv_ref, send_ref, keep_ref):
    half = send_ref.shape[0]
    width = dq_ref.shape[1]
    c = c_ref[0]
    for ref, part in ((send_ref, 1 - c), (keep_ref, c)):
        nt = nt_ref[pl.ds(pl.multiple_of(part * half, half), half), :]
        for i, g in enumerate((dq_ref, dk_ref, dv_ref)):
            ref[:, i * width : (i + 1) * width] = dot(nt, g[...]).astype(BF)


def project_grad(core, nt, dq, dk, dv):
    d, rows = nt.shape
    width = dq.shape[1]
    return pl.pallas_call(
        project_grad_kernel,
        grid_spec=pltpu.PrefetchScalarGridSpec(
            num_scalar_prefetch=1,
            grid=(1,),
            in_specs=[whole((d, rows))] + [whole((rows, width))] * 3,
            out_specs=[whole_out((d // 2, 3 * width))] * 2,
        ),
        out_shape=[struct((d // 2, 3 * width), BF)] * 2,
        compiler_params=params(),
        cost_estimate=cost(rows * d * width * 3, 6e6),
        name="project_grad",
    )(core, nt, dq, dk, dv)


def input_grad_kernel(
    x_ref, gm_ref, gain_ref, q0, k0, v0, wq_ref, wk_ref, wv_ref, q1, k1, v1, wx_ref, out_ref, sums_ref
):
    width = q0.shape[1]
    wx = [wx_ref[:, i * width : (i + 1) * width] for i in range(3)]
    gn = jnp.zeros(gm_ref.shape, F32)
    for g, w in ((q0, wq_ref[...]), (k0, wk_ref[...]), (v0, wv_ref[...]), (q1, wx[0]), (k1, wx[1]), (v1, wx[2])):
        gn = gn + dot(g[...], w, 1, 1)
    n, r = norm_rows(x_ref[...].astype(F32))
    out_ref[...] = (gm_ref[...] + norm_back(gn * gain_ref[...], n, r)).astype(BF)

    @pl.when(pl.program_id(0) == 0)
    def _():
        sums_ref[...] = jnp.zeros_like(sums_ref)

    sums_ref[0:1, :] += jnp.sum(gn * n, axis=0, keepdims=True)
    sums_ref[1:2, :] += jnp.sum(gn, axis=0, keepdims=True)


def input_grad(x, gm, gain, own, wq, wk, wv, other, wx):
    rows, d = x.shape
    width = wq.shape[1]
    blk = 256
    row = lambda w: pl.BlockSpec((blk, w), lambda i: (i, 0))
    return pl.pallas_call(
        input_grad_kernel,
        grid=(rows // blk,),
        in_specs=[row(d), row(d), whole((1, d))]
        + [row(width)] * 3
        + [whole((d, width))] * 3
        + [row(width)] * 3
        + [whole((d, 3 * width))],
        out_specs=[row(d), whole_out((8, d))],
        out_shape=[struct((rows, d), BF), struct((8, d), F32)],
        compiler_params=params(),
        cost_estimate=cost(rows * d * width * 6, 14e6),
        name="input_grad",
    )(x, gm, gain, *own, wq, wk, wv, *other, wx)


def add(a, b):
    return (a.astype(F32) + b.astype(F32)).astype(a.dtype)


class Links:
    def __init__(self, dp_size):
        self.size = dp_size
        self.bits = dp_size.bit_length() - 1
        self.index = lax.axis_index("dp")

    def bit(self, at):
        return (self.index >> at) & 1

    def swap(self, value, at):
        return lax.ppermute(value, "dp", [(i, i ^ (1 << at)) for i in range(self.size)])

    def across(self, value):
        return lax.ppermute(value, "tensor", [(0, 1), (1, 0)])

    def scatter(self, value, at):
        half = value.shape[0] // 2
        mine = self.bit(at)
        send = lax.dynamic_slice_in_dim(value, (1 - mine) * half, half, 0)
        keep = lax.dynamic_slice_in_dim(value, mine * half, half, 0)
        return add(keep, self.swap(send, at))

    def gather(self, value, at):
        other = self.swap(value, at)
        lower = self.bit(at) == 0
        return jnp.concatenate([jnp.where(lower, value, other), jnp.where(lower, other, value)], 0)

    def reduce(self, own_send, own_keep, other_send, other_keep):
        other = add(other_keep, self.swap(other_send, 0))
        own = add(own_keep, self.swap(own_send, 0))
        value = add(own, self.across(other))
        for at in range(1, self.bits):
            value = self.scatter(value, at)
        for at in reversed(range(1, self.bits)):
            value = self.gather(value, at)
        return value, self.swap(value, 0)

    def total(self, value):
        value = value + self.across(value)
        for at in range(self.bits):
            value = value + self.swap(value, at)
        return value


def layer(
    dp_size, inputs, lengths, norm1_gain, norm1_shift, query_weight, query_bias, key_weight, key_bias, value_weight,
    value_bias, out_weight, out_bias, norm2_gain, norm2_shift, up_weight, up_bias, down_weight, down_bias, out_grad,
):
    rows, d = inputs.shape
    width = query_weight.shape[1]
    ff = up_weight.shape[1]
    links = Links(dp_size)
    tensor = lax.axis_index("tensor")
    c = links.bit(0)
    core = c.reshape(1).astype(jnp.int32)
    length = lax.dynamic_slice_in_dim(lengths, tensor, 1, 0)
    cos, sin = (jnp.asarray(t) for t in rotary_tables(rows))
    row = lambda v: v.reshape(1, -1)

    biases = jnp.concatenate([query_bias, key_bias, value_bias, up_bias])
    biases_x = links.across(biases)
    cut = lambda w, axis: lax.dynamic_slice_in_dim(w, c * (w.shape[axis] // 2), w.shape[axis] // 2, axis)
    qkv_part = links.across(jnp.concatenate([cut(w, 0) for w in (query_weight, key_weight, value_weight)], 1))
    out_part = links.across(cut(out_weight, 0))
    up_part = links.across(cut(up_weight, 1))
    down_part = links.across(cut(down_weight, 0))

    def ordered(part, axis):
        other = links.swap(part, 0)
        lower = c == 0
        return jnp.concatenate([jnp.where(lower, part, other), jnp.where(lower, other, part)], axis)

    normed, normed_t, *own = project_own(
        inputs, row(norm1_gain), row(norm1_shift), query_weight, key_weight, value_weight,
        row(biases[: 3 * width]), cos, sin,
    )
    ctx_own, aug_own = attend(length, *own)
    qkv_x = ordered(qkv_part, 0)
    other = project_other(normed, qkv_x, row(biases_x[: 3 * width]), cos, sin)
    ctx_x, aug_x = attend(length, *other)
    out_x = ordered(out_part, 0)
    mid, n2, n2t, out, dn, dd_s, du_s, dd_k, du_k, dbu = ffn_own(
        core, inputs, ctx_own, ctx_x, out_weight, out_x, row(out_bias), row(norm2_gain), row(norm2_shift), out_grad,
        up_weight, down_weight, row(up_bias),
    )
    up_far = links.swap(up_part, 0)
    down_far = links.swap(down_part, 0)
    layer_out, gm, g_own, g_x, dwo, dwo_x, sums2, ddx_s, dux_s, ddx_k, dux_k, dbu_x = ffn_other(
        core, length, mid, n2, n2t, out, dn, out_grad, up_far, down_far, up_part, down_part,
        row(biases_x[3 * width :]), ctx_own, ctx_x, out_weight, out_x, row(norm2_gain), row(down_bias),
    )
    grad_down = links.reduce(dd_s, dd_k, ddx_s, ddx_k)
    grad_up = links.reduce(du_s, du_k, dux_s, dux_k)
    flip = lambda w, part: lax.dynamic_slice_in_dim(w, part * (w.shape[0] // 2), w.shape[0] // 2, 0)
    grad_out = links.reduce(flip(dwo, 1 - c), flip(dwo, c), flip(dwo_x, 1 - c), flip(dwo_x, c))

    *gx, sums_x = attend_back(length, *other, g_x, ctx_x, aug_x, cos, sin)
    qx_s, qx_k = project_grad(core, normed_t, *gx)
    *go, sums_o = attend_back(length, *own, g_own, ctx_own, aug_own, cos, sin)
    qo_s, qo_k = project_grad(core, normed_t, *go)
    grad_qkv = links.reduce(qo_s, qo_k, qx_s, qx_k)
    input_grad_out, sums1 = input_grad(
        inputs, gm, row(norm1_gain), go, query_weight, key_weight, value_weight, gx, qkv_x
    )

    halves = lambda a, b: [jnp.where(tensor == 0, a, b), jnp.where(tensor == 0, b, a)]
    small = jnp.concatenate(
        [sums1[0], sums1[1], sums2[2], sums2[0], sums2[1], sums2[3]]
        + halves(jnp.concatenate([sums_o[:3].reshape(-1), dbu[0]]), jnp.concatenate([sums_x[:3].reshape(-1), dbu_x[0]]))
    )
    small = links.total(small.reshape(-1, 128)).reshape(-1)
    vec = [small[i * d : (i + 1) * d] for i in range(6)]
    side = 3 * width + ff
    mine = lax.dynamic_slice_in_dim(small, 6 * d + tensor * side, side, 0)

    def final(pair, axis):
        lower = c == 0
        a, b = pair
        return jnp.concatenate([jnp.where(lower, a, b), jnp.where(lower, b, a)], axis).astype(F32)

    qkv = final(grad_qkv, 0)
    return (
        layer_out,
        input_grad_out,
        vec[0],
        vec[1],
        qkv[:, :width],
        mine[:width],
        qkv[:, width : 2 * width],
        mine[width : 2 * width],
        qkv[:, 2 * width :],
        mine[2 * width : 3 * width],
        final(grad_out, 0),
        vec[2],
        vec[3],
        vec[4],
        final(grad_up, 1),
        mine[3 * width :],
        final(grad_down, 0),
        vec[5],
    )


def solution(mesh):
    rows = P(("dp", "tensor"), None)
    cols = P(None, "tensor")
    tens = P("tensor")
    return jax.shard_map(
        lambda *args: layer(mesh.shape["dp"], *args),
        mesh=mesh,
        in_specs=(
            rows, P("dp"), P(), P(), cols, tens, cols, tens, cols, tens, P("tensor", None), P(), P(), P(), cols, tens,
            P("tensor", None), P(), rows,
        ),
        out_specs=(
            rows, rows, P(), P(), cols, tens, cols, tens, cols, tens, P("tensor", None), P(), P(), P(), cols, tens,
            P("tensor", None), P(),
        ),
        check_vma=False,
    )
```

time: 1180 us -> 463 us (0.39)
  matrix products: 294 us -> 0 us
  waiting for transfers between devices: 431 us -> 172 us
  Pallas kernels: 0 us -> 189 us
  local copies, waits for them, and re-layouts: 194 us -> 23.1 us
  other arithmetic: 131 us -> 19 us
  blocking collectives: 103 us -> 0 us
  starting transfers between devices: 0.83 us -> 48.9 us
  between operations: 14.9 us -> 2.1 us
    dot_general x32 -> x0, matrix products: 294 us -> none  [the longest x1 34.2 us: shards(): jnp.dot(normed2_all, up_weight, preferred_element_type=jnp.float32)]
    pallas_call x0 -> x11, Pallas kernels: none -> 189 us  [the longest x2 52.9 us: attend_back(): pl.pallas_call(lambda *refs: attend_back_kernel(256, *refs), grid_spec=pl...]
    ppermute x0 -> x54, waiting for transfers between devices: none -> 172 us  [the longest x44 86.4 us: swap(): lax.ppermute(value, 'dp', [(i, i ^ 1 << at) for i in range(self.size)])]
    psum x1 -> x0, waiting for transfers between devices: 168 us -> none  [shards(): lax.psum((grad_query_weight, grad_query_bias, grad_key_weight, grad_key_b...]
    all_gather x4 -> x0, waiting for transfers between devices: 149 us -> none  [the longest x1 47.1 us: shards(): normed_all = lax.all_gather(normed_low, 'tensor', axis=0, tiled=True)]
    dynamic_update_slice x8 -> x0, local copies, waits for them, and re-layouts: 122 us -> none  [shards(): lax.map(lambda bundle: attention_pass(attend_backward, bundle[5], bundle[...]
    reduce_scatter x4 -> x0, waiting for transfers between devices: 114 us -> none  [the longest x1 43.4 us: shards(): lax.psum_scatter(jnp.dot(block_rows, out_weight, preferred_element_type=j...]
    psum x2 -> x0, blocking collectives: 103 us -> none  [the longest x1 63.8 us: shards(): lax.psum((grad_query_weight, grad_query_bias, grad_key_weight, grad_key_b...]
  transfers between devices with their start and end apart: 9 -> 54, of which waited for: 8 -> 22; matrix products, arithmetic and copies ran while one was open for 8% -> 8% of each run, Pallas kernels for 0% -> 33%
where the time goes in v1:
time: 463 us; the launch traced here: 454 us
  Pallas kernels  189 us (41%)
  waiting for transfers between devices  172 us (37%)
  starting transfers between devices  48.9 us (11%)
  local copies, waits for them, and re-layouts  23.1 us (5%)
  other arithmetic  19 us (4%)
    ppermute x44, waiting for transfers between devices, swap(): lax.ppermute(value, 'dp', [(i, i ^ 1 << at) for i in range(self.size)])  86.4 us
    ppermute x10, waiting for transfers between devices, across(): return lax.ppermute(value, 'tensor', [(0, 1), (1, 0)])  85.6 us
    pallas_call x2, Pallas kernels, attend_back(): pl.pallas_call(lambda *refs: attend_back_kernel(256, *refs), grid_spec=pl...  52.9 us
    pallas_call x1, Pallas kernels, ffn_other(): pl.pallas_call(lambda *refs: ffn_other_kernel(per, *refs), grid_spec=pltp...  40.7 us
    pallas_call x1, Pallas kernels, ffn_own(): pl.pallas_call(lambda *refs: ffn_own_kernel(per, *refs), grid_spec=pltpu....  36.1 us
    ppermute x44, starting transfers between devices, swap(): lax.ppermute(value, 'dp', [(i, i ^ 1 << at) for i in range(self.size)])  34.8 us
    pallas_call x2, Pallas kernels, attend(): pl.pallas_call(lambda *refs: attend_kernel(256, *refs), grid_spec=pltpu.P...  23.4 us
    ppermute x10, starting transfers between devices, across(): return lax.ppermute(value, 'tensor', [(0, 1), (1, 0)])  14.1 us
  transfers between devices with their start and end apart: 54, of which 22 were waited for; matrix products, arithmetic and copies ran while one was open for 8% of the time, Pallas kernels for 33%

profile of v1, /device:TPU:0, one launch (start us, length us, event | category | flops | bytes accessed | tf_op | source)
XLA Modules:
  0.0 454.0 jit_solution(18104026765729283022)
XLA Ops:
  16.9 6.9 %project_own.1 = (bf16[1024,768]{1,0:T(8,128)(2,1)}, bf16[768,1024]{1,0:T(8,128)(2,1)}, bf16[1024,384]{1,0:T(8,128)(2,1)}, bf16[1024,384]{1,0:T(8,128)(2,1)}, bf16[1024,384]{1,0:T(8,128)(2,1)}) custom-call(bf16[1024,768]{1,0:T(8,128)(2,1)} %x_ref.3, f32[1,768]{1,0:T(1,128)} %reshape.90.gain_ref, f32[1,768]{1,0:T(1,128)} %reshape.91.shift_ref, ...), custom_call_target="tpu_custom_call" | custom-call | flops 1811939328 | bytes 12000000 | tf_op jit(solution)/shard_map/project_own/pallas_call | solution.py:119
  23.8 9.3 %collective-permute-done.3 = bf16[192,768]{1,0:T(8,128)(2,1)} collective-permute-done((bf16[192,768]{1,0:T(8,128)(2,1)S(1)}, bf16[192,768]{1,0:T(8,128)(2,1)}, u32[]{:S(2)}, u32[]{:S(2)}) %collective-permute-start.3) | collective-permute-done | bytes 294944 | tf_op jit(solution)/shard_map/ppermute | solution.py:593
  33.6 11.7 %attend.2 = (bf16[1024,384]{1,0:T(8,128)(2,1)}, bf16[1024,384]{1,0:T(8,128)(2,1)}) custom-call(s32[1]{0:T(128)} %dynamic_slice.108.refs_0_.refs_1_, bf16[1024,384]{1,0:T(8,128)(2,1)} %get-tuple-element.66.refs_1_, bf16[1024,384]{1,0:T(8,128)(2,1)} %get-tuple-element.67.refs_2_, bf16[1024,384]{1,0:T(8,128)(2,1)} %get-tuple-element.68.refs_3_), custom_call_target="tpu_custom_call" | custom-call | flops 6442450944 | bytes 3932160 | tf_op jit(solution)/shard_map/attend/pallas_call | solution.py:199
  58.4 24.4 %collective-permute-done.7.refs_11_ = bf16[768,768]{1,0:T(8,128)(2,1)} collective-permute-done((bf16[768,768]{1,0:T(8,128)(2,1)S(1)}, bf16[768,768]{1,0:T(8,128)(2,1)}, u32[]{:S(2)}, u32[]{:S(2)}) %collective-permute-start.7) | collective-permute-done | bytes 1179680 | tf_op jit(solution)/shard_map/ppermute | solution.py:593
  85.6 6.2 %project_other.1 = (bf16[1024,384]{1,0:T(8,128)(2,1)}, bf16[1024,384]{1,0:T(8,128)(2,1)}, bf16[1024,384]{1,0:T(8,128)(2,1)}) custom-call(bf16[1024,768]{1,0:T(8,128)(2,1)} %get-tuple-element.70.n_ref, bf16[768,1152]{1,0:T(8,128)(2,1)} %pad_maximum_fusion.w_ref.wx_ref, f32[1,1152]{1,0:T(1,128)} %reshape.93.b_ref, f32[1024,128]{1,0:T(8,128)} %constant.41.clone.cos_ref.refs_7_, ...), custom_call_target="tpu_custom_call" | custom-call | flops 1811939328 | bytes 8000000 | tf_op jit(solution)/shard_map/project_other/pallas_call | solution.py:138
  91.8 11.7 %attend.3 = (bf16[1024,384]{1,0:T(8,128)(2,1)}, bf16[1024,384]{1,0:T(8,128)(2,1)}) custom-call(s32[1]{0:T(128)} %dynamic_slice.108.refs_0_.refs_1_, bf16[1024,384]{1,0:T(8,128)(2,1)} %get-tuple-element.71.refs_1_, bf16[1024,384]{1,0:T(8,128)(2,1)} %get-tuple-element.72.refs_2_, bf16[1024,384]{1,0:T(8,128)(2,1)} %get-tuple-element.73.refs_3_), custom_call_target="tpu_custom_call" | custom-call | flops 6442450944 | bytes 3932160 | tf_op jit(solution)/shard_map/attend/pallas_call | solution.py:199
  103.5 36.1 %ffn_own.1 = (f32[1024,768]{1,0:T(8,128)}, bf16[1024,768]{1,0:T(8,128)(2,1)}, bf16[768,1024]{1,0:T(8,128)(2,1)}, f32[1024,768]{1,0:T(8,128)}, f32[1024,768]{1,0:...) custom-call(s32[1]{0:T(128)} %bitcast.refs_0_.c_ref, ...), custom_call_target="tpu_custom_call" | custom-call | flops 15703474176 | bytes 40000000 | tf_op jit(solution)/shard_map/ffn_own/pallas_call | solution.py:376
  141.4 40.7 %ffn_other.1 = (bf16[1024,768]{1,0:T(8,128)(2,1)}, f32[1024,768]{1,0:T(8,128)}, bf16[1024,384]{1,0:T(8,128)(2,1)}, bf16[1024,384]{1,0:T(8,128)(2,1)}, bf16[384,7...) custom-call(s32[1]{0:T(128)} %bitcast.refs_0_.c_ref, ...), custom_call_target="tpu_custom_call" | custom-call | flops 16911433728 | bytes 50000000 | tf_op jit(solution)/shard_map/ffn_other/pallas_call | solution.py:471
  184.8 31.2 %attend_back.2 = (bf16[1024,384]{1,0:T(8,128)(2,1)}, bf16[1024,384]{1,0:T(8,128)(2,1)}, bf16[1024,384]{1,0:T(8,128)(2,1)}, f32[8,384]{1,0:T(8,128)}) custom-call(s32[1]{0:T(128)} %dynamic_slice.108.refs_0_.refs_1_, bf16[1024,384]{1,0:T(8,128)(2,1)} %get-tuple-element.66.refs_1_, bf16[1024,384]{1,0:T(8,128)(2,1)} %get-tuple-element.67.refs_2_, ...), custom_call_target="tpu_custom_call" | custom-call | flops 16106127360 | bytes 7077888 | tf_op jit(solution)/shard_map/attend_back/pallas_call | solution.py:266
  216.0 21.6 %attend_back.3 = (bf16[1024,384]{1,0:T(8,128)(2,1)}, bf16[1024,384]{1,0:T(8,128)(2,1)}, bf16[1024,384]{1,0:T(8,128)(2,1)}, f32[8,384]{1,0:T(8,128)}) custom-call(s32[1]{0:T(128)} %dynamic_slice.108.refs_0_.refs_1_, bf16[1024,384]{1,0:T(8,128)(2,1)} %get-tuple-element.71.refs_1_, bf16[1024,384]{1,0:T(8,128)(2,1)} %get-tuple-element.72.refs_2_, ...), custom_call_target="tpu_custom_call" | custom-call | flops 16106127360 | bytes 7077888 | tf_op jit(solution)/shard_map/attend_back/pallas_call | solution.py:266
  237.7 11.3 %input_grad.1 = (bf16[1024,768]{1,0:T(8,128)(2,1)}, f32[8,768]{1,0:T(8,128)}) custom-call(bf16[1024,768]{1,0:T(8,128)(2,1)} %x_ref.3, f32[1024,768]{1,0:T(8,128)} %get-tuple-element.81.gm_ref, f32[1,768]{1,0:T(1,128)} %reshape.90.gain_ref, bf16[1024,384]{1,0:T(8,128)(2,1)} %get-tuple-element.84.q0.dq_ref, bf16[1024,384]{1,0:T(8,128)(2,1)} %get-tuple-element.85.k0.dk_ref, ...), custom_call_target="tpu_custom_call" | custom-call | flops 3623878656 | bytes 14000000 | tf_op jit(solution)/shard_map/input_grad/pallas_call | solution.py:560
  252.4 8.2 %collective-permute-done.9 = f32[78,128]{1,0:T(8,128)S(1)} collective-permute-done((f32[78,128]{1,0:T(8,128)S(1)}, f32[78,128]{1,0:T(8,128)S(1)}, u32[]{:S(2)}, u32[]{:S(2)}) %collective-permute-start.9) | collective-permute-done | bytes 39968 | tf_op jit(solution)/shard_map/ppermute | solution.py:593
  269.5 5.7 %project_grad.3 = (bf16[384,1152]{1,0:T(8,128)(2,1)}, bf16[384,1152]{1,0:T(8,128)(2,1)}) custom-call(s32[1]{0:T(128)} %bitcast.refs_0_.c_ref, bf16[768,1024]{1,0:T(8,128)(2,1)} %get-tuple-element.99.nt_ref, bf16[1024,384]{1,0:T(8,128)(2,1)} %get-tuple-element.89.q1.dq_ref, bf16[1024,384]{1,0:T(8,128)(2,1)} %get-tuple-element.90.k1.dk_ref, ...), custom_call_target="tpu_custom_call" | custom-call | flops 1811939328 | bytes 6000000 | tf_op jit(solution)/shard_map/project_grad/pallas_call | solution.py:521
  300.1 13.1 %collective-permute-done.16 = bf16[384,1152]{1,0:T(8,128)(2,1)S(1)} collective-permute-done((bf16[384,1152]{1,0:T(8,128)(2,1)S(1)}, bf16[384,1152]{1,0:T(8,128)(2,1)S(1)}, u32[]{:S(2)}, u32[]{:S(2)}) %collective-permute-start.16) | collective-permute-done | bytes 884768 | tf_op jit(solution)/shard_map/ppermute | solution.py:593
  317.4 8.8 %collective-permute-done.17 = bf16[192,1152]{1,0:T(8,128)(2,1)S(1)} collective-permute-done((bf16[192,1152]{1,0:T(8,128)(2,1)S(1)}, bf16[192,1152]{1,0:T(8,128)(2,1)S(1)}, u32[]{:S(2)}, u32[]{:S(2)}) %collective-permute-start.17) | collective-permute-done | bytes 442400 | tf_op jit(solution)/shard_map/ppermute | solution.py:590
  328.4 6.3 %collective-permute-done.18 = bf16[96,1152]{1,0:T(8,128)(2,1)S(1)} collective-permute-done((bf16[96,1152]{1,0:T(8,128)(2,1)S(1)}, bf16[96,1152]{1,0:T(8,128)(2,1)S(1)}, u32[]{:S(2)}, u32[]{:S(2)}) %collective-permute-start.18) | collective-permute-done | bytes 221216 | tf_op jit(solution)/shard_map/ppermute | solution.py:590
  335.2 9.1 %collective-permute-done.46 = bf16[768,768]{1,0:T(8,128)(2,1)S(1)} collective-permute-done((bf16[768,768]{1,0:T(8,128)(2,1)S(1)}, bf16[768,768]{1,0:T(8,128)(2,1)S(1)}, u32[]{:S(2)}, u32[]{:S(2)}) %collective-permute-start.46) | collective-permute-done | bytes 1179680 | tf_op jit(solution)/shard_map/ppermute | solution.py:593
  351.8 17.1 %collective-permute-done.36 = bf16[768,768]{1,0:T(8,128)(2,1)S(1)} collective-permute-done((bf16[768,768]{1,0:T(8,128)(2,1)S(1)}, bf16[768,768]{1,0:T(8,128)(2,1)S(1)}, u32[]{:S(2)}, u32[]{:S(2)}) %collective-permute-start.36) | collective-permute-done | bytes 1179680 | tf_op jit(solution)/shard_map/ppermute | solution.py:593
  372.4 13.5 %collective-permute-done.37 = bf16[384,768]{1,0:T(8,128)(2,1)S(1)} collective-permute-done((bf16[384,768]{1,0:T(8,128)(2,1)S(1)}, bf16[384,768]{1,0:T(8,128)(2,1)S(1)}, u32[]{:S(2)}, u32[]{:S(2)}) %collective-permute-start.37) | collective-permute-done | bytes 589856 | tf_op jit(solution)/shard_map/ppermute | solution.py:590
  388.2 6.8 %collective-permute-done.38 = bf16[192,768]{1,0:T(8,128)(2,1)S(1)} collective-permute-done((bf16[192,768]{1,0:T(8,128)(2,1)S(1)}, bf16[192,768]{1,0:T(8,128)(2,1)S(1)}, u32[]{:S(2)}, u32[]{:S(2)}) %collective-permute-start.38) | collective-permute-done | bytes 294944 | tf_op jit(solution)/shard_map/ppermute | solution.py:590
  398.4 6.7 %collective-permute-done.39 = bf16[96,768]{1,0:T(8,128)(2,1)S(1)} collective-permute-done((bf16[96,768]{1,0:T(8,128)(2,1)S(1)}, bf16[96,768]{1,0:T(8,128)(2,1)S(1)}, u32[]{:S(2)}, u32[]{:S(2)}) %collective-permute-start.39) | collective-permute-done | bytes 147488 | tf_op jit(solution)/shard_map/ppermute | solution.py:590
  413.9 7.1 %collective-permute-done.51 = bf16[192,768]{1,0:T(8,128)(2,1)S(1)} collective-permute-done((bf16[192,768]{1,0:T(8,128)(2,1)S(1)}, bf16[192,768]{1,0:T(8,128)(2,1)S(1)}, u32[]{:S(2)}, u32[]{:S(2)}) %collective-permute-start.51) | collective-permute-done | bytes 294944 | tf_op jit(solution)/shard_map/ppermute | solution.py:590
  427.7 8.7 %collective-permute-done.52 = bf16[384,768]{1,0:T(8,128)(2,1)S(1)} collective-permute-done((bf16[384,768]{1,0:T(8,128)(2,1)S(1)}, bf16[384,768]{1,0:T(8,128)(2,1)S(1)}, u32[]{:S(2)}, u32[]{:S(2)}) %collective-permute-start.52) | collective-permute-done | bytes 589856 | tf_op jit(solution)/shard_map/ppermute | solution.py:590
  437.5 7.3 %collective-permute-done.42 = bf16[384,768]{1,0:T(8,128)(2,1)S(1)} collective-permute-done((bf16[384,768]{1,0:T(8,128)(2,1)S(1)}, bf16[384,768]{1,0:T(8,128)(2,1)S(1)}, u32[]{:S(2)}, u32[]{:S(2)}) %collective-permute-start.42) | collective-permute-done | bytes 589856 | tf_op jit(solution)/shard_map/ppermute | solution.py:590
  (268 shorter events, 122.1 us)
Async XLA Ops:
  2.9 30.2 %collective-permute-start = (bf16[384,1152]{1,0:T(8,128)(2,1)S(1)}, bf16[384,1152]{1,0:T(8,128)(2,1)}, u32[]{:S(2)}, u32[]{:S(2)}) collective-permute-start(bf16[384,1152]{1,0:T(8,128)(2,1)S(1)} %pad_maximum_fusion.3), channel_id=1, source_target_pairs={{0,1},{1,0},{2,3},{3,2},{4,5},{5,4},{6,7},{7,6},{8,9},{9,8},{10,11... | collective-permute-start | bytes 2654216 | tf_op jit(solution)/shard_map/ppermute | solution.py:593
  6.6 43.1 %collective-permute-start.2 = (f32[2688]{0:T(1024)}, f32[2688]{0:T(1024)}, u32[]{:S(2)}, u32[]{:S(2)}) collective-permute-start(f32[2688]{0:T(1024)} %pad_maximum_fusion.15), channel_id=1, source_target_pairs={{0,1},{1,0},{2,3},{3,2},{4,5},{5,4},{6,7},{7,6},{8,9},{9,8},{10,11... | collective-permute-start | bytes 32264 | tf_op jit(solution)/shard_map/ppermute | solution.py:593
  7.1 26.0 %collective-permute-start.3 = (bf16[192,768]{1,0:T(8,128)(2,1)S(1)}, bf16[192,768]{1,0:T(8,128)(2,1)}, u32[]{:S(2)}, u32[]{:S(2)}) collective-permute-start(bf16[192,768]{1,0:T(8,128)(2,1)S(1)} %constant_dynamic-slice_fusion.16), channel_id=1, source_target_pairs={{0,1},{1,0},{2,3},{3,2},{4,5},{5,4},{6,7},{7,6},{8,9},{9,8},{10,11... | collective-permute-start | bytes 884744 | tf_op jit(solution)/shard_map/ppermute | solution.py:593
  10.2 48.2 %collective-permute-start.5 = (bf16[768,768]{1,0:T(8,128)(2,1)S(1)}, bf16[768,768]{1,0:T(8,128)(2,1)}, u32[]{:S(2)}, u32[]{:S(2)}) collective-permute-start(bf16[768,768]{1,0:T(8,128)(2,1)S(1)} %constant_dynamic-slice_fusion.15), channel_id=1, source_target_pairs={{0,1},{1,0},{2,3},{3,2},{4,5},{5,4},{6,7},{7,6},{8,9},{9,8},{10,11... | collective-permute-start | bytes 3538952 | tf_op jit(solution)/shard_map/ppermute | solution.py:593
  10.9 71.9 %collective-permute-start.7 = (bf16[768,768]{1,0:T(8,128)(2,1)S(1)}, bf16[768,768]{1,0:T(8,128)(2,1)}, u32[]{:S(2)}, u32[]{:S(2)}) collective-permute-start(bf16[768,768]{1,0:T(8,128)(2,1)S(1)} %constant_dynamic-slice_fusion.14), channel_id=1, source_target_pairs={{0,1},{1,0},{2,3},{3,2},{4,5},{5,4},{6,7},{7,6},{8,9},{9,8},{10,11... | collective-permute-start | bytes 3538952 | tf_op jit(solution)/shard_map/ppermute | solution.py:593
  33.1 19.1 %collective-permute-start.4 = (bf16[192,768]{1,0:T(8,128)(2,1)}, bf16[192,768]{1,0:T(8,128)(2,1)S(1)}, u32[]{:S(2)}, u32[]{:S(2)}) collective-permute-start(bf16[192,768]{1,0:T(8,128)(2,1)} %collective-permute-done.3), channel_id=1, source_target_pairs={{0,2},{2,0},{4,6},{6,4},{8,10},{10,8},{12,14},{14,12},{16,18},{18,... | collective-permute-start | bytes 884744 | tf_op jit(solution)/shard_map/ppermute | solution.py:590
  33.1 49.7 %collective-permute-start.1 = (bf16[384,1152]{1,0:T(8,128)(2,1)}, bf16[384,1152]{1,0:T(8,128)(2,1)S(1)}, u32[]{:S(2)}, u32[]{:S(2)}) collective-permute-start(bf16[384,1152]{1,0:T(8,128)(2,1)} %collective-permute-done), channel_id=1, source_target_pairs={{0,2},{2,0},{4,6},{6,4},{8,10},{10,8},{12,14},{14,12},{16,18},{18,... | collective-permute-start | bytes 2654216 | tf_op jit(solution)/shard_map/ppermute | solution.py:590
  58.4 82.0 %collective-permute-start.6 = (bf16[768,768]{1,0:T(8,128)(2,1)}, bf16[768,768]{1,0:T(8,128)(2,1)}, u32[]{:S(2)}, u32[]{:S(2)}) collective-permute-start(bf16[768,768]{1,0:T(8,128)(2,1)} %collective-permute-done.5.refs_10_), channel_id=1, source_target_pairs={{0,2},{2,0},{4,6},{6,4},{8,10},{10,8},{12,14},{14,12},{16,18},{18,... | collective-permute-start | bytes 3538952 | tf_op jit(solution)/shard_map/ppermute | solution.py:590
  82.9 57.5 %collective-permute-start.8 = (bf16[768,768]{1,0:T(8,128)(2,1)}, bf16[768,768]{1,0:T(8,128)(2,1)S(1)}, u32[]{:S(2)}, u32[]{:S(2)}) collective-permute-start(bf16[768,768]{1,0:T(8,128)(2,1)} %collective-permute-done.7.refs_11_), channel_id=1, source_target_pairs={{0,2},{2,0},{4,6},{6,4},{8,10},{10,8},{12,14},{14,12},{16,18},{18,... | collective-permute-start | bytes 3538952 | tf_op jit(solution)/shard_map/ppermute | solution.py:590
  183.1 67.1 %collective-permute-start.25 = (bf16[192,768]{1,0:T(8,128)(2,1)S(1)}, bf16[192,768]{1,0:T(8,128)(2,1)S(1)}, u32[]{:S(2)}, u32[]{:S(2)}) collective-permute-start(bf16[192,768]{1,0:T(8,128)(2,1)S(1)} %constant_dynamic-slice_fusion.9), channel_id=1, source_target_pairs={{0,2},{2,0},{4,6},{6,4},{8,10},{10,8},{12,14},{14,12},{16,18},{18,... | collective-permute-start | bytes 884744 | tf_op jit(solution)/shard_map/ppermute | solution.py:590
  184.7 76.0 %collective-permute-start.24 = (bf16[192,768]{1,0:T(8,128)(2,1)S(1)}, bf16[192,768]{1,0:T(8,128)(2,1)S(1)}, u32[]{:S(2)}, u32[]{:S(2)}) collective-permute-start(bf16[192,768]{1,0:T(8,128)(2,1)S(1)} %constant_dynamic-slice_fusion.10), channel_id=1, source_target_pairs={{0,2},{2,0},{4,6},{6,4},{8,10},{10,8},{12,14},{14,12},{16,18},{18,... | collective-permute-start | bytes 884744 | tf_op jit(solution)/shard_map/ppermute | solution.py:590
  275.2 16.4 %collective-permute-start.15 = (bf16[384,1152]{1,0:T(8,128)(2,1)}, bf16[384,1152]{1,0:T(8,128)(2,1)S(1)}, u32[]{:S(2)}, u32[]{:S(2)}) collective-permute-start(bf16[384,1152]{1,0:T(8,128)(2,1)} %get-tuple-element.103), channel_id=1, source_target_pairs={{0,2},{2,0},{4,6},{6,4},{8,10},{10,8},{12,14},{14,12},{16,18},{18,... | collective-permute-start | bytes 2654216 | tf_op jit(solution)/shard_map/ppermute | solution.py:590
  278.4 56.8 %collective-permute-start.44 = (bf16[768,768]{1,0:T(8,128)(2,1)S(1)}, bf16[768,768]{1,0:T(8,128)(2,1)S(1)}, u32[]{:S(2)}, u32[]{:S(2)}) collective-permute-start(bf16[768,768]{1,0:T(8,128)(2,1)S(1)} %copy-done.25), channel_id=1, source_target_pairs={{0,2},{2,0},{4,6},{6,4},{8,10},{10,8},{12,14},{14,12},{16,18},{18,... | collective-permute-start | bytes 3538952 | tf_op jit(solution)/shard_map/ppermute | solution.py:590
  288.9 24.6 %collective-permute-start.45 = (bf16[768,768]{1,0:T(8,128)(2,1)}, bf16[768,768]{1,0:T(8,128)(2,1)S(1)}, u32[]{:S(2)}, u32[]{:S(2)}) collective-permute-start(bf16[768,768]{1,0:T(8,128)(2,1)} %get-tuple-element.113), channel_id=1, source_target_pairs={{0,2},{2,0},{4,6},{6,4},{8,10},{10,8},{12,14},{14,12},{16,18},{18,... | collective-permute-start | bytes 3538952 | tf_op jit(solution)/shard_map/ppermute | solution.py:590
  291.8 21.4 %collective-permute-start.16 = (bf16[384,1152]{1,0:T(8,128)(2,1)S(1)}, bf16[384,1152]{1,0:T(8,128)(2,1)S(1)}, u32[]{:S(2)}, u32[]{:S(2)}) collective-permute-start(bf16[384,1152]{1,0:T(8,128)(2,1)S(1)} %add_convert_fusion.7), channel_id=1, source_target_pairs={{0,1},{1,0},{2,3},{3,2},{4,5},{5,4},{6,7},{7,6},{8,9},{9,8},{10,11... | collective-permute-start | bytes 2654216 | tf_op jit(solution)/shard_map/ppermute | solution.py:593
  299.4 16.1 %collective-permute-start.35 = (bf16[768,768]{1,0:T(8,128)(2,1)S(1)}, bf16[768,768]{1,0:T(8,128)(2,1)S(1)}, u32[]{:S(2)}, u32[]{:S(2)}) collective-permute-start(bf16[768,768]{1,0:T(8,128)(2,1)S(1)} %copy-done.26), channel_id=1, source_target_pairs={{0,2},{2,0},{4,6},{6,4},{8,10},{10,8},{12,14},{14,12},{16,18},{18,... | collective-permute-start | bytes 3538952 | tf_op jit(solution)/shard_map/ppermute | solution.py:590
  299.5 52.3 %collective-permute-start.34 = (bf16[768,768]{1,0:T(8,128)(2,1)S(1)}, bf16[768,768]{1,0:T(8,128)(2,1)S(1)}, u32[]{:S(2)}, u32[]{:S(2)}) collective-permute-start(bf16[768,768]{1,0:T(8,128)(2,1)S(1)} %copy-done.24), channel_id=1, source_target_pairs={{0,2},{2,0},{4,6},{6,4},{8,10},{10,8},{12,14},{14,12},{16,18},{18,... | collective-permute-start | bytes 3538952 | tf_op jit(solution)/shard_map/ppermute | solution.py:590
  315.5 28.9 %collective-permute-start.46 = (bf16[768,768]{1,0:T(8,128)(2,1)S(1)}, bf16[768,768]{1,0:T(8,128)(2,1)S(1)}, u32[]{:S(2)}, u32[]{:S(2)}) collective-permute-start(bf16[768,768]{1,0:T(8,128)(2,1)S(1)} %add_convert_fusion.1), channel_id=1, source_target_pairs={{0,1},{1,0},{2,3},{3,2},{4,5},{5,4},{6,7},{7,6},{8,9},{9,8},{10,11... | collective-permute-start | bytes 3538952 | tf_op jit(solution)/shard_map/ppermute | solution.py:593
  326.2 42.7 %collective-permute-start.36 = (bf16[768,768]{1,0:T(8,128)(2,1)S(1)}, bf16[768,768]{1,0:T(8,128)(2,1)S(1)}, u32[]{:S(2)}, u32[]{:S(2)}) collective-permute-start(bf16[768,768]{1,0:T(8,128)(2,1)S(1)} %add_convert_fusion.4), channel_id=1, source_target_pairs={{0,1},{1,0},{2,3},{3,2},{4,5},{5,4},{6,7},{7,6},{8,9},{9,8},{10,11... | collective-permute-start | bytes 3538952 | tf_op jit(solution)/shard_map/ppermute | solution.py:593
  345.3 26.4 %collective-permute-start.47 = (bf16[384,768]{1,0:T(8,128)(2,1)S(1)}, bf16[384,768]{1,0:T(8,128)(2,1)S(1)}, u32[]{:S(2)}, u32[]{:S(2)}) collective-permute-start(bf16[384,768]{1,0:T(8,128)(2,1)S(1)} %constant_dynamic-slice_fusion.2), channel_id=1, source_target_pairs={{0,4},{2,6},{4,0},{6,2},{8,12},{10,14},{12,8},{14,10},{16,20},{18,... | collective-permute-start | bytes 1769480 | tf_op jit(solution)/shard_map/ppermute | solution.py:590
  351.7 18.9 %collective-permute-start.21 = (bf16[96,1152]{1,0:T(8,128)(2,1)S(1)}, bf16[96,1152]{1,0:T(8,128)(2,1)S(1)}, u32[]{:S(2)}, u32[]{:S(2)}) collective-permute-start(bf16[96,1152]{1,0:T(8,128)(2,1)S(1)} %pad_maximum_fusion.12), channel_id=1, source_target_pairs={{0,8},{2,10},{4,12},{6,14},{8,0},{10,2},{12,4},{14,6},{16,24},{18,... | collective-permute-start | bytes 663560 | tf_op jit(solution)/shard_map/ppermute | solution.py:590
  369.5 16.3 %collective-permute-start.37 = (bf16[384,768]{1,0:T(8,128)(2,1)S(1)}, bf16[384,768]{1,0:T(8,128)(2,1)S(1)}, u32[]{:S(2)}, u32[]{:S(2)}) collective-permute-start(bf16[384,768]{1,0:T(8,128)(2,1)S(1)} %constant_dynamic-slice_fusion.5), channel_id=1, source_target_pairs={{0,4},{2,6},{4,0},{6,2},{8,12},{10,14},{12,8},{14,10},{16,20},{18,... | collective-permute-start | bytes 1769480 | tf_op jit(solution)/shard_map/ppermute | solution.py:590
  370.8 24.5 %collective-permute-start.22 = (bf16[192,1152]{1,0:T(8,128)(2,1)S(1)}, bf16[192,1152]{1,0:T(8,128)(2,1)S(1)}, u32[]{:S(2)}, u32[]{:S(2)}) collective-permute-start(bf16[192,1152]{1,0:T(8,128)(2,1)S(1)} %pad_maximum_fusion.8), channel_id=1, source_target_pairs={{0,4},{2,6},{4,0},{6,2},{8,12},{10,14},{12,8},{14,10},{16,20},{18,... | collective-permute-start | bytes 1327112 | tf_op jit(solution)/shard_map/ppermute | solution.py:590
  425.3 19.5 %collective-permute-start.42 = (bf16[384,768]{1,0:T(8,128)(2,1)S(1)}, bf16[384,768]{1,0:T(8,128)(2,1)S(1)}, u32[]{:S(2)}, u32[]{:S(2)}) collective-permute-start(bf16[384,768]{1,0:T(8,128)(2,1)S(1)} %pad_maximum_fusion.6), channel_id=1, source_target_pairs={{0,4},{2,6},{4,0},{6,2},{8,12},{10,14},{12,8},{14,10},{16,20},{18,... | collective-permute-start | bytes 1769480 | tf_op jit(solution)/shard_map/ppermute | solution.py:590
  (58 other events, 516.7 us)

commit v2 on v1

v2 whole, which is shorter than its diff:
```python
import math

import jax
import jax.numpy as jnp
import numpy as np
from jax import lax
from jax.experimental import pallas as pl
from jax.experimental.pallas import tpu as pltpu
from jax.sharding import PartitionSpec as P

HEAD_DIM = 64
EPS = 1e-05
LOG2E = math.log2(math.e)
LN2 = math.log(2.0)
F32 = jnp.float32
BF = jnp.bfloat16
BIG = -1e30


def dot(a, b, ca=1, cb=0):
    return lax.dot_general(a, b, (((ca,), (cb,)), ((), ())), preferred_element_type=F32)


def cost(macs, nbytes, exps=0):
    return pl.CostEstimate(flops=int(2 * macs), bytes_accessed=int(nbytes), transcendentals=int(exps))


def busy(micros):
    return pl.CostEstimate(flops=int(micros * 1.1e9), bytes_accessed=1000, transcendentals=0)


EST = {
    "move": busy(0.01),
    "heads_own": busy(16),
    "heads_other": busy(100),
    "ffn_own": busy(0.01),
    "ffn_mine": busy(100),
    "ffn_far": busy(100),
    "share": busy(8),
    "input_grad": busy(8),
    "halve": busy(20),
}


def struct(shape, dtype):
    return jax.ShapeDtypeStruct(shape, dtype)


def whole(shape):
    return pl.BlockSpec(shape, lambda *_: (0,) * len(shape), pipeline_mode=pl.Buffered(1))


def whole_out(shape):
    return pl.BlockSpec(shape, lambda *_: (0,) * len(shape))


ANY = pl.BlockSpec(memory_space=pl.ANY)


def call(kernel, after, *, in_specs, out_specs, out_shape, estimate, name, grid=(1,), prefetch=0, scratch=(), alias=None, mib=28):
    after = tuple(after)
    n_in = prefetch + len(in_specs)

    def body(*refs):
        kernel(*refs[:n_in], *refs[n_in + len(after) :])

    run = pl.pallas_call(
        body,
        grid_spec=pltpu.PrefetchScalarGridSpec(
            num_scalar_prefetch=prefetch,
            grid=grid,
            in_specs=list(in_specs) + [ANY] * len(after),
            out_specs=out_specs,
            scratch_shapes=list(scratch),
        ),
        out_shape=out_shape,
        compiler_params=pltpu.CompilerParams(vmem_limit_bytes=mib << 20),
        input_output_aliases=alias or {},
        cost_estimate=estimate,
        name=name,
    )
    return lambda *args: run(*args, *after)


def norm_rows(v):
    mean = jnp.mean(v, axis=1, keepdims=True)
    cent = v - mean
    var = jnp.mean(cent * cent, axis=1, keepdims=True)
    r = lax.rsqrt(var + EPS)
    return cent * r, r


def norm_back(e, n, r):
    return r * (e - jnp.mean(e, axis=1, keepdims=True) - n * jnp.mean(e * n, axis=1, keepdims=True))


def rotary_tables(rows):
    half = HEAD_DIM // 2
    freq = (10000.0 ** (-2.0 * np.arange(half, dtype=np.float32) / HEAD_DIM)).astype(np.float32)
    ang = (np.arange(rows, dtype=np.float32)[:, None] * freq[None, :]).astype(np.float64)
    cos = np.cos(ang).astype(np.float32)
    sin = np.sin(ang).astype(np.float32)
    return np.concatenate([cos] * 4, 1), np.concatenate([-sin, sin] * 2, 1)


def swap_halves(v):
    lane = lax.broadcasted_iota(jnp.int32, v.shape, 1)
    return jnp.where((lane & 32) == 0, pltpu.roll(v, 96, 1), pltpu.roll(v, 32, 1))


def rotate(v, cos, sin):
    return v * cos + swap_halves(v) * sin


def rotate_back(v, cos, sin):
    return v * cos - swap_halves(v) * sin


class Row:
    def __init__(self, d, width, ff):
        at = 0
        for name, size in (
            ("gain1", d), ("shift1", d), ("out_bias", d), ("gain2", d), ("shift2", d), ("down_bias", d),
            ("qkv", 3 * width), ("up", ff),
        ):
            setattr(self, name, slice(at, at + size))
            at += size


def pull(src, dst, sem):
    copy = pltpu.make_async_copy(src, dst, sem)
    copy.start()
    return copy


def arrange(bits, arrays, shapes, moves, name, after=(), mib=28):
    def kernel(bits_ref, *refs):
        ins, outs, sem = refs[: len(arrays)], refs[len(arrays) : -1], refs[-1]
        copies = [pull(src, dst, sem.at[i]) for i, (src, dst) in enumerate(moves(bits_ref, ins, outs))]
        for copy in copies:
            copy.wait()

    return call(
        kernel,
        after,
        prefetch=1,
        in_specs=[ANY] * len(arrays),
        out_specs=[whole_out(shape) for shape in shapes],
        out_shape=[struct(shape, BF) for shape in shapes],
        scratch=[pltpu.SemaphoreType.DMA((8,))],
        estimate=EST["move"],
        name=name,
        mib=mib,
    )(bits, *arrays)


def block(bit, size):
    return pl.ds(pl.multiple_of(bit * size, size), size)


def fold(bits, parts, rows, outs, name, after=(), width=None):
    arrays = [p[0] for p in parts]
    width = width or arrays[0].shape[1]
    dtype = arrays[0].dtype
    half = rows // 2
    shapes = [(half, width)] * 2 if isinstance(outs, int) else [(n, width) for _, n in outs]

    def kernel(bits_ref, *refs):
        ins, outs_r, acc = refs[: len(parts)], refs[len(parts) : -1], refs[-1]
        seen = []
        for ref, (_, src, dst, n) in zip(ins, parts):
            value = ref[src : src + n, 0:width].astype(F32)
            fresh = not any(dst < b and a < dst + n for a, b in seen)
            acc[dst : dst + n, :] = value if fresh else acc[dst : dst + n, :] + value
            seen.append((dst, dst + n))
        if isinstance(outs, int):
            bit = bits_ref[outs]
            for ref, at in zip(outs_r, (1 - bit, bit)):
                ref[...] = acc[pl.ds(pl.multiple_of(at * half, 8 if half % 8 == 0 else 1), half), :].astype(dtype)
        else:
            for ref, (start, n) in zip(outs_r, outs):
                ref[...] = acc[start : start + n, :].astype(dtype)

    return call(
        kernel,
        after,
        prefetch=1,
        in_specs=[whole(a.shape) for a in arrays],
        out_specs=[whole_out(shape) for shape in shapes],
        out_shape=[struct(shape, dtype) for shape in shapes],
        scratch=[pltpu.VMEM((rows, width), F32)],
        estimate=EST["move"],
        name=name,
    )(bits, *arrays)


def put_qkv(pre, cos, sin, q_ref, k_ref, v_ref):
    width = q_ref.shape[1]
    for i in range(width // 128):
        sl = slice(i * 128, (i + 1) * 128)
        q_ref[:, sl] = (rotate(pre[0][:, sl], cos, sin) * (LOG2E / 8.0)).astype(BF)
        k_ref[:, sl] = rotate(pre[1][:, sl], cos, sin).astype(BF)
        v_ref[:, sl] = pre[2][:, sl].astype(BF)


def split3(v):
    hi = v.astype(BF)
    rest = v - hi.astype(F32)
    mid = rest.astype(BF)
    lo = rest - mid.astype(F32)
    return hi.astype(F32), mid.astype(F32), lo


def spread(lane, first, one, two):
    out = jnp.where(lane == 0, first, 0.0)
    for at, part in enumerate((*split3(one), *split3(two))):
        out = jnp.where(lane == at + 1, part, out)
    return out.astype(BF)


def attend_pair(length, q_ref, k_ref, v_ref, ctx_ref, aug_ref):
    bq = 256
    rows = q_ref.shape[0]
    lane1 = lax.broadcasted_iota(jnp.int32, (1, 128), 1)
    krow = lax.broadcasted_iota(jnp.int32, (rows, 128), 0)
    klane = lax.broadcasted_iota(jnp.int32, (rows, 128), 1)
    lane = lax.broadcasted_iota(jnp.int32, (bq, 128), 1)
    qrow = lax.broadcasted_iota(jnp.int32, (bq, 128), 0)
    kaug = jnp.where((klane == 0) & (krow >= length), BIG, 0.0).astype(BF)
    k = jnp.concatenate([k_ref[...], kaug], 1)
    v = jnp.concatenate([v_ref[...], jnp.ones((rows, 128), BF)], 1)
    qaug = jnp.where(lane == 0, 1.0, 0.0).astype(BF)
    for i in range(rows // bq):
        sl = slice(i * bq, (i + 1) * bq)
        q = q_ref[sl, :]
        outs, totals = [], []
        for h in range(2):
            keep = ((lane1 < 64) if h == 0 else (lane1 >= 64)).astype(BF)
            s = dot(jnp.concatenate([q * keep, qaug], 1), k, 1, 1)
            top = jnp.max(s, axis=1, keepdims=True)
            p = jnp.exp2(s - top).astype(BF)
            o = dot(p, v)
            total = o[:, 128:]
            outs.append(o[:, :128] / total)
            totals.append(top + jnp.log2(total))
        ctx = jnp.where(lane < 64, outs[0], outs[1])
        ctx_ref[sl, :] = jnp.where(qrow + i * bq < length, ctx, 0.0).astype(BF)
        aug_ref[sl, :] = spread(lane, 1.0, totals[0], totals[1])


def attend_all(length, q, k, v, ctx, aug):
    @pl.loop(0, q.shape[1] // 128)
    def _(p):
        sl = pl.ds(pl.multiple_of(p * 128, 128), 128)
        attend_pair(length, *(ref.at[:, sl] for ref in (q, k, v, ctx, aug)))


def heads_own_kernel(
    at, cut, bits_ref, len_ref, x_ref, vec_ref, wq_ref, wk_ref, wv_ref, cos_ref, sin_ref, wu_h, wd_h,
    n_h, nt_h, q_h, k_h, v_h, ctx_h, aug_h, near_h, rest_h,
    n_s, nt_s, q_s, k_s, v_s, ctx_s, aug_s, near_s, rest_s, sem,
):
    rows = x_ref.shape[0]
    width = q_s.shape[1]
    loads = [
        pull(src, dst, sem.at[i]) for i, (src, dst) in enumerate(cut(bits_ref, (wu_h, wd_h), (near_s, rest_s)))
    ]
    blk = 256
    bias = vec_ref[:, at.qkv]
    for i in range(rows // blk):
        sl = slice(i * blk, (i + 1) * blk)
        n, _ = norm_rows(x_ref[sl, :].astype(F32))
        low = (n * vec_ref[:, at.gain1] + vec_ref[:, at.shift1]).astype(BF)
        n_s[sl, :] = low
        nt_s[:, sl] = low.T
        pre = [
            dot(low, w[...]) + bias[:, j * width : (j + 1) * width] for j, w in enumerate((wq_ref, wk_ref, wv_ref))
        ]
        put_qkv(pre, cos_ref[sl, :], sin_ref[sl, :], *(ref.at[sl, :] for ref in (q_s, k_s, v_s)))
    for load in loads:
        load.wait()
    pairs = [
        (near_s, near_h), (rest_s, rest_h), (n_s, n_h), (nt_s, nt_h), (q_s, q_h), (k_s, k_h), (v_s, v_h)
    ]
    stores = [pull(src, dst, sem.at[8 + i]) for i, (src, dst) in enumerate(pairs)]
    attend_all(len_ref[0], q_s, k_s, v_s, ctx_s, aug_s)
    stores += [pull(ctx_s, ctx_h, sem.at[15]), pull(aug_s, aug_h, sem.at[16])]
    for store in stores:
        store.wait()


def heads_own(at, cut, shapes, bits, length, x, vec, wq, wk, wv, cos, sin, wu, wd, after=()):
    rows, d = x.shape
    width = wq.shape[1]
    outs = [(rows, d), (d, rows)] + [(rows, width)] * 5 + list(shapes)
    return call(
        lambda *refs: heads_own_kernel(at, cut, *refs),
        after,
        prefetch=2,
        in_specs=[whole(a.shape) for a in (x, vec, wq, wk, wv, cos, sin)] + [ANY] * 2,
        out_specs=[ANY] * len(outs),
        out_shape=[struct(shape, BF) for shape in outs],
        scratch=[pltpu.VMEM(shape, BF) for shape in outs] + [pltpu.SemaphoreType.DMA((17,))],
        estimate=EST["heads_own"],
        name="heads_own",
        mib=56,
    )(bits, length, x, vec, wq, wk, wv, cos, sin, wu, wd)


def heads_other_kernel(
    bits_ref, len_ref, n_ref, wm_ref, wf_ref, b_ref, cos_ref, sin_ref, q_h, k_h, v_h, ctx_h, aug_h,
    q_s, k_s, v_s, ctx_s, aug_s, sem,
):
    rows = n_ref.shape[0]
    width = q_s.shape[1]
    half = wm_ref.shape[0]
    c = bits_ref[0]
    blk = 256
    for i in range(rows // blk):
        sl = slice(i * blk, (i + 1) * blk)
        pre = dot(n_ref[sl, block(c, half)], wm_ref[...]) + dot(n_ref[sl, block(1 - c, half)], wf_ref[...])
        pre = pre + b_ref[:, : 3 * width]
        put_qkv(
            [pre[:, j * width : (j + 1) * width] for j in range(3)], cos_ref[sl, :], sin_ref[sl, :],
            *(ref.at[sl, :] for ref in (q_s, k_s, v_s)),
        )
    stores = [pull(src, dst, sem.at[i]) for i, (src, dst) in enumerate(((q_s, q_h), (k_s, k_h), (v_s, v_h)))]
    attend_all(len_ref[0], q_s, k_s, v_s, ctx_s, aug_s)
    stores += [pull(ctx_s, ctx_h, sem.at[3]), pull(aug_s, aug_h, sem.at[4])]
    for store in stores:
        store.wait()


def heads_other(bits, length, n, w_mine, w_far, bias, cos, sin, after=()):
    rows = n.shape[0]
    width = w_mine.shape[1] // 3
    outs = [(rows, width)] * 5
    return call(
        heads_other_kernel,
        after,
        prefetch=2,
        in_specs=[whole(a.shape) for a in (n, w_mine, w_far, bias, cos, sin)],
        out_specs=[ANY] * 5,
        out_shape=[struct(shape, BF) for shape in outs],
        scratch=[pltpu.VMEM(shape, BF) for shape in outs] + [pltpu.SemaphoreType.DMA((5,))],
        estimate=EST["heads_other"],
        name="heads_other",
        mib=56,
    )(bits, length, n, w_mine, w_far, bias, cos, sin)


def attend_back_kernel(
    bq, bits_ref, len_ref, q_ref, k_ref, v_ref, g_ref, ctx_ref, aug_ref, cos_ref, sin_ref, nt_ref, wo_ref,
    d_ref, sum_ref, send_ref, keep_ref, dqt, dall,
):
    rows = q_ref.shape[0]
    length = len_ref[0]
    lane1 = lax.broadcasted_iota(jnp.int32, (1, 128), 1)
    krow = lax.broadcasted_iota(jnp.int32, (rows, 128), 0)
    klane = lax.broadcasted_iota(jnp.int32, (rows, 128), 1)
    lane = lax.broadcasted_iota(jnp.int32, (bq, 128), 1)
    k = k_ref[...]
    v = v_ref[...]
    kt = k.T
    dks, dvs = [], []
    for h in range(2):
        keep = ((lane1 < 64) if h == 0 else (lane1 >= 64)).astype(BF)
        first = 1 + 3 * h
        mine = jnp.where((klane >= first) & (klane < first + 3), -1.0, 0.0)
        kaug = jnp.where((klane == 0) & (krow >= length), BIG, mine).astype(BF)
        kh = jnp.concatenate([k * keep, kaug], 1)
        vh = jnp.concatenate([v * keep, mine.astype(BF)], 1)
        dk = jnp.zeros((rows, 128), F32)
        dv = jnp.zeros((rows, 128), F32)
        for i in range(rows // bq):
            sl = slice(i * bq, (i + 1) * bq)
            q = q_ref[sl, :]
            g = g_ref[sl, :]
            prod = g.astype(F32) * ctx_ref[sl, :].astype(F32)
            d0 = jnp.sum(jnp.where(lane < 64, prod, 0.0), 1, keepdims=True)
            d1 = jnp.sum(jnp.where(lane < 64, 0.0, prod), 1, keepdims=True)
            gaug = spread(lane, 0.0, d0, d1)
            st = dot(kh, jnp.concatenate([q, aug_ref[sl, :]], 1), 1, 1)
            pt = jnp.exp2(st)
            dpt = dot(vh, jnp.concatenate([g, gaug], 1), 1, 1)
            ds = (pt * dpt).astype(BF)
            dv = dv + dot(pt.astype(BF), g)
            dk = dk + dot(ds, q)
            dqt[h * 64 : (h + 1) * 64, sl] = dot(kt[h * 64 : (h + 1) * 64, :], ds)
        dks.append(dk)
        dvs.append(dv)
    cos = cos_ref[...]
    sin = sin_ref[...]
    dq = rotate_back(dqt[...].T * (1.0 / 8.0), cos, sin).astype(BF)
    dk = rotate_back(jnp.where(klane < 64, dks[0], dks[1]) * LN2, cos, sin).astype(BF)
    dv = jnp.where(klane < 64, dvs[0], dvs[1]).astype(BF)
    for at, val in enumerate((dq, dk, dv)):
        sl = slice(at * 128, (at + 1) * 128)
        d_ref[:, sl] = val
        sum_ref[:, sl] = jnp.sum(val.astype(F32), axis=0, keepdims=True)
    j = pl.program_id(0)
    dall[:, block(j, 384)] = jnp.concatenate([dq, dk, dv], 1)

    @pl.when(j == pl.num_programs(0) - 1)
    def _():
        half = send_ref.shape[0]
        c = bits_ref[0]
        for ref, part in ((send_ref, 1 - c), (keep_ref, c)):
            width = dall.shape[1]
            ref[:, 0:width] = dot(nt_ref[block(part, half), :], dall[...]).astype(BF)
            ref[:, width:] = wo_ref[block(part, half), :]


def attend_back(bits, length, q, k, v, g, ctx, aug, cos, sin, nt, wo, after=(), est=100):
    rows, width = q.shape
    d = 2 * width
    bs = pl.BlockSpec((rows, 128), lambda j, *_: (0, j))
    return call(
        lambda *refs: attend_back_kernel(256, *refs),
        after,
        prefetch=2,
        grid=(width // 128,),
        in_specs=[bs] * 6 + [whole((rows, 128))] * 2 + [whole(nt.shape), whole(wo.shape)],
        out_specs=[pl.BlockSpec((rows, 384), lambda j, *_: (0, j)), pl.BlockSpec((1, 384), lambda j, *_: (0, j))]
        + [whole_out((d // 2, 4 * width))] * 2,
        out_shape=[struct((rows, 3 * width), BF), struct((1, 3 * width), F32)] + [struct((d // 2, 4 * width), BF)] * 2,
        scratch=[pltpu.VMEM((128, rows), F32), pltpu.VMEM((rows, 3 * width), BF)],
        estimate=busy(est),
        name="attend_back",
        mib=56,
    )(bits, length, q, k, v, g, ctx, aug, cos, sin, nt, wo)


def gelu_pair(h):
    z = jnp.abs(h) * (0.3275911 / math.sqrt(2.0)) + 1.0
    t = pl.reciprocal(z, approx=True)
    t = t * (2.0 - z * t)
    e = jnp.exp2(h * h * (-0.5 * LOG2E))
    poly = 0.5 * 1.061405429 * t - 0.5 * 1.453152027
    poly = poly * t + 0.5 * 1.421413741
    poly = poly * t - 0.5 * 0.284496736
    poly = poly * t + 0.5 * 0.254829592
    w = poly * t * e
    cdf = jnp.where(h >= 0.0, 1.0 - w, w)
    return h * cdf, cdf + h * e * (1.0 / math.sqrt(2.0 * math.pi))


def ffn_quarter(n2, n2t, og, wu, wd, bias, out_acc, dn_acc, act_s, dh_s, gd, gu, first, before=None, done=None):
    rows, d = og.shape
    part = wd.shape[0]
    blk = 256
    dbias = jnp.zeros((1, part), F32)
    if before is not None:
        before(0, blk)
    for i in range(rows // blk):
        sl = slice(i * blk, (i + 1) * blk)
        if before is not None and i + 1 < rows // blk:
            before(i + 1, blk)
        h = dot(n2[sl, :], wu[...]) + bias
        act, slope = gelu_pair(h)
        act = act.astype(BF)
        dh = (slope * dot(og[sl, :], wd[...], 1, 1)).astype(BF)
        act_s[sl, :] = act
        dh_s[sl, :] = dh
        dbias = dbias + jnp.sum(dh.astype(F32), axis=0, keepdims=True)
        o = dot(act, wd[...])
        e = dot(dh, wu[...], 1, 1)
        out_acc[sl, :] = o if first else out_acc[sl, :] + o
        dn_acc[sl, :] = e if first else dn_acc[sl, :] + e
        if done is not None and i > 0:
            done(i - 1, blk)
    if done is not None:
        done(rows // blk - 1, blk)
    gd[...] = dot(act_s[...], og[...], 0, 0).astype(BF)
    gu[...] = dot(n2t[...], dh_s[...]).astype(BF)
    return dbias


def ffn_own_kernel(
    at, bits_ref, x_ref, co_ref, cx_ref, woo_ref, wox, vec_ref, og_h, wu_h, wd_h,
    mid_h, n2_h, n2t_h, out_h, dn_h, send_h, keep_h, db_ref,
    og, wu, wd, mid, n2, n2t, out, dn, outb, dnb, act_s, dh_s, gd, gu, sem,
):
    rows, d = x_ref.shape
    part = wu_h.shape[1] // 2
    c = bits_ref[0]
    cols = [block(p, part) for p in (1 - c, c)]
    biases = [pl.ds(pl.multiple_of(at.up.start + p * part, 128), part) for p in (1 - c, c)]
    loads = [pull(og_h, og, sem.at[0])]
    for q in range(2):
        loads.append(pull(wu_h.at[:, cols[q]], wu.at[q], sem.at[1 + 2 * q]))
        loads.append(pull(wd_h.at[cols[q], :], wd.at[q], sem.at[2 + 2 * q]))
    stores = []

    def enter(i, blk):
        sl = slice(i * blk, (i + 1) * blk)
        att = dot(co_ref[sl, :], woo_ref[...]) + dot(cx_ref[sl, :], wox[...])
        v = x_ref[sl, :].astype(F32) + att + vec_ref[:, at.out_bias]
        mid[sl, :] = v
        n, _ = norm_rows(v)
        low = (n * vec_ref[:, at.gain2] + vec_ref[:, at.shift2]).astype(BF)
        n2[sl, :] = low
        n2t[:, sl] = low.T
        if i == 0:
            for load in loads:
                load.wait()
        if (i + 1) * blk == rows:
            stores.extend([pull(mid, mid_h, sem.at[5]), pull(n2, n2_h, sem.at[6]), pull(n2t, n2t_h, sem.at[7])])

    def flush(i, blk):
        sl = pl.ds(i * blk, blk)
        outb[sl, :] = out[sl, :].astype(BF)
        dnb[sl, :] = dn[sl, :].astype(BF)
        stores.append(pull(outb.at[sl, :], out_h.at[sl, :], sem.at[8 + i]))
        stores.append(pull(dnb.at[sl, :], dn_h.at[sl, :], sem.at[12 + i]))

    for q in range(2):
        db_ref[:, cols[q]] = ffn_quarter(
            n2, n2t, og, wu.at[q], wd.at[q], vec_ref[:, biases[q]], out, dn, act_s, dh_s, gd.at[q], gu.at[q], q == 0,
            enter if q == 0 else None, flush if q == 1 else None,
        )
        stores.append(pull(gd.at[q], (send_h, keep_h)[q].at[0:part, :], sem.at[16 + q]))
        stores.append(pull(gu.at[q], (send_h, keep_h)[q].at[part:, :], sem.at[20 + q]))
    for store in stores:
        store.wait()


def ffn_own(at, bits, x, ctx_own, ctx_other, wo_own, wo_other, vec, og, wu, wd, after=()):
    rows, d = x.shape
    ff = wu.shape[1]
    part = ff // 2
    half = ctx_own.shape[1]
    return call(
        lambda *refs: ffn_own_kernel(at, *refs),
        after,
        prefetch=1,
        in_specs=[
            whole((rows, d)), whole((rows, half)), whole((rows, half)), whole((half, d)), whole((half, d)), whole(vec.shape),
        ] + [ANY] * 3,
        out_specs=[ANY] * 7 + [whole_out((1, ff))],
        scratch=[
            pltpu.VMEM((rows, d), BF), pltpu.VMEM((2, d, part), BF), pltpu.VMEM((2, part, d), BF),
            pltpu.VMEM((rows, d), F32), pltpu.VMEM((rows, d), BF), pltpu.VMEM((d, rows), BF),
            pltpu.VMEM((rows, d), F32), pltpu.VMEM((rows, d), F32), pltpu.VMEM((rows, d), BF), pltpu.VMEM((rows, d), BF),
            pltpu.VMEM((rows, part), BF), pltpu.VMEM((rows, part), BF),
            pltpu.VMEM((2, part, d), BF), pltpu.VMEM((2, d, part), BF),
            pltpu.SemaphoreType.DMA((22,)),
        ],
        out_shape=[
            struct((rows, d), F32), struct((rows, d), BF), struct((d, rows), BF), struct((rows, d), BF),
            struct((rows, d), BF), struct((part + d, d), BF), struct((part + d, d), BF),
            struct((1, ff), F32),
        ],
        estimate=EST["ffn_own"],
        name="ffn_own",
        mib=56,
    )(bits, x, ctx_own, ctx_other, wo_own, wo_other, vec, og, wu, wd)


BLOCK_BITS = 4


def sub_block(s, q, x, n):
    out = q + 2 * x
    for k in range(2, n):
        out = out + (((s >> (n - 1 - k)) & 1) << k)
    return out


def put_blocks(grads, stack, q, n, sem, at):
    count = 1 << (n - 2)
    size = grads[0].shape[0] // count
    return [
        pull(
            grads[x].at[s * size : (s + 1) * size, :],
            stack.at[pl.ds(pl.multiple_of(sub_block(s, q, x, n) * size, size), size), :],
            sem.at[at + x * count + s],
        )
        for x in range(2)
        for s in range(count)
    ]


def gather_weights(bits_ref, near, near_x, rest, w, sem, at):
    rows = near.shape[0]
    b = bits_ref[1]
    return [
        pull(near, w.at[block(b, rows), :], sem.at[at]),
        pull(near_x, w.at[block(1 - b, rows), :], sem.at[at + 1]),
        pull(rest, w.at[2 * rows :, :], sem.at[at + 2]),
    ]


def ffn_mine_kernel(
    n, bits_ref, n2_ref, b_ref, near_h, near_x_h, rest_h, og_h, n2t_h, out_h, dn_h, stack_h, db_ref,
    w_ref, og, n2t, out, dn, outb, dnb, act_s, dh_s, gd, gu, sem,
):
    d = og.shape[1]
    part = w_ref.shape[0] - d
    c = bits_ref[0]
    bias_at = b_ref.shape[1] - 2 * part
    at = 10 + (1 << (n - 1))
    loads = gather_weights(bits_ref, near_h, near_x_h, rest_h, w_ref, sem, at)
    loads += [pull(og_h, og, sem.at[0]), pull(n2t_h, n2t, sem.at[1])]
    for load in loads:
        load.wait()
    stores = []

    def flush(i, blk):
        sl = pl.ds(i * blk, blk)
        outb[sl, :] = out[sl, :].astype(BF)
        dnb[sl, :] = dn[sl, :].astype(BF)
        stores.append(pull(outb.at[sl, :], out_h.at[sl, :], sem.at[2 + i]))
        stores.append(pull(dnb.at[sl, :], dn_h.at[sl, :], sem.at[6 + i]))

    bias = b_ref[:, pl.ds(pl.multiple_of(bias_at + c * part, 128), part)]
    db_ref[...] = ffn_quarter(
        n2_ref, n2t, og, w_ref.at[0:d, :], w_ref.at[d:, :], bias, out, dn, act_s, dh_s, gd, gu, True, None, flush
    )
    stores += put_blocks((gd, gu), stack_h, c, n, sem, 10)
    for store in stores:
        store.wait()


def ffn_mine(bits, n2, near, near_x, rest, bias, og, n2t, after=()):
    rows, d = og.shape
    part = 2 * near.shape[0] + rest.shape[0] - d
    n = min(bits.shape[0], BLOCK_BITS)
    return call(
        lambda *refs: ffn_mine_kernel(n, *refs),
        after,
        prefetch=1,
        in_specs=[whole((rows, d)), whole(bias.shape)] + [ANY] * 5,
        out_specs=[ANY] * 3 + [whole_out((1, part))],
        scratch=[
            pltpu.VMEM((d + part, d), BF),
            pltpu.VMEM((rows, d), BF), pltpu.VMEM((d, rows), BF), pltpu.VMEM((rows, d), F32), pltpu.VMEM((rows, d), F32),
            pltpu.VMEM((rows, d), BF), pltpu.VMEM((rows, d), BF),
            pltpu.VMEM((rows, part), BF), pltpu.VMEM((rows, part), BF), pltpu.VMEM((part, d), BF), pltpu.VMEM((d, part), BF),
            pltpu.SemaphoreType.DMA((13 + (1 << (n - 1)),)),
        ],
        out_shape=[
            struct((rows, d), BF), struct((rows, d), BF), struct((4 * part, d), BF), struct((1, part), F32),
        ],
        estimate=EST["ffn_mine"],
        name="ffn_mine",
        mib=56,
    )(bits, n2, bias, near, near_x, rest, og, n2t)


def ffn_far_kernel(
    at, n, bits_ref, len_ref, n2_ref, b_ref, vec_ref, near_h, near_x_h, rest_h, og_h, n2t_h, mid_h, out1_h, dn1_h, out2_h, dn2_h,
    co_h, cx_h, woo_h, wox_h, stack_in,
    lay_h, gm_h, dco_h, dcx_h, stack_h, dwoo_h, dwox_h, sums_ref, db_ref,
    w_ref, og, n2t, mid, out1, dn1, out2, dn2, co, cx, woo, wox, out, dn, act_s, dh_s, gd, gu, lay, gmb, dco, dcx, dwoo, dwox, sem,
):
    rows, d = og.shape
    part = w_ref.shape[0] - d
    half = co.shape[1]
    c = bits_ref[0]
    length = len_ref[0]
    bias_at = b_ref.shape[1] - 2 * part
    first = gather_weights(bits_ref, near_h, near_x_h, rest_h, w_ref, sem, 18 + (1 << (n - 1)))
    loads = [
        pull(src, dst, sem.at[i])
        for i, (src, dst) in enumerate((
            (og_h, og), (n2t_h, n2t), (mid_h, mid), (dn1_h, dn1), (dn2_h, dn2), (out1_h, out1), (out2_h, out2),
            (woo_h, woo), (wox_h, wox), (co_h, co), (cx_h, cx),
        ))
    ]
    for load in first + loads[:1]:
        load.wait()
    sums_ref[...] = jnp.zeros_like(sums_ref)
    stores = []

    def finish(i, blk):
        if i == 0:
            for load in loads[1:]:
                load.wait()
        sl = slice(i * blk, (i + 1) * blk)
        v = mid[sl, :]
        out_sum = out1[sl, :].astype(F32) + out2[sl, :].astype(F32) + out[sl, :]
        lay[sl, :] = (v + out_sum + vec_ref[:, at.down_bias]).astype(BF)
        unit, r = norm_rows(v)
        gn = dn1[sl, :].astype(F32) + dn2[sl, :].astype(F32) + dn[sl, :]
        o = og[sl, :].astype(F32)
        g = o + norm_back(gn * vec_ref[:, at.gain2], unit, r)
        mid[sl, :] = g
        low = g.astype(BF)
        gmb[sl, :] = low
        for k, val in enumerate((g, gn * unit, gn, o)):
            sums_ref[k : k + 1, :] += jnp.sum(val, axis=0, keepdims=True)
        valid = lax.broadcasted_iota(jnp.int32, (blk, 1), 0) + i * blk < length
        dco[sl, :] = jnp.where(valid, dot(low, woo[...], 1, 1), 0.0).astype(BF)
        dcx[sl, :] = jnp.where(valid, dot(low, wox[...], 1, 1), 0.0).astype(BF)

    bias = b_ref[:, pl.ds(pl.multiple_of(bias_at + (1 - c) * part, 128), part)]
    db_ref[...] = ffn_quarter(
        n2_ref, n2t, og, w_ref.at[0:d, :], w_ref.at[d:, :], bias, out, dn, act_s, dh_s, gd, gu, True, None, finish
    )
    stores = put_blocks((gd, gu), stack_h, 1 - c, n, sem, 18)
    stores += [
        pull(src, dst, sem.at[12 + k])
        for k, (src, dst) in enumerate(((lay, lay_h), (mid, gm_h), (dco, dco_h), (dcx, dcx_h)))
    ]
    dwoo[...] = dot(gmb[...], co[...], 0, 0).astype(BF)
    dwox[...] = dot(gmb[...], cx[...], 0, 0).astype(BF)
    stores += [pull(dwoo, dwoo_h, sem.at[16]), pull(dwox, dwox_h, sem.at[17])]
    for store in stores:
        store.wait()


def ffn_far(
    at, bits, length, n2, near, near_x, rest, bias, vec, og, n2t, mid, out1, dn1, out2, dn2, ctx_own, ctx_other, wo_own,
    wo_other, stack, after=(),
):
    rows, d = og.shape
    part = 2 * near.shape[0] + rest.shape[0] - d
    n = min(bits.shape[0], BLOCK_BITS)
    half = ctx_own.shape[1]
    bf = lambda *shape: pltpu.VMEM(shape, BF)
    f32 = lambda *shape: pltpu.VMEM(shape, F32)
    return call(
        lambda *refs: ffn_far_kernel(at, n, *refs),
        after,
        prefetch=2,
        in_specs=[whole((rows, d)), whole(bias.shape), whole(vec.shape)] + [ANY] * 15,
        out_specs=[ANY] * 7 + [whole_out((8, d)), whole_out((1, part))],
        scratch=[
            bf(d + part, d), bf(rows, d), bf(d, rows), f32(rows, d), bf(rows, d), bf(rows, d), bf(rows, d), bf(rows, d),
            bf(rows, half), bf(rows, half), bf(half, d), bf(half, d), f32(rows, d), f32(rows, d),
            bf(rows, part), bf(rows, part), bf(part, d), bf(d, part), bf(rows, d), bf(rows, d), bf(rows, half),
            bf(rows, half), bf(d, half), bf(d, half), pltpu.SemaphoreType.DMA((21 + (1 << (n - 1)),)),
        ],
        out_shape=[
            struct((rows, d), BF), struct((rows, d), F32), struct((rows, half), BF), struct((rows, half), BF),
            struct(stack.shape, BF), struct((d, half), BF), struct((d, half), BF), struct((8, d), F32), struct((1, part), F32),
        ],
        alias={19: 4},
        estimate=EST["ffn_far"],
        name="ffn_far",
        mib=56,
    )(
        bits, length, n2, bias, vec, near, near_x, rest, og, n2t, mid, out1, dn1, out2, dn2, ctx_own, ctx_other, wo_own,
        wo_other, stack,
    )


def by_pairs(wcat, matrices, rows, width):
    for p in range(width // 128):
        for i in range(3):
            to = slice((3 * p + i) * 128, (3 * p + i + 1) * 128)
            ref, base = matrices[i]
            wcat[rows, to] = ref[:, base + p * 128 : base + (p + 1) * 128]


def share_kernel(bits_ref, g_ref, wm, wf, out_ref, wcat):
    width = g_ref.shape[1] // 3
    c = bits_ref[0]
    half = wm.shape[0]

    @pl.when(pl.program_id(0) == 0)
    def _():
        for ref, part in ((wm, c), (wf, 1 - c)):
            by_pairs(wcat, [(ref, i * width) for i in range(3)], block(part, half), width)

    out_ref[...] = dot(g_ref[...], wcat[...], 1, 1).astype(BF)


def input_share(bits, g, w_mine, w_far, after=()):
    rows, cols = g.shape
    d = 2 * w_mine.shape[0]
    blk = 512
    row = lambda w: pl.BlockSpec((blk, w), lambda i, *_: (i, 0))
    return call(
        share_kernel, after, prefetch=1, grid=(rows // blk,),
        in_specs=[row(cols), whole(w_mine.shape), whole(w_far.shape)], out_specs=row(d),
        out_shape=struct((rows, d), BF), scratch=[pltpu.VMEM((d, cols), BF)],
        estimate=EST["share"], name="input_share", mib=56,
    )(bits, g, w_mine, w_far)


def input_grad_kernel(at, x_ref, gm_ref, vec_ref, g_ref, share_ref, wq, wk, wv, out_ref, sums_ref, wcat):
    width = wq.shape[1]

    @pl.when(pl.program_id(0) == 0)
    def _():
        sums_ref[...] = jnp.zeros_like(sums_ref)
        by_pairs(wcat, [(ref, 0) for ref in (wq, wk, wv)], slice(None), width)

    gn = dot(g_ref[...], wcat[...], 1, 1) + share_ref[...].astype(F32)
    n, r = norm_rows(x_ref[...].astype(F32))
    out_ref[...] = (gm_ref[...] + norm_back(gn * vec_ref[:, at.gain1], n, r)).astype(BF)
    sums_ref[0:1, :] += jnp.sum(gn * n, axis=0, keepdims=True)
    sums_ref[1:2, :] += jnp.sum(gn, axis=0, keepdims=True)


def input_grad(at, x, gm, vec, g, share, wq, wk, wv, after=()):
    rows, d = x.shape
    width = wq.shape[1]
    blk = 256
    row = lambda w: pl.BlockSpec((blk, w), lambda i, *_: (i, 0))
    return call(
        lambda *refs: input_grad_kernel(at, *refs),
        after,
        grid=(rows // blk,),
        in_specs=[row(d), row(d), whole(vec.shape), row(3 * width), row(d)] + [whole((d, width))] * 3,
        out_specs=[row(d), whole_out((8, d))],
        out_shape=[struct((rows, d), BF), struct((8, d), F32)],
        scratch=[pltpu.VMEM((d, 3 * width), BF)],
        estimate=EST["input_grad"],
        name="input_grad",
        mib=56,
    )(x, gm, vec, g, share, wq, wk, wv)


def wide_qkv(bits, mine, other, after=()):
    half, width = mine.shape
    width //= 4

    def kernel(bits_ref, m_ref, o_ref, *outs):
        c = bits_ref[0]

        def put(ref):
            for i, out in enumerate(outs[:3]):
                for p in range(width // 128):
                    out[:, p * 128 : (p + 1) * 128] = ref[:, (3 * p + i) * 128 : (3 * p + i + 1) * 128].astype(F32)
            outs[3][...] = ref[:, 3 * width :].astype(F32).T

        own = pl.program_id(0) == c

        @pl.when(own)
        def _():
            put(m_ref)

        @pl.when(jnp.logical_not(own))
        def _():
            put(o_ref)

    return call(
        kernel, after, prefetch=1, grid=(2,),
        in_specs=[whole(mine.shape)] * 2,
        out_specs=[pl.BlockSpec((half, width), lambda i, *_: (i, 0))] * 3
        + [pl.BlockSpec((width, half), lambda i, *_: (0, i))],
        out_shape=[struct((2 * half, width), F32)] * 3 + [struct((width, 2 * half), F32)],
        estimate=EST["move"], name="wide_qkv", mib=56,
    )(bits, mine, other)


def wide_ffn(bits, stack, after=()):
    rows, d = stack.shape
    n = min(bits.shape[0], BLOCK_BITS)
    part = rows // 4
    count = 1 << (n - 2)
    size = part // count

    def kernel(bits_ref, d_ref, u_ref, down_ref, up_ref):
        down_ref[...] = d_ref[...].astype(F32)
        up_ref[...] = u_ref[...].astype(F32)

    def place(x):
        return lambda t, *_: (sub_block(lax.rem(t, count), t // count, x, n), 0)

    return call(
        kernel, after, prefetch=1, grid=(2 * count,),
        in_specs=[pl.BlockSpec((size, d), place(0)), pl.BlockSpec((size, d), place(1))],
        out_specs=[
            pl.BlockSpec((size, d), lambda t, *_: (t, 0)),
            pl.BlockSpec((size, d), lambda t, *_: (lax.rem(t, count), t // count)),
        ],
        out_shape=[struct((2 * part, d), F32), struct((part, 2 * d), F32)],
        estimate=EST["move"], name="wide_ffn", mib=56,
    )(bits, stack, stack)


class Links:
    def __init__(self, dp_size):
        self.size = dp_size
        self.bits = dp_size.bit_length() - 1
        index = lax.axis_index("dp")
        self.value = jnp.stack([(index >> i) & 1 for i in range(self.bits)]).astype(jnp.int32)

    def swap(self, value, at):
        return lax.ppermute(value, "dp", [(i, i ^ (1 << at)) for i in range(self.size)])

    def across(self, value):
        return lax.ppermute(value, "tensor", [(0, 1), (1, 0)])

    def join(self, mine, other, at, after=()):
        half, width = mine.shape
        if half % 16:
            low = self.value[at] == 0
            return jnp.concatenate([jnp.where(low, mine, other), jnp.where(low, other, mine)], 0)

        def moves(bits, ins, outs):
            return [
                (ins[0], outs[0].at[block(bits[at], half), :]), (ins[1], outs[0].at[block(1 - bits[at], half), :])
            ]

        return arrange(self.value, [mine, other], [(2 * half, width)], moves, "join", after)[0]


def halve(bits, keep, recv, bit, after=()):
    keep, recv, *_ = lax.optimization_barrier((keep, recv, *after))
    size = keep.shape[0] // 2

    def half(at):
        a, b = (lax.dynamic_slice_in_dim(v, at * size, size, 0).astype(F32) for v in (keep, recv))
        return (a + b).astype(BF)

    return half(1 - bits[bit]), half(bits[bit])


class Halve:
    def __init__(self, links, keep, recv):
        self.links, self.keep, self.recv, self.at = links, keep, recv, 0
        low = min(links.bits, BLOCK_BITS)
        self.order = [*range(low), *reversed(range(low, links.bits))]
        self.done = False

    def advance(self, after):
        links, size = self.links, self.keep.shape[0]
        self.at += 1
        self.done = self.at == links.bits
        if self.done:
            parts = [(self.keep, 0, 0, size), (self.recv, 0, 0, size)]
            self.keep, = fold(links.value, parts, size, [(0, size)], "fold_own", after)
            return
        bit = self.order[self.at]
        send, self.keep = halve(links.value, self.keep, self.recv, bit, after)
        self.recv = links.swap(send, bit)


RIDE = 32


def ride_kernel(rows, cut, bits_ref, *refs):
    *ins, small_ref, send_ref, keep_ref, next_ref, acc = refs
    width = small_ref.shape[1]
    small = small_ref[...]
    total = None
    for ref in ins:
        value = ref[0:rows, :].astype(F32)
        total = value if total is None else total + value
        if ref.shape[0] > rows:
            riding = ref[rows : rows + RIDE, :].astype(F32)
            small = small + riding[0:8] + riding[8:16] + riding[16:24]
    next_ref[...] = small
    if send_ref is None:
        keep_ref[...] = total.astype(BF)
        return
    acc[...] = total
    if cut is None:
        size = rows
        send_ref[0:size, :] = total.astype(BF)
        keep_ref[...] = total.astype(BF)
    else:
        size = rows // 2
        bit = bits_ref[cut]
        low, high = acc[0:size, :], acc[size : 2 * size, :]
        send_ref[0:size, :] = jnp.where(bit == 0, high, low).astype(BF)
        keep_ref[...] = jnp.where(bit == 0, low, high).astype(BF)
    parts = [p.astype(BF) for p in split3(small)] + [jnp.zeros((RIDE - 24, width), BF)]
    send_ref[size:, :] = jnp.concatenate(parts, 0)


def ride(bits, parts, small, cut, last, after=()):
    rows = parts[0].shape[0]
    width = small.shape[1]
    size = rows // 2 if cut is not None else rows
    shapes = [struct((size, width), BF), struct(small.shape, F32)]
    if not last:
        shapes.insert(0, struct((size + RIDE, width), BF))

    def kernel(bits_ref, *refs):
        refs = list(refs)
        if last:
            refs.insert(len(parts) + 1, None)
        ride_kernel(rows, cut, bits_ref, *refs)

    out = call(
        kernel, after, prefetch=1, in_specs=[whole(a.shape) for a in (*parts, small)],
        out_specs=[whole_out(t.shape) for t in shapes], out_shape=shapes,
        scratch=[pltpu.VMEM((rows, width), F32)], estimate=EST["move"], name="ride",
    )(bits, *parts, small)
    return (None, *out) if last else out


def layer(
    dp_size, inputs, lengths, norm1_gain, norm1_shift, query_weight, query_bias, key_weight, key_bias, value_weight,
    value_bias, out_weight, out_bias, norm2_gain, norm2_shift, up_weight, up_bias, down_weight, down_bias, out_grad,
):
    rows, d = inputs.shape
    width = query_weight.shape[1]
    ff = up_weight.shape[1]
    part = ff // 2
    links = Links(dp_size)
    bits = links.value
    tensor = lax.axis_index("tensor")
    length = lax.dynamic_slice_in_dim(lengths, tensor, 1, 0)
    cos, sin = (jnp.asarray(t) for t in rotary_tables(rows))
    at = Row(d, width, ff)
    vec = jnp.concatenate(
        [norm1_gain, norm1_shift, out_bias, norm2_gain, norm2_shift, down_bias, query_bias, key_bias, value_bias, up_bias]
    ).reshape(1, -1)

    def qkv_moves(bits_ref, ins, outs):
        return [
            (w.at[block(bits_ref[0], d // 2), :], outs[0].at[:, i * width : (i + 1) * width]) for i, w in enumerate(ins)
        ]

    near_rows = 5 * d // 12
    half = width // 2
    def cut_moves(bits_ref, ins, outs):
        c, b = bits_ref[0], bits_ref[1]
        wu, wd = ins
        near, rest = outs
        cols = block(c, part)
        return [
            (wu.at[block(b, near_rows), cols], near),
            (wu.at[2 * near_rows :, cols], rest.at[0 : d - 2 * near_rows, :]),
            (wd.at[block(c, part), :], rest.at[d - 2 * near_rows :, :]),
        ]

    qkv_mine, = arrange(bits, [query_weight, key_weight, value_weight], [(d // 2, 3 * width)], qkv_moves, "cut_qkv", mib=56)
    qkv_mine = links.across(qkv_mine)
    normed, normed_t, *own, ctx_own, aug_own, near, rest = heads_own(
        at, cut_moves, [(near_rows, d), (d + part - 2 * near_rows, d)], bits, length, inputs, vec, query_weight,
        key_weight, value_weight, cos, sin, up_weight, down_weight,
    )
    bias_x = links.across(vec[:, at.qkv.start :])
    near, out_x = links.across(near), links.across(out_weight)
    qkv_mine, _ = lax.optimization_barrier((qkv_mine, ctx_own))
    qkv_far = links.swap(qkv_mine, 0)
    *other, ctx_x, aug_x = heads_other(bits, length, normed, qkv_mine, qkv_far, bias_x, cos, sin, after=(ctx_own,))
    near, out_x, rest, ctx_x = lax.optimization_barrier((near, out_x, rest, ctx_x))
    rest = links.across(rest)
    near_x = links.swap(near, 1)
    near_far = links.swap(near, 0)
    mid, n2, n2t, out1, dn1, w_send, w_keep, dbu = ffn_own(
        at, bits, inputs, ctx_own, ctx_x, out_weight, out_x, vec, out_grad, up_weight, down_weight
    )

    w_recv = links.swap(w_send, 0)
    near_x_far, rest_far = links.swap(near_x, 0), links.swap(rest, 0)
    out2, dn2, stack, dbu_mine = ffn_mine(bits, n2, near, near_x, rest, bias_x, out_grad, n2t, after=(mid,))
    own_sum = Halve(links, w_keep, w_recv)
    own_sum.advance((out2,))
    layer_out, gm, g_own, g_x, stack, dwo, dwo_x, sums2, dbu_far = ffn_far(
        at, bits, length, n2, near_far, near_x_far, rest_far, bias_x, vec, out_grad, n2t, mid, out1, dn1, out2, dn2,
        ctx_own, ctx_x, out_weight, out_x, stack, after=(own_sum.keep,),
    )
    blocks = min(dp_size, 1 << BLOCK_BITS)

    def turned(rows_, first, second):
        return rows_.reshape(first, second, -1, d).swapaxes(0, 1).reshape(-1, d)

    if dp_size > blocks:
        stack = turned(stack, blocks, dp_size // blocks)
    stack = lax.psum_scatter(stack, "dp", scatter_dimension=0, tiled=True)
    n = d // 2
    gx, sums_x, qx_s, qx_k = attend_back(
        bits, length, *other, g_x, ctx_x, aug_x, cos, sin, normed_t, dwo_x
    )
    qx_r = links.swap(qx_s, 0)
    own_sum.advance((qx_k,))
    share = input_share(bits, gx, qkv_mine, qkv_far, after=(own_sum.keep,))
    qx, = fold(bits, [(qx_k, 0, 0, n), (qx_r, 0, 0, n)], n, [(0, n)], "fold_qkv_core", after=(share,))
    qx_y = links.across(qx)
    go, sums_o, qo_s, qo_k = attend_back(
        bits, length, *own, g_own, ctx_own, aug_own, cos, sin, normed_t, dwo, after=(qx,), est=12
    )
    own_sum.advance((qo_k,))
    qo_r = links.swap(qo_s, 0)
    input_grad_out, sums1 = input_grad(
        at, inputs, gm, vec, go, share, query_weight, key_weight, value_weight, after=(own_sum.keep,)
    )
    q, = fold(bits, [(qo_k, 0, 0, n), (qx_y, 0, 0, n)], n, [(0, n)], "fold_qkv_y", after=(sums1,))
    q_s, q_k = halve(bits, q, qo_r, 1)
    q_r = links.swap(q_s, 1)
    stack, q_k = lax.optimization_barrier((stack, q_k))
    stack_r = links.across(stack)
    while not own_sum.done:
        own_sum.advance((q_k,))
    size = stack.shape[0]
    parts = [(stack_r, 0, 0, size), (own_sum.keep, 0, 0, size)]
    stack, = fold(bits, parts, size, [(0, size)], "fold_stack", after=(own_sum.keep,))
    gathered = lax.all_gather(stack, "dp", axis=0, tiled=True)
    if dp_size > blocks:
        gathered = turned(gathered, dp_size // blocks, blocks)

    c = bits[0]
    halves = lambda a, b: [jnp.where(tensor == 0, a, b), jnp.where(tensor == 0, b, a)]
    mine_up, far_up = jnp.where(c == 0, dbu_mine, dbu_far), jnp.where(c == 0, dbu_far, dbu_mine)
    small = jnp.concatenate(
        [sums1[:2].reshape(-1), sums2[:4].reshape(-1)]
        + halves(
            jnp.concatenate([v.reshape(-1) for v in (sums_o, dbu)]),
            jnp.concatenate([v.reshape(-1) for v in (sums_x, mine_up, far_up)]),
        )
    )
    used = small.shape[0]
    cols = q.shape[1]
    small = jnp.pad(small, (0, 8 * cols - used)).reshape(8, cols)

    last = links.bits - 1
    parts = [q_k, q_r]
    after = (stack,)
    for bit in range(2, links.bits):
        send, keep, small = ride(bits, parts, small, bit if bit < last else None, False, after)
        after = ()
        parts = [keep, links.swap(send, bit)]
    _, q, small = ride(bits, parts, small, None, True)
    small_r = links.across(small)
    others = [0, 1]
    for bit in reversed(range(1, last)):
        q_r = links.swap(q, bit)
        after = ()
        if others:
            size = small.shape[0]
            small, = fold(bits, [(small, 0, 0, size), (small_r, 0, 0, size)], size, [(0, size)], "fold_small", after=(q,))
            small_r = links.swap(small, others.pop(0))
            after = (small,)
        if bit == 1:
            grad_down, grad_up = wide_ffn(bits, gathered, after=after)
            after = (grad_up,)
        q = links.join(q, q_r, bit, after=after)
    q_far = links.swap(q, 0)
    small = small + small_r
    for bit in others:
        small = small + links.swap(small, bit)
    grad_q, grad_k, grad_v, grad_out = wide_qkv(bits, q, q_far)

    small = small.reshape(-1)
    gain1, shift1, out_b, gain2, shift2, down_b = (small[i * d : (i + 1) * d] for i in range(6))
    side = 3 * width + ff
    mine = lax.dynamic_slice_in_dim(small, 6 * d + tensor * side, side, 0)
    qkv_bias = mine[: 3 * width].reshape(-1, 3, 128)
    return (
        layer_out, input_grad_out, gain1, shift1,
        grad_q, qkv_bias[:, 0].reshape(-1), grad_k, qkv_bias[:, 1].reshape(-1), grad_v, qkv_bias[:, 2].reshape(-1),
        grad_out, out_b, gain2, shift2, grad_up, mine[3 * width :], grad_down, down_b,
    )


def solution(mesh):
    rows = P(("dp", "tensor"), None)
    cols = P(None, "tensor")
    tens = P("tensor")
    return jax.shard_map(
        lambda *args: layer(mesh.shape["dp"], *args),
        mesh=mesh,
        in_specs=(
            rows, P("dp"), P(), P(), cols, tens, cols, tens, cols, tens, P("tensor", None), P(), P(), P(), cols, tens,
            P("tensor", None), P(), rows,
        ),
        out_specs=(
            rows, rows, P(), P(), cols, tens, cols, tens, cols, tens, P("tensor", None), P(), P(), P(), cols, tens,
            P("tensor", None), P(),
        ),
        check_vma=False,
    )
```

time: 463 us -> 361 us (0.78); the launches traced: 454 us -> 357 us
  waiting for transfers between devices: 172 us -> 106 us
  starting transfers between devices: 48.9 us -> 21.3 us
  between operations: 2.1 us -> 15 us
  other arithmetic: 19 us -> 7.81 us
  local copies, waits for them, and re-layouts: 23.1 us -> 12.3 us
  Pallas kernels: 189 us -> 195 us
    ppermute x10 -> x8, waiting for transfers between devices: 85.6 us -> 17.6 us  [across(): return lax.ppermute(value, 'tensor', [(0, 1), (1, 0)])]
    ppermute x44 -> x19, starting transfers between devices: 34.8 us -> 12.8 us  [swap(): lax.ppermute(value, 'dp', [(i, i ^ 1 << at) for i in range(self.size)])]
    reduce_scatter x0 -> x1, waiting for transfers between devices: none -> 13.3 us  [layer(): stack = lax.psum_scatter(stack, 'dp', scatter_dimension=0, tiled=True)]
    ppermute x44 -> x19, waiting for transfers between devices: 86.4 us -> 74.9 us  [swap(): lax.ppermute(value, 'dp', [(i, i ^ 1 << at) for i in range(self.size)])]
    reshape x12 -> x5, local copies, waits for them, and re-layouts: 8.64 us -> 0.66 us  [the longest x1 0.62 us: layer(): vec = jnp.concatenate([norm1_gain, norm1_shift, out_bias, norm2_gain, nor...]
    unnamed x62 -> x93, local copies, waits for them, and re-layouts: 1.17 us -> 7.59 us
    dynamic_slice x19 -> x0, local copies, waits for them, and re-layouts: 6.02 us -> none  [the longest x5 3.71 us: layer(): lax.dynamic_slice_in_dim(w, c * (w.shape[axis] // 2), w.shape[axis] // 2,...]
    pallas_call x11 -> x23, Pallas kernels: 189 us -> 195 us  [call(): return lambda *args: run(*args, *after)]
  transfers between devices with their start and end apart: 54 -> 29, of which waited for: 22 -> 13; matrix products, arithmetic and copies ran while one was open for 8% -> 3% of each run, Pallas kernels for 33% -> 52%
where the time goes in v2:
time: 361 us; the launch traced here: 357 us
  Pallas kernels  195 us (54%)
  waiting for transfers between devices  106 us (29%)
  starting transfers between devices  21.3 us (6%)
  between operations  15 us (4%)
  local copies, waits for them, and re-layouts  12.3 us (3%)
  other arithmetic  7.81 us (2%)
    pallas_call x23, Pallas kernels, call(): return lambda *args: run(*args, *after)  195 us
    ppermute x19, waiting for transfers between devices, swap(): lax.ppermute(value, 'dp', [(i, i ^ 1 << at) for i in range(self.size)])  74.9 us
    ppermute x8, waiting for transfers between devices, across(): return lax.ppermute(value, 'tensor', [(0, 1), (1, 0)])  17.6 us
    reduce_scatter x1, waiting for transfers between devices, layer(): stack = lax.psum_scatter(stack, 'dp', scatter_dimension=0, tiled=True)  13.3 us
    ppermute x19, starting transfers between devices, swap(): lax.ppermute(value, 'dp', [(i, i ^ 1 << at) for i in range(self.size)])  12.8 us
    ppermute x8, starting transfers between devices, across(): return lax.ppermute(value, 'tensor', [(0, 1), (1, 0)])  8.43 us
    unnamed x93, local copies, waits for them, and re-layouts  7.59 us
  transfers between devices with their start and end apart: 29, of which 13 were waited for; matrix products, arithmetic and copies ran while one was open for 3% of the time, Pallas kernels for 52%

profile of v2, /device:TPU:0, one launch (start us, length us, event | category | flops | bytes accessed | tf_op | source)
XLA Modules:
  0.0 357.2 jit_solution(16307803640121628195)
XLA Ops:
  8.0 2.9 cut_qkv.1
  10.9 3.0 collective-permute-start.2
  15.4 19.6 %heads_own.1 = (bf16[1024,768]{1,0:T(8,128)(2,1)}, bf16[768,1024]{1,0:T(8,128)(2,1)}, bf16[1024,384]{1,0:T(8,128)(2,1)}, bf16[1024,384]{1,0:T(8,128)(2,1)}, bf16...) custom-call(s32[4]{0:T(128)} %pad_add_fusion.refs_0_, ...), custom_call_target="tpu_custom_call" | custom-call | flops 17600000000 | bytes 1000 | tf_op jit(solution)/shard_map/heads_own/pallas_call | solution.py:82
  40.5 17.2 %heads_other.1 = (bf16[1024,384]{1,0:T(8,128)(2,1)}, bf16[1024,384]{1,0:T(8,128)(2,1)}, bf16[1024,384]{1,0:T(8,128)(2,1)}, bf16[1024,384]{1,0:T(8,128)(2,1)}, bf16[1024,384]{1,0:T(8,128)(2,1)}) custom-call(s32[4]{0:T(128)} %pad_add_fusion.refs_0_, s32[1]{0:T(128)} %dynamic_slice.54.refs_1_, bf16[1024,768]{1,0:T(8,128)(2,1)} %get-tuple-element.95.refs_2_, ...), custom_call_target="tpu_custom_call" | custom-call | flops 109999996928 | bytes 1000 | tf_op jit(solution)/shard_map/heads_other/pallas_call | solution.py:82
  57.8 4.8 %collective-permute-done.1.refs_5_.refs_18_ = bf16[384,768]{1,0:T(8,128)(2,1)S(1)} collective-permute-done((bf16[384,768]{1,0:T(8,128)(2,1)S(1)}, bf16[384,768]{1,0:T(8,128)(2,1)S(1)}, u32[]{:S(2)}, u32[]{:S(2)}) %collective-permute-start.1) | collective-permute-done | bytes 589856 | tf_op jit(solution)/shard_map/ppermute | solution.py:887
  65.5 27.6 %ffn_own.1 = (f32[1024,768]{1,0:T(8,128)}, bf16[1024,768]{1,0:T(8,128)(2,1)}, bf16[768,1024]{1,0:T(8,128)(2,1)}, bf16[1024,768]{1,0:T(8,128)(2,1)}, bf16[1024,76...) custom-call(s32[4]{0:T(128)} %pad_add_fusion.refs_0_, ...), custom_call_target="tpu_custom_call" | custom-call | flops 11000000 | bytes 1000 | tf_op jit(solution)/shard_map/ffn_own/pallas_call | solution.py:82
  94.4 16.3 %ffn_mine.1 = (bf16[1024,768]{1,0:T(8,128)(2,1)}, bf16[1024,768]{1,0:T(8,128)(2,1)}, bf16[3072,768]{1,0:T(8,128)(2,1)}, f32[1,768]{1,0:T(1,128)}) custom-call(s32[4]{0:T(128)} %pad_add_fusion.refs_0_, bf16[1024,768]{1,0:T(8,128)(2,1)} %get-tuple-element.100.refs_1_.refs_2_, f32[1,2688]{1,0:T(1,128)} %copy-done.40, ...), custom_call_target="tpu_custom_call" | custom-call | flops 109999996928 | bytes 1000 | tf_op jit(solution)/shard_map/ffn_mine/pallas_call | solution.py:82
  115.3 22.8 %ffn_far.1 = (bf16[1024,768]{1,0:T(8,128)(2,1)}, f32[1024,768]{1,0:T(8,128)}, bf16[1024,384]{1,0:T(8,128)(2,1)}, bf16[1024,384]{1,0:T(8,128)(2,1)}, bf16[3072,76...) custom-call(s32[4]{0:T(128)} %pad_add_fusion.refs_0_, ...), custom_call_target="tpu_custom_call", output_to_operand_aliasing={{4}: (19, {})} | custom-call | flops 109999996928 | bytes 1000 | tf_op jit(solution)/shard_map/ffn_far/pallas_call | solution.py:82
  138.2 26.1 %attend_back.2 = (bf16[1024,1152]{1,0:T(8,128)(2,1)}, f32[1,1152]{1,0:T(1,128)}, bf16[384,1536]{1,0:T(8,128)(2,1)}, bf16[384,1536]{1,0:T(8,128)(2,1)}) custom-call(s32[4]{0:T(128)} %pad_add_fusion.refs_0_, s32[1]{0:T(128)} %dynamic_slice.54.refs_1_, bf16[1024,384]{1,0:T(8,128)(2,1)} %get-tuple-element.123.refs_2_, ...), custom_call_target="tpu_custom_call" | custom-call | flops 109999996928 | bytes 1000 | tf_op jit(solution)/shard_map/attend_back/pallas_call | solution.py:82
  168.7 6.2 %input_share.1.refs_3_.refs_4_ = bf16[1024,768]{1,0:T(8,128)(2,1)} custom-call(s32[4]{0:T(128)} %pad_add_fusion.refs_0_, bf16[1024,1152]{1,0:T(8,128)(2,1)} %get-tuple-element.131.refs_1_, bf16[384,1152]{1,0:T(8,128)(2,1)} %copy-done.36, bf16[384,1152]{1,0:T(8,128)(2,1)} %copy-done.37, bf16[384,768]{1,0:T(8,128)(2,1)} %get-tuple-element.136.refs_4_), custom_call_target="tpu_custom_call" | custom-call | flops 8800000000 | bytes 1000 | tf_op jit(solution)/shard_map/input_share/pallas_call | solution.py:82
  178.6 26.3 %attend_back.3 = (bf16[1024,1152]{1,0:T(8,128)(2,1)}, f32[1,1152]{1,0:T(1,128)}, bf16[384,1536]{1,0:T(8,128)(2,1)}, bf16[384,1536]{1,0:T(8,128)(2,1)}) custom-call(s32[4]{0:T(128)} %pad_add_fusion.refs_0_, s32[1]{0:T(128)} %dynamic_slice.54.refs_1_, bf16[1024,384]{1,0:T(8,128)(2,1)} %get-tuple-element.116.refs_2_, ...), custom_call_target="tpu_custom_call" | custom-call | flops 13200000000 | bytes 1000 | tf_op jit(solution)/shard_map/attend_back/pallas_call | solution.py:82
  206.0 2.6 collective-permute-start.18
  208.6 8.4 %input_grad.1 = (bf16[1024,768]{1,0:T(8,128)(2,1)}, f32[8,768]{1,0:T(8,128)}) custom-call(bf16[1024,768]{1,0:T(8,128)(2,1)} %refs_0_.1, f32[1024,768]{1,0:T(8,128)} %get-tuple-element.115.refs_1_, f32[1,7296]{1,0:T(1,128)} %reshape.75.refs_3_.refs_6_.refs_4_.refs_2_, bf16[1024,1152]{1,0:T(8,128)(2,1)} %get-tuple-element.134.refs_3_, ...), custom_call_target="tpu_custom_call" | custom-call | flops 8800000000 | bytes 1000 | tf_op jit(solution)/shard_map/input_grad/pallas_call | solution.py:82
  220.2 13.3 %reduce-scatter.2.cloned.1.call-done = bf16[192,768]{1,0:T(8,128)(2,1)} async-done(((bf16[3072,768]{1,0:T(8,128)(2,1)}), bf16[192,768]{1,0:T(8,128)(2,1)}) %reduce-scatter.2.cloned.1.call-update) | async-done | bytes 294928 | tf_op jit(solution)/shard_map/reduce_scatter | solution.py:1060
  234.2 6.9 %collective-permute-done.17.refs_1_ = bf16[192,768]{1,0:T(8,128)(2,1)S(1)} collective-permute-done((bf16[192,768]{1,0:T(8,128)(2,1)}, bf16[192,768]{1,0:T(8,128)(2,1)S(1)}, u32[]{:S(2)}, u32[]{:S(2)}) %collective-permute-start.17) | collective-permute-done | bytes 294944 | tf_op jit(solution)/shard_map/ppermute | solution.py:887
  244.4 14.9 %collective-permute-done.16.refs_2_ = bf16[192,1536]{1,0:T(8,128)(2,1)S(1)} collective-permute-done((bf16[192,1536]{1,0:T(8,128)(2,1)S(1)}, bf16[192,1536]{1,0:T(8,128)(2,1)S(1)}, u32[]{:S(2)}, u32[]{:S(2)}) %collective-permute-start.16) | collective-permute-done | bytes 589856 | tf_op jit(solution)/shard_map/ppermute | solution.py:884
  260.1 12.6 %collective-permute-done.19.refs_2_ = bf16[128,1536]{1,0:T(8,128)(2,1)S(1)} collective-permute-done((bf16[128,1536]{1,0:T(8,128)(2,1)S(1)}, bf16[128,1536]{1,0:T(8,128)(2,1)S(1)}, u32[]{:S(2)}, u32[]{:S(2)}) %collective-permute-start.19) | collective-permute-done | bytes 393248 | tf_op jit(solution)/shard_map/ppermute | solution.py:884
  274.5 36.1 %collective-permute-done.20.refs_2_ = bf16[128,1536]{1,0:T(8,128)(2,1)S(1)} collective-permute-done((bf16[128,1536]{1,0:T(8,128)(2,1)S(1)}, bf16[128,1536]{1,0:T(8,128)(2,1)S(1)}, u32[]{:S(2)}, u32[]{:S(2)}) %collective-permute-start.20) | collective-permute-done | bytes 393248 | tf_op jit(solution)/shard_map/ppermute | solution.py:884
  311.4 4.1 %collective-permute-done.21.refs_2_ = f32[8,1536]{1,0:T(8,128)S(1)} collective-permute-done((f32[8,1536]{1,0:T(8,128)S(1)}, f32[8,1536]{1,0:T(8,128)S(1)}, u32[]{:S(2)}, u32[]{:S(2)}) %collective-permute-start.21) | collective-permute-done | bytes 49184 | tf_op jit(solution)/shard_map/ppermute | solution.py:887
  316.0 4.4 %collective-permute-done.23.refs_2_ = bf16[96,1536]{1,0:T(8,128)(2,1)S(1)} collective-permute-done((bf16[96,1536]{1,0:T(8,128)(2,1)S(1)}, bf16[96,1536]{1,0:T(8,128)(2,1)S(1)}, u32[]{:S(2)}, u32[]{:S(2)}) %collective-permute-start.23) | collective-permute-done | bytes 294944 | tf_op jit(solution)/shard_map/ppermute | solution.py:884
  325.0 8.3 %wide_ffn.1 = (f32[1536,768]{1,0:T(8,128)}, f32[768,1536]{1,0:T(8,128)}) custom-call(s32[4]{0:T(128)} %pad_add_fusion.refs_0_, bf16[3072,768]{1,0:T(8,128)(2,1)} %all-gather.2.cloned.1.call-done.refs_1_.refs_2_, bf16[3072,768]{1,0:T(8,128)(2,1)} %all-gather.2.cloned.1.call-done.refs_1_.refs_2_, f32[8,1536]{1,0:T(8,128)} %copy-done.7), custom_call_target="tpu_custom_call" | custom-call | flops 11000000 | bytes 1000 | tf_op jit(solution)/shard_map/wide_ffn/pallas_call | solution.py:82
  333.4 2.5 collective-permute-done.25.refs_2_
  340.2 3.1 collective-permute-done.24
  345.4 4.7 %wide_qkv.1 = (f32[768,384]{1,0:T(8,128)}, f32[768,384]{1,0:T(8,128)}, f32[768,384]{1,0:T(8,128)}, f32[384,768]{1,0:T(8,128)}) custom-call(s32[4]{0:T(128)} %pad_add_fusion.refs_0_, bf16[384,1536]{1,0:T(8,128)(2,1)} %copy-done, bf16[384,1536]{1,0:T(8,128)(2,1)} %collective-permute-done.26.refs_2_), custom_call_target="tpu_custom_call" | custom-call | flops 11000000 | bytes 1000 | tf_op jit(solution)/shard_map/wide_qkv/pallas_call | solution.py:82
  (180 shorter events, 47.3 us)
Async XLA Ops:
  7.2 226.3 %reduce-scatter.2.cloned.1.call-start = ((), (), s32[]{:S(2)}) async-start(), calls=%async_computation.1 | async-start | bytes 5013504 | tf_op jit(solution)/shard_map/reduce_scatter | solution.py:1060
  10.9 24.1 %collective-permute-start.2 = (bf16[384,1152]{1,0:T(8,128)(2,1)}, bf16[384,1152]{1,0:T(8,128)(2,1)S(1)}, u32[]{:S(2)}, u32[]{:S(2)}) collective-permute-start(bf16[384,1152]{1,0:T(8,128)(2,1)} %cut_qkv.1), channel_id=1, source_target_pairs={{0,1},{1,0},{2,3},{3,2},{4,5},{5,4},{6,7},{7,6},{8,9},{9,8},{10,11... | collective-permute-start | bytes 2654216 | tf_op jit(solution)/shard_map/ppermute | solution.py:887
  36.3 21.5 %collective-permute-start = (bf16[320,768]{1,0:T(8,128)(2,1)}, bf16[320,768]{1,0:T(8,128)(2,1)}, u32[]{:S(2)}, u32[]{:S(2)}) collective-permute-start(bf16[320,768]{1,0:T(8,128)(2,1)} %get-tuple-element.93), channel_id=1, source_target_pairs={{0,1},{1,0},{2,3},{3,2},{4,5},{5,4},{6,7},{7,6},{8,9},{9,8},{10,11... | collective-permute-start | bytes 1474568 | tf_op jit(solution)/shard_map/ppermute | solution.py:887
  37.9 24.7 %collective-permute-start.1 = (bf16[384,768]{1,0:T(8,128)(2,1)S(1)}, bf16[384,768]{1,0:T(8,128)(2,1)S(1)}, u32[]{:S(2)}, u32[]{:S(2)}) collective-permute-start(bf16[384,768]{1,0:T(8,128)(2,1)S(1)} %copy-done.16), channel_id=1, source_target_pairs={{0,1},{1,0},{2,3},{3,2},{4,5},{5,4},{6,7},{7,6},{8,9},{9,8},{10,11... | collective-permute-start | bytes 1769480 | tf_op jit(solution)/shard_map/ppermute | solution.py:887
  62.6 31.7 %collective-permute-start.8 = (bf16[896,768]{1,0:T(8,128)(2,1)S(1)}, bf16[896,768]{1,0:T(8,128)(2,1)}, u32[]{:S(2)}, u32[]{:S(2)}) collective-permute-start(bf16[896,768]{1,0:T(8,128)(2,1)S(1)} %copy-done.34), channel_id=1, source_target_pairs={{0,1},{1,0},{2,3},{3,2},{4,5},{5,4},{6,7},{7,6},{8,9},{9,8},{10,11... | collective-permute-start | bytes 4128776 | tf_op jit(solution)/shard_map/ppermute | solution.py:887
  64.0 29.7 %collective-permute-start.6 = (bf16[320,768]{1,0:T(8,128)(2,1)}, bf16[320,768]{1,0:T(8,128)(2,1)S(1)}, u32[]{:S(2)}, u32[]{:S(2)}) collective-permute-start(bf16[320,768]{1,0:T(8,128)(2,1)} %collective-permute-done.refs_3_), channel_id=1, source_target_pairs={{0,4},{2,6},{4,0},{6,2},{8,12},{10,14},{12,8},{14,10},{16,20},{18,... | collective-permute-start | bytes 1474568 | tf_op jit(solution)/shard_map/ppermute | solution.py:884
  65.5 48.5 %collective-permute-start.5 = (bf16[320,768]{1,0:T(8,128)(2,1)}, bf16[320,768]{1,0:T(8,128)(2,1)S(1)}, u32[]{:S(2)}, u32[]{:S(2)}) collective-permute-start(bf16[320,768]{1,0:T(8,128)(2,1)} %collective-permute-done.refs_3_), channel_id=1, source_target_pairs={{0,2},{2,0},{4,6},{6,4},{8,10},{10,8},{12,14},{14,12},{16,18},{18,... | collective-permute-start | bytes 1474568 | tf_op jit(solution)/shard_map/ppermute | solution.py:884
  93.1 17.6 %collective-permute-start.10 = (bf16[1536,768]{1,0:T(8,128)(2,1)}, bf16[1536,768]{1,0:T(8,128)(2,1)S(1)}, u32[]{:S(2)}, u32[]{:S(2)}) collective-permute-start(bf16[1536,768]{1,0:T(8,128)(2,1)} %get-tuple-element.111), channel_id=1, source_target_pairs={{0,2},{2,0},{4,6},{6,4},{8,10},{10,8},{12,14},{14,12},{16,18},{18,... | collective-permute-start | bytes 7077896 | tf_op jit(solution)/shard_map/ppermute | solution.py:884
  93.7 20.3 %collective-permute-start.7 = (bf16[320,768]{1,0:T(8,128)(2,1)S(1)}, bf16[320,768]{1,0:T(8,128)(2,1)}, u32[]{:S(2)}, u32[]{:S(2)}) collective-permute-start(bf16[320,768]{1,0:T(8,128)(2,1)S(1)} %collective-permute-done.6.refs_4_), channel_id=1, source_target_pairs={{0,2},{2,0},{4,6},{6,4},{8,10},{10,8},{12,14},{14,12},{16,18},{18,... | collective-permute-start | bytes 1474568 | tf_op jit(solution)/shard_map/ppermute | solution.py:884
  94.3 19.7 %collective-permute-start.9 = (bf16[896,768]{1,0:T(8,128)(2,1)}, bf16[896,768]{1,0:T(8,128)(2,1)S(1)}, u32[]{:S(2)}, u32[]{:S(2)}) collective-permute-start(bf16[896,768]{1,0:T(8,128)(2,1)} %collective-permute-done.8.refs_5_), channel_id=1, source_target_pairs={{0,2},{2,0},{4,6},{6,4},{8,10},{10,8},{12,14},{14,12},{16,18},{18,... | collective-permute-start | bytes 4128776 | tf_op jit(solution)/shard_map/ppermute | solution.py:884
  112.7 51.9 %collective-permute-start.12 = (bf16[768,768]{1,0:T(8,128)(2,1)}, bf16[768,768]{1,0:T(8,128)(2,1)}, u32[]{:S(2)}, u32[]{:S(2)}) collective-permute-start(bf16[768,768]{1,0:T(8,128)(2,1)} %get-tuple-element.171), channel_id=1, source_target_pairs={{0,4},{2,6},{4,0},{6,2},{8,12},{10,14},{12,8},{14,10},{16,20},{18,... | collective-permute-start | bytes 3538952 | tf_op jit(solution)/shard_map/ppermute | solution.py:884
  138.1 186.9 %all-gather.2.cloned.1.call-start = ((), (), s32[]{:S(2)}) async-start(), calls=%async_computation.2 | async-start | bytes 5013504 | tf_op jit(solution)/shard_map/all_gather | solution.py:1088
  164.3 10.7 %collective-permute-start.11 = (bf16[384,1536]{1,0:T(8,128)(2,1)}, bf16[384,1536]{1,0:T(8,128)(2,1)S(1)}, u32[]{:S(2)}, u32[]{:S(2)}) collective-permute-start(bf16[384,1536]{1,0:T(8,128)(2,1)} %get-tuple-element.130), channel_id=1, source_target_pairs={{0,2},{2,0},{4,6},{6,4},{8,10},{10,8},{12,14},{14,12},{16,18},{18,... | collective-permute-start | bytes 3538952 | tf_op jit(solution)/shard_map/ppermute | solution.py:884
  167.1 37.9 %collective-permute-start.13 = (bf16[384,768]{1,0:T(8,128)(2,1)}, bf16[384,768]{1,0:T(8,128)(2,1)S(1)}, u32[]{:S(2)}, u32[]{:S(2)}) collective-permute-start(bf16[384,768]{1,0:T(8,128)(2,1)} %get-tuple-element.175), channel_id=1, source_target_pairs={{0,8},{2,10},{4,12},{6,14},{8,0},{10,2},{12,4},{14,6},{16,24},{18,... | collective-permute-start | bytes 1769480 | tf_op jit(solution)/shard_map/ppermute | solution.py:884
  177.2 39.7 %collective-permute-start.14 = (bf16[384,1536]{1,0:T(8,128)(2,1)S(1)}, bf16[384,1536]{1,0:T(8,128)(2,1)S(1)}, u32[]{:S(2)}, u32[]{:S(2)}) collective-permute-start(bf16[384,1536]{1,0:T(8,128)(2,1)S(1)} %fold_qkv_core.1.refs_12_), channel_id=1, source_target_pairs={{0,1},{1,0},{2,3},{3,2},{4,5},{5,4},{6,7},{7,6},{8,9},{9,8},{10,11... | collective-permute-start | bytes 3538952 | tf_op jit(solution)/shard_map/ppermute | solution.py:887
  204.9 13.6 %collective-permute-start.15 = (bf16[384,1536]{1,0:T(8,128)(2,1)}, bf16[384,1536]{1,0:T(8,128)(2,1)}, u32[]{:S(2)}, u32[]{:S(2)}) collective-permute-start(bf16[384,1536]{1,0:T(8,128)(2,1)} %get-tuple-element.141), channel_id=1, source_target_pairs={{0,2},{2,0},{4,6},{6,4},{8,10},{10,8},{12,14},{14,12},{16,18},{18,... | collective-permute-start | bytes 3538952 | tf_op jit(solution)/shard_map/ppermute | solution.py:884
  206.0 27.6 %collective-permute-start.18 = (bf16[192,768]{1,0:T(8,128)(2,1)}, bf16[192,768]{1,0:T(8,128)(2,1)S(1)}, u32[]{:S(2)}, u32[]{:S(2)}) collective-permute-start(bf16[192,768]{1,0:T(8,128)(2,1)} %get-tuple-element.177), channel_id=1, source_target_pairs={{0,16},{2,18},{4,20},{6,22},{8,24},{10,26},{12,28},{14,30},{16,0},... | collective-permute-start | bytes 884744 | tf_op jit(solution)/shard_map/ppermute | solution.py:884
  233.5 7.6 %collective-permute-start.17 = (bf16[192,768]{1,0:T(8,128)(2,1)}, bf16[192,768]{1,0:T(8,128)(2,1)S(1)}, u32[]{:S(2)}, u32[]{:S(2)}) collective-permute-start(bf16[192,768]{1,0:T(8,128)(2,1)} %reduce-scatter.2.cloned.1.call-done), channel_id=1, source_target_pairs={{0,1},{1,0},{2,3},{3,2},{4,5},{5,4},{6,7},{7,6},{8,9},{9,8},{10,11... | collective-permute-start | bytes 884744 | tf_op jit(solution)/shard_map/ppermute | solution.py:887
  242.5 16.8 %collective-permute-start.16 = (bf16[192,1536]{1,0:T(8,128)(2,1)S(1)}, bf16[192,1536]{1,0:T(8,128)(2,1)S(1)}, u32[]{:S(2)}, u32[]{:S(2)}) collective-permute-start(bf16[192,1536]{1,0:T(8,128)(2,1)S(1)} %get-tuple-element.173), channel_id=1, source_target_pairs={{0,4},{2,6},{4,0},{6,2},{8,12},{10,14},{12,8},{14,10},{16,20},{18,... | collective-permute-start | bytes 1769480 | tf_op jit(solution)/shard_map/ppermute | solution.py:884
  260.1 12.6 %collective-permute-start.19 = (bf16[128,1536]{1,0:T(8,128)(2,1)S(1)}, bf16[128,1536]{1,0:T(8,128)(2,1)S(1)}, u32[]{:S(2)}, u32[]{:S(2)}) collective-permute-start(bf16[128,1536]{1,0:T(8,128)(2,1)S(1)} %get-tuple-element.153), channel_id=1, source_target_pairs={{0,8},{2,10},{4,12},{6,14},{8,0},{10,2},{12,4},{14,6},{16,24},{18,... | collective-permute-start | bytes 1179656 | tf_op jit(solution)/shard_map/ppermute | solution.py:884
  273.3 37.3 %collective-permute-start.20 = (bf16[128,1536]{1,0:T(8,128)(2,1)S(1)}, bf16[128,1536]{1,0:T(8,128)(2,1)S(1)}, u32[]{:S(2)}, u32[]{:S(2)}) collective-permute-start(bf16[128,1536]{1,0:T(8,128)(2,1)S(1)} %get-tuple-element.156), channel_id=1, source_target_pairs={{0,16},{2,18},{4,20},{6,22},{8,24},{10,26},{12,28},{14,30},{16,0},... | collective-permute-start | bytes 1179656 | tf_op jit(solution)/shard_map/ppermute | solution.py:884
  311.3 9.2 %collective-permute-start.23 = (bf16[96,1536]{1,0:T(8,128)(2,1)S(1)}, bf16[96,1536]{1,0:T(8,128)(2,1)S(1)}, u32[]{:S(2)}, u32[]{:S(2)}) collective-permute-start(bf16[96,1536]{1,0:T(8,128)(2,1)S(1)} %get-tuple-element.159.refs_3_.refs_1_), channel_id=1, source_target_pairs={{0,8},{2,10},{4,12},{6,14},{8,0},{10,2},{12,4},{14,6},{16,24},{18,... | collective-permute-start | bytes 884744 | tf_op jit(solution)/shard_map/ppermute | solution.py:884
  321.2 14.7 %collective-permute-start.25 = (bf16[192,1536]{1,0:T(8,128)(2,1)S(1)}, bf16[192,1536]{1,0:T(8,128)(2,1)S(1)}, u32[]{:S(2)}, u32[]{:S(2)}) collective-permute-start(bf16[192,1536]{1,0:T(8,128)(2,1)S(1)} %join.2.refs_3_.refs_1_), channel_id=1, source_target_pairs={{0,4},{2,6},{4,0},{6,2},{8,12},{10,14},{12,8},{14,10},{16,20},{18,... | collective-permute-start | bytes 1769480 | tf_op jit(solution)/shard_map/ppermute | solution.py:884
  339.1 6.3 %collective-permute-start.26 = (bf16[384,1536]{1,0:T(8,128)(2,1)S(1)}, bf16[384,1536]{1,0:T(8,128)(2,1)}, u32[]{:S(2)}, u32[]{:S(2)}) collective-permute-start(bf16[384,1536]{1,0:T(8,128)(2,1)S(1)} %join.3.refs_1_), channel_id=1, source_target_pairs={{0,2},{2,0},{4,6},{6,4},{8,10},{10,8},{12,14},{14,12},{16,18},{18,... | collective-permute-start | bytes 3538952 | tf_op jit(solution)/shard_map/ppermute | solution.py:884
  (47 other events, 340.5 us)
Sparse Core Ops, SparseCore 0:
  138.3 95.1 reduce-scatter.1
  242.6 70.8 all-gather.1

commit v3 on v2

--- a/solution.py
+++ b/solution.py
@@ -308,7 +308,7 @@
 
 
 def heads_other_kernel(
-    bits_ref, len_ref, n_ref, wm_ref, wf_ref, b_ref, cos_ref, sin_ref, q_h, k_h, v_h, ctx_h, aug_h,
+    at, bits_ref, len_ref, n_ref, wm_ref, wf_ref, b_ref, cos_ref, sin_ref, q_h, k_h, v_h, ctx_h, aug_h,
     q_s, k_s, v_s, ctx_s, aug_s, sem,
 ):
     rows = n_ref.shape[0]
@@ -319,7 +319,7 @@
     for i in range(rows // blk):
         sl = slice(i * blk, (i + 1) * blk)
         pre = dot(n_ref[sl, block(c, half)], wm_ref[...]) + dot(n_ref[sl, block(1 - c, half)], wf_ref[...])
-        pre = pre + b_ref[:, : 3 * width]
+        pre = pre + b_ref[:, at.qkv]
         put_qkv(
             [pre[:, j * width : (j + 1) * width] for j in range(3)], cos_ref[sl, :], sin_ref[sl, :],
             *(ref.at[sl, :] for ref in (q_s, k_s, v_s)),
@@ -331,12 +331,12 @@
         store.wait()
 
 
-def heads_other(bits, length, n, w_mine, w_far, bias, cos, sin, after=()):
+def heads_other(at, bits, length, n, w_mine, w_far, bias, cos, sin, after=()):
     rows = n.shape[0]
     width = w_mine.shape[1] // 3
     outs = [(rows, width)] * 5
     return call(
-        heads_other_kernel,
+        lambda *refs: heads_other_kernel(at, *refs),
         after,
         prefetch=2,
         in_specs=[whole(a.shape) for a in (n, w_mine, w_far, bias, cos, sin)],
@@ -814,37 +814,37 @@
     )(x, gm, vec, g, share, wq, wk, wv)
 
 
-def wide_qkv(bits, mine, other, after=()):
-    half, width = mine.shape
+def wide_qkv(bits, near, far, after=()):
+    size, width = near[0].shape
     width //= 4
 
-    def kernel(bits_ref, m_ref, o_ref, *outs):
-        c = bits_ref[0]
-
-        def put(ref):
-            for i, out in enumerate(outs[:3]):
-                for p in range(width // 128):
-                    out[:, p * 128 : (p + 1) * 128] = ref[:, (3 * p + i) * 128 : (3 * p + i + 1) * 128].astype(F32)
-            outs[3][...] = ref[:, 3 * width :].astype(F32).T
-
-        own = pl.program_id(0) == c
-
-        @pl.when(own)
-        def _():
-            put(m_ref)
-
-        @pl.when(jnp.logical_not(own))
-        def _():
-            put(o_ref)
+    def kernel(bits_ref, *refs):
+        ins, outs, turn = refs[:4], refs[4:8], refs[8]
+        base = (pl.program_id(0) != bits_ref[0]).astype(jnp.int32) * 2
+        for half in range(2):
+            want = base + (half != bits_ref[1]).astype(jnp.int32)
+            rows = slice(half * size, (half + 1) * size)
+            for k in range(4):
+
+                @pl.when(want == k)
+                def _():
+                    ref = ins[k]
+                    for i, out in enumerate(outs[:3]):
+                        for p in range(width // 128):
+                            src = slice((3 * p + i) * 128, (3 * p + i + 1) * 128)
+                            out[rows, p * 128 : (p + 1) * 128] = ref[:, src].astype(F32)
+                    turn[rows, :] = ref[:, 3 * width :].astype(F32)
+
+        outs[3][...] = turn[...].T
 
     return call(
         kernel, after, prefetch=1, grid=(2,),
-        in_specs=[whole(mine.shape)] * 2,
-        out_specs=[pl.BlockSpec((half, width), lambda i, *_: (i, 0))] * 3
-        + [pl.BlockSpec((width, half), lambda i, *_: (0, i))],
-        out_shape=[struct((2 * half, width), F32)] * 3 + [struct((width, 2 * half), F32)],
-        estimate=EST["move"], name="wide_qkv", mib=56,
-    )(bits, mine, other)
+        in_specs=[whole((size, 4 * width))] * 4,
+        out_specs=[pl.BlockSpec((2 * size, width), lambda i, *_: (i, 0))] * 3
+        + [pl.BlockSpec((width, 2 * size), lambda i, *_: (0, i))],
+        out_shape=[struct((4 * size, width), F32)] * 3 + [struct((width, 4 * size), F32)],
+        scratch=[pltpu.VMEM((2 * size, width), F32)], estimate=EST["move"], name="wide_qkv", mib=56,
+    )(bits, *near, *far)
 
 
 def wide_ffn(bits, stack, after=()):
@@ -854,23 +854,24 @@
     count = 1 << (n - 2)
     size = part // count
 
-    def kernel(bits_ref, d_ref, u_ref, down_ref, up_ref):
-        down_ref[...] = d_ref[...].astype(F32)
-        up_ref[...] = u_ref[...].astype(F32)
-
-    def place(x):
-        return lambda t, *_: (sub_block(lax.rem(t, count), t // count, x, n), 0)
+    def kernel(bits_ref, *refs):
+        for x in range(2):
+            for k in range(2):
+                refs[4 + x][k * size : (k + 1) * size, :] = refs[2 * x + k][...].astype(F32)
+
+    def place(x, k):
+        return lambda q, t, *_: (sub_block(2 * t + k, q, x, n), 0)
 
     return call(
-        kernel, after, prefetch=1, grid=(2 * count,),
-        in_specs=[pl.BlockSpec((size, d), place(0)), pl.BlockSpec((size, d), place(1))],
+        kernel, after, prefetch=1, grid=(2, count // 2),
+        in_specs=[pl.BlockSpec((size, d), place(x, k)) for x in range(2) for k in range(2)],
         out_specs=[
-            pl.BlockSpec((size, d), lambda t, *_: (t, 0)),
-            pl.BlockSpec((size, d), lambda t, *_: (lax.rem(t, count), t // count)),
+            pl.BlockSpec((2 * size, d), lambda q, t, *_: (q * (count // 2) + t, 0)),
+            pl.BlockSpec((2 * size, d), lambda q, t, *_: (t, q)),
         ],
         out_shape=[struct((2 * part, d), F32), struct((part, 2 * d), F32)],
         estimate=EST["move"], name="wide_ffn", mib=56,
-    )(bits, stack, stack)
+    )(bits, stack, stack, stack, stack)
 
 
 class Links:
@@ -1028,11 +1029,11 @@
         at, cut_moves, [(near_rows, d), (d + part - 2 * near_rows, d)], bits, length, inputs, vec, query_weight,
         key_weight, value_weight, cos, sin, up_weight, down_weight,
     )
-    bias_x = links.across(vec[:, at.qkv.start :])
+    bias_x = links.across(vec)
     near, out_x = links.across(near), links.across(out_weight)
     qkv_mine, _ = lax.optimization_barrier((qkv_mine, ctx_own))
     qkv_far = links.swap(qkv_mine, 0)
-    *other, ctx_x, aug_x = heads_other(bits, length, normed, qkv_mine, qkv_far, bias_x, cos, sin, after=(ctx_own,))
+    *other, ctx_x, aug_x = heads_other(at, bits, length, normed, qkv_mine, qkv_far, bias_x, cos, sin, after=(ctx_own,))
     near, out_x, rest, ctx_x = lax.optimization_barrier((near, out_x, rest, ctx_x))
     rest = links.across(rest)
     near_x = links.swap(near, 1)
@@ -1084,7 +1085,7 @@
         own_sum.advance((q_k,))
     size = stack.shape[0]
     parts = [(stack_r, 0, 0, size), (own_sum.keep, 0, 0, size)]
-    stack, = fold(bits, parts, size, [(0, size)], "fold_stack", after=(own_sum.keep,))
+    stack, = fold(bits, parts, size, [(0, size)], "fold_stack", after=(own_sum.keep, q_r))
     gathered = lax.all_gather(stack, "dp", axis=0, tiled=True)
     if dp_size > blocks:
         gathered = turned(gathered, dp_size // blocks, blocks)
@@ -1111,25 +1112,20 @@
         after = ()
         parts = [keep, links.swap(send, bit)]
     _, q, small = ride(bits, parts, small, None, True)
-    small_r = links.across(small)
-    others = [0, 1]
-    for bit in reversed(range(1, last)):
+    for bit in reversed(range(2, last)):
         q_r = links.swap(q, bit)
-        after = ()
-        if others:
+        if bit == last - 1:
             size = small.shape[0]
-            small, = fold(bits, [(small, 0, 0, size), (small_r, 0, 0, size)], size, [(0, size)], "fold_small", after=(q,))
-            small_r = links.swap(small, others.pop(0))
-            after = (small,)
-        if bit == 1:
-            grad_down, grad_up = wide_ffn(bits, gathered, after=after)
-            after = (grad_up,)
-        q = links.join(q, q_r, bit, after=after)
+            for swap in (links.across, lambda v: links.swap(v, 0), lambda v: links.swap(v, 1)):
+                parts = [(small, 0, 0, size), (swap(small), 0, 0, size)]
+                small, = fold(bits, parts, size, [(0, size)], "fold_small", after=(q,))
+        q = links.join(q, q_r, bit, after=(small,))
+    q_r = links.swap(q, 1)
     q_far = links.swap(q, 0)
-    small = small + small_r
-    for bit in others:
-        small = small + links.swap(small, bit)
-    grad_q, grad_k, grad_v, grad_out = wide_qkv(bits, q, q_far)
+    grad_down, grad_up = wide_ffn(bits, gathered, after=(q,))
+    q_r, grad_up = lax.optimization_barrier((q_r, grad_up))
+    q_r_far = links.swap(q_r, 0)
+    grad_q, grad_k, grad_v, grad_out = wide_qkv(bits, (q, q_r), (q_far, q_r_far), after=(grad_up,))
 
     small = small.reshape(-1)
     gain1, shift1, out_b, gain2, shift2, down_b = (small[i * d : (i + 1) * d] for i in range(6))

time: 361 us -> 334 us (0.925)
  waiting for transfers between devices: 106 us -> 78.2 us
    reduce_scatter x1, waiting for transfers between devices: 13.3 us -> 1.49 us  [layer(): stack = lax.psum_scatter(stack, 'dp', scatter_dimension=0, tiled=True)]
    ppermute x19 -> x20, waiting for transfers between devices: 74.9 us -> 64 us  [swap(): lax.ppermute(value, 'dp', [(i, i ^ 1 << at) for i in range(self.size)])]
    ppermute x8, waiting for transfers between devices: 17.6 us -> 10.1 us  [across(): return lax.ppermute(value, 'tensor', [(0, 1), (1, 0)])]
    ppermute x19 -> x20, starting transfers between devices: 12.8 us -> 14.3 us  [swap(): lax.ppermute(value, 'dp', [(i, i ^ 1 << at) for i in range(self.size)])]
  transfers between devices with their start and end apart: 29 -> 30, of which waited for: 13 -> 13; matrix products, arithmetic and copies ran while one was open for 3% -> 3% of each run, Pallas kernels for 52% -> 56%
where the time goes in v3:
time: 334 us; the launch traced here: 329 us
  Pallas kernels  193 us (58%)
  waiting for transfers between devices  78.2 us (23%)
  starting transfers between devices  24.6 us (7%)
  between operations  15.1 us (5%)
  local copies, waits for them, and re-layouts  10.2 us (3%)
  other arithmetic  7.73 us (2%)
    pallas_call x23, Pallas kernels, call(): return lambda *args: run(*args, *after)  193 us
    ppermute x20, waiting for transfers between devices, swap(): lax.ppermute(value, 'dp', [(i, i ^ 1 << at) for i in range(self.size)])  64 us
    ppermute x20, starting transfers between devices, swap(): lax.ppermute(value, 'dp', [(i, i ^ 1 << at) for i in range(self.size)])  14.3 us
    ppermute x8, starting transfers between devices, across(): return lax.ppermute(value, 'tensor', [(0, 1), (1, 0)])  10.2 us
    ppermute x8, waiting for transfers between devices, across(): return lax.ppermute(value, 'tensor', [(0, 1), (1, 0)])  10.1 us
    convert_element_type x4, other arithmetic, half(): return (a + b).astype(BF)  7.05 us
  transfers between devices with their start and end apart: 30, of which 13 were waited for; matrix products, arithmetic and copies ran while one was open for 3% of the time, Pallas kernels for 56%

profile of v3, /device:TPU:0, one launch (start us, length us, event | category | flops | bytes accessed | tf_op | source)
XLA Modules:
  0.0 329.3 jit_solution(450631804852491093)
XLA Ops:
  7.9 2.9 cut_qkv.1
  10.8 3.0 collective-permute-start.2
  15.3 19.6 %heads_own.1 = (bf16[1024,768]{1,0:T(8,128)(2,1)}, bf16[768,1024]{1,0:T(8,128)(2,1)}, bf16[1024,384]{1,0:T(8,128)(2,1)}, bf16[1024,384]{1,0:T(8,128)(2,1)}, bf16...) custom-call(s32[4]{0:T(128)} %pad_add_fusion.refs_0_, ...), custom_call_target="tpu_custom_call" | custom-call | flops 17600000000 | bytes 1000 | tf_op jit(solution)/shard_map/heads_own/pallas_call | solution.py:82
  40.2 17.4 %heads_other.1 = (bf16[1024,384]{1,0:T(8,128)(2,1)}, bf16[1024,384]{1,0:T(8,128)(2,1)}, bf16[1024,384]{1,0:T(8,128)(2,1)}, bf16[1024,384]{1,0:T(8,128)(2,1)}, bf16[1024,384]{1,0:T(8,128)(2,1)}) custom-call(s32[4]{0:T(128)} %pad_add_fusion.refs_0_, s32[1]{0:T(128)} %dynamic_slice.54.refs_1_, bf16[1024,768]{1,0:T(8,128)(2,1)} %get-tuple-element.97.refs_2_, ...), custom_call_target="tpu_custom_call" | custom-call | flops 109999996928 | bytes 1000 | tf_op jit(solution)/shard_map/heads_other/pallas_call | solution.py:82
  57.6 4.4 %collective-permute-done.1.refs_5_.refs_18_ = bf16[384,768]{1,0:T(8,128)(2,1)S(1)} collective-permute-done((bf16[384,768]{1,0:T(8,128)(2,1)S(1)}, bf16[384,768]{1,0:T(8,128)(2,1)S(1)}, u32[]{:S(2)}, u32[]{:S(2)}) %collective-permute-start.1) | collective-permute-done | bytes 589856 | tf_op jit(solution)/shard_map/ppermute | solution.py:888
  64.7 27.6 %ffn_own.1 = (f32[1024,768]{1,0:T(8,128)}, bf16[1024,768]{1,0:T(8,128)(2,1)}, bf16[768,1024]{1,0:T(8,128)(2,1)}, bf16[1024,768]{1,0:T(8,128)(2,1)}, bf16[1024,76...) custom-call(s32[4]{0:T(128)} %pad_add_fusion.refs_0_, ...), custom_call_target="tpu_custom_call" | custom-call | flops 11000000 | bytes 1000 | tf_op jit(solution)/shard_map/ffn_own/pallas_call | solution.py:82
  93.8 16.2 %ffn_mine.1 = (bf16[1024,768]{1,0:T(8,128)(2,1)}, bf16[1024,768]{1,0:T(8,128)(2,1)}, bf16[3072,768]{1,0:T(8,128)(2,1)}, f32[1,768]{1,0:T(1,128)}) custom-call(s32[4]{0:T(128)} %pad_add_fusion.refs_0_, bf16[1024,768]{1,0:T(8,128)(2,1)} %get-tuple-element.102.refs_1_.refs_2_, f32[1,7296]{1,0:T(1,128)} %copy-done.40, ...), custom_call_target="tpu_custom_call" | custom-call | flops 109999996928 | bytes 1000 | tf_op jit(solution)/shard_map/ffn_mine/pallas_call | solution.py:82
  114.9 22.9 %ffn_far.1 = (bf16[1024,768]{1,0:T(8,128)(2,1)}, f32[1024,768]{1,0:T(8,128)}, bf16[1024,384]{1,0:T(8,128)(2,1)}, bf16[1024,384]{1,0:T(8,128)(2,1)}, bf16[3072,76...) custom-call(s32[4]{0:T(128)} %pad_add_fusion.refs_0_, ...), custom_call_target="tpu_custom_call", output_to_operand_aliasing={{4}: (19, {})} | custom-call | flops 109999996928 | bytes 1000 | tf_op jit(solution)/shard_map/ffn_far/pallas_call | solution.py:82
  137.8 26.1 %attend_back.2 = (bf16[1024,1152]{1,0:T(8,128)(2,1)}, f32[1,1152]{1,0:T(1,128)}, bf16[384,1536]{1,0:T(8,128)(2,1)}, bf16[384,1536]{1,0:T(8,128)(2,1)}) custom-call(s32[4]{0:T(128)} %pad_add_fusion.refs_0_, s32[1]{0:T(128)} %dynamic_slice.54.refs_1_, bf16[1024,384]{1,0:T(8,128)(2,1)} %get-tuple-element.125.refs_2_, ...), custom_call_target="tpu_custom_call" | custom-call | flops 109999996928 | bytes 1000 | tf_op jit(solution)/shard_map/attend_back/pallas_call | solution.py:82
  164.3 2.5 add_convert_fusion.4
  168.4 6.3 %input_share.1.refs_3_.refs_4_ = bf16[1024,768]{1,0:T(8,128)(2,1)} custom-call(s32[4]{0:T(128)} %pad_add_fusion.refs_0_, bf16[1024,1152]{1,0:T(8,128)(2,1)} %get-tuple-element.133.refs_1_, bf16[384,1152]{1,0:T(8,128)(2,1)} %copy-done.36, bf16[384,1152]{1,0:T(8,128)(2,1)} %copy-done.37, bf16[384,768]{1,0:T(8,128)(2,1)} %get-tuple-element.138.refs_4_), custom_call_target="tpu_custom_call" | custom-call | flops 8800000000 | bytes 1000 | tf_op jit(solution)/shard_map/input_share/pallas_call | solution.py:82
  177.9 26.3 %attend_back.3 = (bf16[1024,1152]{1,0:T(8,128)(2,1)}, f32[1,1152]{1,0:T(1,128)}, bf16[384,1536]{1,0:T(8,128)(2,1)}, bf16[384,1536]{1,0:T(8,128)(2,1)}) custom-call(s32[4]{0:T(128)} %pad_add_fusion.refs_0_, s32[1]{0:T(128)} %dynamic_slice.54.refs_1_, bf16[1024,384]{1,0:T(8,128)(2,1)} %get-tuple-element.118.refs_2_, ...), custom_call_target="tpu_custom_call" | custom-call | flops 13200000000 | bytes 1000 | tf_op jit(solution)/shard_map/attend_back/pallas_call | solution.py:82
  205.3 8.6 %input_grad.1 = (bf16[1024,768]{1,0:T(8,128)(2,1)}, f32[8,768]{1,0:T(8,128)}) custom-call(bf16[1024,768]{1,0:T(8,128)(2,1)} %refs_0_.1, f32[1024,768]{1,0:T(8,128)} %get-tuple-element.117.refs_1_, f32[1,7296]{1,0:T(1,128)} %reshape.75.refs_3_.refs_6_.refs_4_.refs_2_, bf16[1024,1152]{1,0:T(8,128)(2,1)} %get-tuple-element.136.refs_3_, ...), custom_call_target="tpu_custom_call" | custom-call | flops 8800000000 | bytes 1000 | tf_op jit(solution)/shard_map/input_grad/pallas_call | solution.py:82
  217.5 2.6 collective-permute-start.18
  223.0 11.1 %collective-permute-done.18.refs_2_ = bf16[192,768]{1,0:T(8,128)(2,1)S(1)} collective-permute-done((bf16[192,768]{1,0:T(8,128)(2,1)}, bf16[192,768]{1,0:T(8,128)(2,1)S(1)}, u32[]{:S(2)}, u32[]{:S(2)}) %collective-permute-start.18) | collective-permute-done | bytes 294944 | tf_op jit(solution)/shard_map/ppermute | solution.py:885
  238.2 14.7 %collective-permute-done.19.refs_2_ = bf16[128,1536]{1,0:T(8,128)(2,1)S(1)} collective-permute-done((bf16[128,1536]{1,0:T(8,128)(2,1)S(1)}, bf16[128,1536]{1,0:T(8,128)(2,1)S(1)}, u32[]{:S(2)}, u32[]{:S(2)}) %collective-permute-start.19) | collective-permute-done | bytes 393248 | tf_op jit(solution)/shard_map/ppermute | solution.py:885
  255.7 20.0 %collective-permute-done.20.refs_2_ = bf16[128,1536]{1,0:T(8,128)(2,1)S(1)} collective-permute-done((bf16[128,1536]{1,0:T(8,128)(2,1)S(1)}, bf16[128,1536]{1,0:T(8,128)(2,1)S(1)}, u32[]{:S(2)}, u32[]{:S(2)}) %collective-permute-start.20) | collective-permute-done | bytes 393248 | tf_op jit(solution)/shard_map/ppermute | solution.py:885
  277.4 3.1 collective-permute-done.21.refs_2_
  284.5 3.9 %collective-permute-done.23.refs_2_ = f32[8,1536]{1,0:T(8,128)S(1)} collective-permute-done((f32[8,1536]{1,0:T(8,128)S(1)}, f32[8,1536]{1,0:T(8,128)S(1)}, u32[]{:S(2)}, u32[]{:S(2)}) %collective-permute-start.23) | collective-permute-done | bytes 49184 | tf_op jit(solution)/shard_map/ppermute | solution.py:885
  289.0 10.1 %collective-permute-done.24.refs_2_ = bf16[96,1536]{1,0:T(8,128)(2,1)S(1)} collective-permute-done((bf16[96,1536]{1,0:T(8,128)(2,1)S(1)}, bf16[96,1536]{1,0:T(8,128)(2,1)S(1)}, u32[]{:S(2)}, u32[]{:S(2)}) %collective-permute-start.24) | collective-permute-done | bytes 294944 | tf_op jit(solution)/shard_map/ppermute | solution.py:885
  301.3 2.5 all-gather.2.cloned.1.call-done.refs_1_.refs_2_.refs_3_.refs_4_
  303.9 7.0 %wide_ffn.1 = (f32[1536,768]{1,0:T(8,128)}, f32[768,1536]{1,0:T(8,128)}) custom-call(s32[4]{0:T(128)} %pad_add_fusion.refs_0_, bf16[3072,768]{1,0:T(8,128)(2,1)} %all-gather.2.cloned.1.call-done.refs_1_.refs_2_.refs_3_.refs_4_, bf16[3072,768]{1,0:T(8,128)(2,1)} %all-gather.2.cloned.1.call-done.refs_1_.refs_2_.refs_3_.refs_4_, ...), custom_call_target="tpu_custom_call" | custom-call | flops 11000000 | bytes 1000 | tf_op jit(solution)/shard_map/wide_ffn/pallas_call | solution.py:82
  310.9 3.0 collective-permute-done.25.refs_2_
  317.6 4.7 %wide_qkv.1 = (f32[768,384]{1,0:T(8,128)}, f32[768,384]{1,0:T(8,128)}, f32[768,384]{1,0:T(8,128)}, f32[384,768]{1,0:T(8,128)}) custom-call(s32[4]{0:T(128)} %pad_add_fusion.refs_0_, bf16[192,1536]{1,0:T(8,128)(2,1)} %copy-done, bf16[192,1536]{1,0:T(8,128)(2,1)} %copy-done.14, bf16[192,1536]{1,0:T(8,128)(2,1)} %copy-done.15, bf16[192,1536]{1,0:T(8,128)(2,1)} %copy-done.16, ...), custom_call_target="tpu_custom_call" | custom-call | flops 11000000 | bytes 1000 | tf_op jit(solution)/shard_map/wide_qkv/pallas_call | solution.py:82
  (180 shorter events, 47.6 us)
Async XLA Ops:
  7.3 214.3 %reduce-scatter.2.cloned.1.call-start = ((), (), s32[]{:S(2)}) async-start(), calls=%async_computation.1 | async-start | bytes 5013504 | tf_op jit(solution)/shard_map/reduce_scatter | solution.py:1061
  10.8 24.1 %collective-permute-start.2 = (bf16[384,1152]{1,0:T(8,128)(2,1)}, bf16[384,1152]{1,0:T(8,128)(2,1)S(1)}, u32[]{:S(2)}, u32[]{:S(2)}) collective-permute-start(bf16[384,1152]{1,0:T(8,128)(2,1)} %cut_qkv.1), channel_id=1, source_target_pairs={{0,1},{1,0},{2,3},{3,2},{4,5},{5,4},{6,7},{7,6},{8,9},{9,8},{10,11... | collective-permute-start | bytes 2654216 | tf_op jit(solution)/shard_map/ppermute | solution.py:888
  35.5 22.0 %collective-permute-start = (bf16[320,768]{1,0:T(8,128)(2,1)}, bf16[320,768]{1,0:T(8,128)(2,1)}, u32[]{:S(2)}, u32[]{:S(2)}) collective-permute-start(bf16[320,768]{1,0:T(8,128)(2,1)} %get-tuple-element.95), channel_id=1, source_target_pairs={{0,1},{1,0},{2,3},{3,2},{4,5},{5,4},{6,7},{7,6},{8,9},{9,8},{10,11... | collective-permute-start | bytes 1474568 | tf_op jit(solution)/shard_map/ppermute | solution.py:888
  37.1 24.9 %collective-permute-start.1 = (bf16[384,768]{1,0:T(8,128)(2,1)S(1)}, bf16[384,768]{1,0:T(8,128)(2,1)S(1)}, u32[]{:S(2)}, u32[]{:S(2)}) collective-permute-start(bf16[384,768]{1,0:T(8,128)(2,1)S(1)} %copy-done.12), channel_id=1, source_target_pairs={{0,1},{1,0},{2,3},{3,2},{4,5},{5,4},{6,7},{7,6},{8,9},{9,8},{10,11... | collective-permute-start | bytes 1769480 | tf_op jit(solution)/shard_map/ppermute | solution.py:888
  62.0 31.8 %collective-permute-start.8 = (bf16[896,768]{1,0:T(8,128)(2,1)S(1)}, bf16[896,768]{1,0:T(8,128)(2,1)}, u32[]{:S(2)}, u32[]{:S(2)}) collective-permute-start(bf16[896,768]{1,0:T(8,128)(2,1)S(1)} %copy-done.34), channel_id=1, source_target_pairs={{0,1},{1,0},{2,3},{3,2},{4,5},{5,4},{6,7},{7,6},{8,9},{9,8},{10,11... | collective-permute-start | bytes 4128776 | tf_op jit(solution)/shard_map/ppermute | solution.py:888
  63.2 29.7 %collective-permute-start.6 = (bf16[320,768]{1,0:T(8,128)(2,1)}, bf16[320,768]{1,0:T(8,128)(2,1)S(1)}, u32[]{:S(2)}, u32[]{:S(2)}) collective-permute-start(bf16[320,768]{1,0:T(8,128)(2,1)} %collective-permute-done.refs_3_), channel_id=1, source_target_pairs={{0,4},{2,6},{4,0},{6,2},{8,12},{10,14},{12,8},{14,10},{16,20},{18,... | collective-permute-start | bytes 1474568 | tf_op jit(solution)/shard_map/ppermute | solution.py:885
  64.7 48.9 %collective-permute-start.5 = (bf16[320,768]{1,0:T(8,128)(2,1)}, bf16[320,768]{1,0:T(8,128)(2,1)S(1)}, u32[]{:S(2)}, u32[]{:S(2)}) collective-permute-start(bf16[320,768]{1,0:T(8,128)(2,1)} %collective-permute-done.refs_3_), channel_id=1, source_target_pairs={{0,2},{2,0},{4,6},{6,4},{8,10},{10,8},{12,14},{14,12},{16,18},{18,... | collective-permute-start | bytes 1474568 | tf_op jit(solution)/shard_map/ppermute | solution.py:885
  92.3 17.8 %collective-permute-start.10 = (bf16[1536,768]{1,0:T(8,128)(2,1)}, bf16[1536,768]{1,0:T(8,128)(2,1)S(1)}, u32[]{:S(2)}, u32[]{:S(2)}) collective-permute-start(bf16[1536,768]{1,0:T(8,128)(2,1)} %get-tuple-element.113), channel_id=1, source_target_pairs={{0,2},{2,0},{4,6},{6,4},{8,10},{10,8},{12,14},{14,12},{16,18},{18,... | collective-permute-start | bytes 7077896 | tf_op jit(solution)/shard_map/ppermute | solution.py:885
  92.9 20.7 %collective-permute-start.7 = (bf16[320,768]{1,0:T(8,128)(2,1)S(1)}, bf16[320,768]{1,0:T(8,128)(2,1)}, u32[]{:S(2)}, u32[]{:S(2)}) collective-permute-start(bf16[320,768]{1,0:T(8,128)(2,1)S(1)} %collective-permute-done.6.refs_4_), channel_id=1, source_target_pairs={{0,2},{2,0},{4,6},{6,4},{8,10},{10,8},{12,14},{14,12},{16,18},{18,... | collective-permute-start | bytes 1474568 | tf_op jit(solution)/shard_map/ppermute | solution.py:885
  93.8 19.8 %collective-permute-start.9 = (bf16[896,768]{1,0:T(8,128)(2,1)}, bf16[896,768]{1,0:T(8,128)(2,1)S(1)}, u32[]{:S(2)}, u32[]{:S(2)}) collective-permute-start(bf16[896,768]{1,0:T(8,128)(2,1)} %collective-permute-done.8.refs_5_), channel_id=1, source_target_pairs={{0,2},{2,0},{4,6},{6,4},{8,10},{10,8},{12,14},{14,12},{16,18},{18,... | collective-permute-start | bytes 4128776 | tf_op jit(solution)/shard_map/ppermute | solution.py:885
  112.1 52.2 %collective-permute-start.12 = (bf16[768,768]{1,0:T(8,128)(2,1)}, bf16[768,768]{1,0:T(8,128)(2,1)}, u32[]{:S(2)}, u32[]{:S(2)}) collective-permute-start(bf16[768,768]{1,0:T(8,128)(2,1)} %get-tuple-element.175), channel_id=1, source_target_pairs={{0,4},{2,6},{4,0},{6,2},{8,12},{10,14},{12,8},{14,10},{16,20},{18,... | collective-permute-start | bytes 3538952 | tf_op jit(solution)/shard_map/ppermute | solution.py:885
  137.8 166.1 %all-gather.2.cloned.1.call-start = ((), (), s32[]{:S(2)}) async-start(), calls=%async_computation.2 | async-start | bytes 5013504 | tf_op jit(solution)/shard_map/all_gather | solution.py:1089
  164.0 10.7 %collective-permute-start.11 = (bf16[384,1536]{1,0:T(8,128)(2,1)}, bf16[384,1536]{1,0:T(8,128)(2,1)S(1)}, u32[]{:S(2)}, u32[]{:S(2)}) collective-permute-start(bf16[384,1536]{1,0:T(8,128)(2,1)} %get-tuple-element.132), channel_id=1, source_target_pairs={{0,2},{2,0},{4,6},{6,4},{8,10},{10,8},{12,14},{14,12},{16,18},{18,... | collective-permute-start | bytes 3538952 | tf_op jit(solution)/shard_map/ppermute | solution.py:885
  166.8 37.5 %collective-permute-start.13 = (bf16[384,768]{1,0:T(8,128)(2,1)}, bf16[384,768]{1,0:T(8,128)(2,1)S(1)}, u32[]{:S(2)}, u32[]{:S(2)}) collective-permute-start(bf16[384,768]{1,0:T(8,128)(2,1)} %get-tuple-element.179), channel_id=1, source_target_pairs={{0,8},{2,10},{4,12},{6,14},{8,0},{10,2},{12,4},{14,6},{16,24},{18,... | collective-permute-start | bytes 1769480 | tf_op jit(solution)/shard_map/ppermute | solution.py:885
  176.9 37.0 %collective-permute-start.14 = (bf16[384,1536]{1,0:T(8,128)(2,1)S(1)}, bf16[384,1536]{1,0:T(8,128)(2,1)S(1)}, u32[]{:S(2)}, u32[]{:S(2)}) collective-permute-start(bf16[384,1536]{1,0:T(8,128)(2,1)S(1)} %fold_qkv_core.1.refs_12_), channel_id=1, source_target_pairs={{0,1},{1,0},{2,3},{3,2},{4,5},{5,4},{6,7},{7,6},{8,9},{9,8},{10,11... | collective-permute-start | bytes 3538952 | tf_op jit(solution)/shard_map/ppermute | solution.py:888
  204.2 11.3 %collective-permute-start.15 = (bf16[384,1536]{1,0:T(8,128)(2,1)}, bf16[384,1536]{1,0:T(8,128)(2,1)}, u32[]{:S(2)}, u32[]{:S(2)}) collective-permute-start(bf16[384,1536]{1,0:T(8,128)(2,1)} %get-tuple-element.143), channel_id=1, source_target_pairs={{0,2},{2,0},{4,6},{6,4},{8,10},{10,8},{12,14},{14,12},{16,18},{18,... | collective-permute-start | bytes 3538952 | tf_op jit(solution)/shard_map/ppermute | solution.py:885
  217.1 17.7 %collective-permute-start.16 = (bf16[192,1536]{1,0:T(8,128)(2,1)S(1)}, bf16[192,1536]{1,0:T(8,128)(2,1)S(1)}, u32[]{:S(2)}, u32[]{:S(2)}) collective-permute-start(bf16[192,1536]{1,0:T(8,128)(2,1)S(1)} %get-tuple-element.177), channel_id=1, source_target_pairs={{0,4},{2,6},{4,0},{6,2},{8,12},{10,14},{12,8},{14,10},{16,20},{18,... | collective-permute-start | bytes 1769480 | tf_op jit(solution)/shard_map/ppermute | solution.py:885
  217.5 16.6 %collective-permute-start.18 = (bf16[192,768]{1,0:T(8,128)(2,1)}, bf16[192,768]{1,0:T(8,128)(2,1)S(1)}, u32[]{:S(2)}, u32[]{:S(2)}) collective-permute-start(bf16[192,768]{1,0:T(8,128)(2,1)} %get-tuple-element.181), channel_id=1, source_target_pairs={{0,16},{2,18},{4,20},{6,22},{8,24},{10,26},{12,28},{14,30},{16,0},... | collective-permute-start | bytes 884744 | tf_op jit(solution)/shard_map/ppermute | solution.py:885
  221.6 13.2 %collective-permute-start.17 = (bf16[192,768]{1,0:T(8,128)(2,1)}, bf16[192,768]{1,0:T(8,128)(2,1)S(1)}, u32[]{:S(2)}, u32[]{:S(2)}) collective-permute-start(bf16[192,768]{1,0:T(8,128)(2,1)} %reduce-scatter.2.cloned.1.call-done), channel_id=1, source_target_pairs={{0,1},{1,0},{2,3},{3,2},{4,5},{5,4},{6,7},{7,6},{8,9},{9,8},{10,11... | collective-permute-start | bytes 884744 | tf_op jit(solution)/shard_map/ppermute | solution.py:888
  237.9 14.9 %collective-permute-start.19 = (bf16[128,1536]{1,0:T(8,128)(2,1)S(1)}, bf16[128,1536]{1,0:T(8,128)(2,1)S(1)}, u32[]{:S(2)}, u32[]{:S(2)}) collective-permute-start(bf16[128,1536]{1,0:T(8,128)(2,1)S(1)} %get-tuple-element.155), channel_id=1, source_target_pairs={{0,8},{2,10},{4,12},{6,14},{8,0},{10,2},{12,4},{14,6},{16,24},{18,... | collective-permute-start | bytes 1179656 | tf_op jit(solution)/shard_map/ppermute | solution.py:885
  253.5 22.2 %collective-permute-start.20 = (bf16[128,1536]{1,0:T(8,128)(2,1)S(1)}, bf16[128,1536]{1,0:T(8,128)(2,1)S(1)}, u32[]{:S(2)}, u32[]{:S(2)}) collective-permute-start(bf16[128,1536]{1,0:T(8,128)(2,1)S(1)} %get-tuple-element.158), channel_id=1, source_target_pairs={{0,16},{2,18},{4,20},{6,22},{8,24},{10,26},{12,28},{14,30},{16,0},... | collective-permute-start | bytes 1179656 | tf_op jit(solution)/shard_map/ppermute | solution.py:885
  276.3 22.7 %collective-permute-start.24 = (bf16[96,1536]{1,0:T(8,128)(2,1)S(1)}, bf16[96,1536]{1,0:T(8,128)(2,1)S(1)}, u32[]{:S(2)}, u32[]{:S(2)}) collective-permute-start(bf16[96,1536]{1,0:T(8,128)(2,1)S(1)} %get-tuple-element.161.refs_3_.refs_1_), channel_id=1, source_target_pairs={{0,8},{2,10},{4,12},{6,14},{8,0},{10,2},{12,4},{14,6},{16,24},{18,... | collective-permute-start | bytes 884744 | tf_op jit(solution)/shard_map/ppermute | solution.py:885
  299.8 14.1 %collective-permute-start.25 = (bf16[192,1536]{1,0:T(8,128)(2,1)S(1)}, bf16[192,1536]{1,0:T(8,128)(2,1)S(1)}, u32[]{:S(2)}, u32[]{:S(2)}) collective-permute-start(bf16[192,1536]{1,0:T(8,128)(2,1)S(1)} %join.1.refs_5_.refs_1_), channel_id=1, source_target_pairs={{0,4},{2,6},{4,0},{6,2},{8,12},{10,14},{12,8},{14,10},{16,20},{18,... | collective-permute-start | bytes 1769480 | tf_op jit(solution)/shard_map/ppermute | solution.py:885
  301.3 14.6 %collective-permute-start.26 = (bf16[192,1536]{1,0:T(8,128)(2,1)S(1)}, bf16[192,1536]{1,0:T(8,128)(2,1)S(1)}, u32[]{:S(2)}, u32[]{:S(2)}) collective-permute-start(bf16[192,1536]{1,0:T(8,128)(2,1)S(1)} %join.1.refs_5_.refs_1_), channel_id=1, source_target_pairs={{0,2},{2,0},{4,6},{6,4},{8,10},{10,8},{12,14},{14,12},{16,18},{18,... | collective-permute-start | bytes 1769480 | tf_op jit(solution)/shard_map/ppermute | solution.py:885
  (48 other events, 307.7 us)
Sparse Core Ops, SparseCore 0:
  137.9 83.6 reduce-scatter.1
  236.3 67.5 all-gather.1
